TPU v7x, 128 devices: a whole 4x4x4 slice. The times are simulated.
128 devices in a mesh: seq: 8 (over y, core), mem: 16 (over x, z).
Axes of the slice: x: 4, y: 4, z: 4, core: 2. Of those that a mesh axis runs over, the one named last changes fastest.
Arguments:
- tokens: bfloat16 [16, 2048, 2048], P('mem', 'seq')
- block_ids: int32 [16, 16, 8], P('mem', 'seq'), may hold values from 0 to 127, as said below
- memory: bfloat16 [128, 2, 128, 1024], P('mem')
- w_query: bfloat16 [2048, 1024], replicated, may hold values from -0.125 to 0.125
- w_key: bfloat16 [2048, 1024], replicated, may hold values from -0.125 to 0.125
- w_value: bfloat16 [2048, 1024], replicated, may hold values from -0.125 to 0.125
- w_out: bfloat16 [1024, 2048], replicated, may hold values from -0.1875 to 0.1875
- gate_bias: float32 [8], replicated, may hold values from -2 to 2
Outputs:
- layer_out: bfloat16 [16, 2048, 2048], P('mem', 'seq')
Inputs may be any that keep to these rules, and one draw needn't show every extreme that they name: `block_ids`: among the 16 ids of one device (its 2 query blocks), at most 2 are held by the same index m of mem (ids 8m to 8m+7), and some index holds exactly 2; the 8 ids of one query block are distinct.
All inputs are finite; a program needn't handle non-finite values.
Results may differ from a plain program's by a relative error of at most 0.008.
The roundings to bfloat16 on the way count: a program that leaves them out, or rounds other values in their place, can miss the bound.
Values may be sent and summed in bfloat16 or wider, within the bound.
No kernel may reach another device: no remote copies, remote signals or barrier semaphores. Data moves between devices by JAX's collectives and lax.ppermute only.
A program may use at most 192 MiB of HBM per device.

v0:
```python
import jax
import jax.numpy as jnp
from jax import lax
from jax.sharding import PartitionSpec as P

WIN = 1024


def shards(tokens, block_ids, memory, w_query, w_key, w_value, w_out, gate_bias):
    tok = tokens.shape[1]
    width = w_query.shape[1]
    heads = gate_bias.shape[0]
    hsize = width // heads
    scale = hsize ** (-0.5)
    flat = tokens[0]
    query = jnp.dot(flat, w_query, preferred_element_type=jnp.float32).astype(jnp.bfloat16)
    keys_own = jnp.dot(flat, w_key, preferred_element_type=jnp.float32).astype(jnp.bfloat16)
    values_own = jnp.dot(flat, w_value, preferred_element_type=jnp.float32).astype(jnp.bfloat16)
    paired = jnp.stack([keys_own, values_own])
    position = lax.axis_index("seq")
    reach = (WIN + tok - 1) // tok
    grouped = lax.all_gather(paired, "seq", axis=1, tiled=True)
    padding = jnp.zeros((2, reach * tok, width), jnp.bfloat16)
    padded = jnp.concatenate([padding, grouped], axis=1)
    window = lax.dynamic_slice_in_dim(padded, position * tok, (reach + 1) * tok, 1)
    qheads = query.reshape(tok, heads, hsize)
    wkeys = window[0].reshape((reach + 1) * tok, heads, hsize)
    wvalues = window[1].reshape((reach + 1) * tok, heads, hsize)
    scores = jnp.einsum("qhd,khd->hqk", qheads, wkeys, preferred_element_type=jnp.float32) * scale
    qpos = position * tok + jnp.arange(tok, dtype=jnp.int32)
    kpos = position * tok - reach * tok + jnp.arange((reach + 1) * tok, dtype=jnp.int32)
    valid = (
        (kpos[None, :] >= 0)
        & (kpos[None, :] <= qpos[:, None])
        & (qpos[:, None] - kpos[None, :] < WIN)
    )
    scores = jnp.where(valid[None], scores, -1e30)
    probs = jax.nn.softmax(scores, axis=-1).astype(jnp.bfloat16)
    local_out = jnp.einsum("hqk,khd->qhd", probs, wvalues, preferred_element_type=jnp.float32)
    qblocks = block_ids.shape[1]
    topb = block_ids.shape[2]
    ids = block_ids[0].reshape(qblocks * topb)
    wanted = ids.shape[0]
    held = memory.shape[0]
    tile_shape = memory.shape[1:]
    qblk = tok // qblocks
    memb = tile_shape[1]
    holders = lax.axis_size("mem")
    capacity = max(2, 2 * wanted // holders)
    slots = holders * capacity
    holder = ids // held
    local = ids % held
    hits = (holder[:, None] == jnp.arange(holders, dtype=jnp.int32)[None, :]).astype(jnp.int32)
    before = jnp.cumsum(hits, axis=0) - hits
    rank = jnp.sum(before * hits, axis=1)
    slot = holder * capacity + rank
    matched = slot[:, None] == jnp.arange(slots, dtype=jnp.int32)[None, :]
    table = jnp.sum(jnp.where(matched, local[:, None], 0), axis=0)
    table = table.reshape(holders, capacity)
    asked = lax.all_to_all(table, "mem", split_axis=0, concat_axis=0, tiled=True)
    stored = memory[asked.reshape(slots)]
    outgoing = stored.reshape((holders, capacity) + tile_shape)
    arrived = lax.all_to_all(outgoing, "mem", split_axis=0, concat_axis=0, tiled=True)
    chosen = arrived.reshape((slots,) + tile_shape)[slot]
    chosen = chosen.reshape(qblocks, topb, 2, memb, width)
    mkeys = chosen[:, :, 0].reshape(qblocks, topb * memb, heads, hsize)
    mvalues = chosen[:, :, 1].reshape(qblocks, topb * memb, heads, hsize)
    qgrouped = query.reshape(qblocks, qblk, heads, hsize)
    mscores = (
        jnp.einsum("bqhd,bkhd->bhqk", qgrouped, mkeys, preferred_element_type=jnp.float32) * scale
    )
    mprobs = jax.nn.softmax(mscores, axis=-1).astype(jnp.bfloat16)
    memory_out = jnp.einsum("bhqk,bkhd->bqhd", mprobs, mvalues, preferred_element_type=jnp.float32)
    memory_out = memory_out.reshape(tok, heads, hsize)
    gate = jax.nn.sigmoid(gate_bias)[:, None]
    mixed = (gate * memory_out + (1.0 - gate) * local_out).astype(jnp.bfloat16).reshape(tok, width)
    result = jnp.dot(mixed, w_out, preferred_element_type=jnp.float32).astype(jnp.bfloat16)
    return result[None]


def solution(mesh):
    in_specs = (
        P("mem", "seq", None),
        P("mem", "seq", None),
        P("mem", None, None, None),
        P(),
        P(),
        P(),
        P(),
        P(),
    )
    out_specs = P("mem", "seq", None)
    return jax.shard_map(shards, mesh=mesh, in_specs=in_specs, out_specs=out_specs, check_vma=False)
```

profile of v0, /device:TPU:76, one launch (start us, length us, event | category | flops | bytes accessed | tf_op | source)
XLA Modules:
  0.0 392.0 jit_solution(3622256489956404406)
XLA Ops:
  6.5 0.8 reshape_squeeze.17
  7.5 0.2 select_reduce_fusion.1
  7.8 0.7 all_to_all.9
  8.5 7.4 %all-to-all-start = ((s32[16,1,2]{2,1,0:T(1,128)}), s32[16,1,2]{2,1,0:T(1,128)S(1)}, u32[]{:S(2)}, u32[]{:S(2)}) async-start(s32[16,1,2]{2,1,0:T(1,128)} %bitcast), calls=%async_computation | async-start | bytes 16384 | tf_op jit(solution)/shard_map/all_to_all | solution.py:60
  15.9 3.4 fusion.27
  19.3 0.5 broadcast.285
  19.9 0.7 reduce.3
  20.6 9.4 %gather_fusion = bf16[32,2,128,1024]{3,2,1,0:T(8,128)(2,1)} fusion(bf16[8,2,128,1024]{3,2,1,0:T(8,128)(2,1)} %param.10, s32[1024]{0:T(1024)S(1)} %pad_clamp_fusion.1), kind=kCustom, calls=%fused_computation | custom fusion | bytes 33554560 | tf_op jit(solution)/shard_map/gather | solution.py:61
  30.0 9.0 %all-to-all-start.1 = ((bf16[16,2,2,128,1024]{4,3,2,1,0:T(8,128)(2,1)}), bf16[16,2,2,128,1024]{4,3,2,1,0:T(8,128)(2,1)}, u32[]{:S(2)}, u32[]{:S(2)}) async-start(bf16[16,2,2,128,1024]{4,3,2,1,0:T(8,128)(2,1)} %bitcast.78), calls=%async_computation.1 | async-start | bytes 33554432 | tf_op jit(solution)/shard_map/all_to_all | solution.py:63
  39.1 3.4 fusion.28
  42.5 1.1 pad_maximum_fusion
  43.7 3.4 convolution_convert_fusion.3
  47.1 0.1 copy.57
  47.3 0.5 fusion.25
  47.8 46.3 %all-gather.2.cloned.1.call-done = bf16[2,2048,1024]{2,1,0:T(8,128)(2,1)} async-done(((bf16[2,256,1024]{2,1,0:T(8,128)(2,1)}), bf16[2,2048,1024]{2,1,0:T(8,128)(2,1)}) %all-gather.2.cloned.1.call-update) | async-done | bytes 8388624 | tf_op jit(solution)/shard_map/all_gather | solution.py:22
  94.1 4.9 %fusion.15 = (bf16[160,8,8,128]{3,1,2,0:T(8,128)(2,1)S(1)}, bf16[1,1280,1024]{2,1,0:T(8,128)(2,1)}) fusion(s32[]{:T(128)S(6)} %select_n.68, bf16[2,2048,1024]{2,1,0:T(8,128)(2,1)} %all-gather.2.cloned.1.call-done, s32[]{:T(128)S(6)} %add.112), kind=kLoop, calls=%fused_computation.23 | loop fusion | bytes 13631496
  99.0 2.1 copy.60
  101.1 4.4 %copy.53 = bf16[1,1280,1024]{1,2,0:T(8,128)(2,1)} copy(bf16[1,1280,1024]{2,1,0:T(8,128)(2,1)} %get-tuple-element.10) | data formatting | bytes 5242880 | tf_op jit(solution)/shard_map/reshape;squeeze | solution.py:28
  105.4 9.7 %fusion.61 = (f32[8,256]{1,0:T(8,128)S(1)}, f32[8,256,1280]{2,1,0:T(8,128)}) fusion(pred[256,1280]{1,0:T(8,128)(4,1)S(1)} %fusion.25, bf16[1280,8,128]{2,1,0:T(8,128)(2,1)} %bitcast.86, bf16[256,1024]{1,0:T(8,128)(2,1)S(1)} %convolution_convert_fusion.3), kind=kOutput, calls=%fused_computation.82 | convolution fusion | flops 681575680 | bytes 13967360 | tf_op jit(solution)/shard_map/sub | solution.py:38
  115.1 226.7 %all-to-all-done.1 = bf16[16,2,2,128,1024]{4,3,2,1,0:T(8,128)(2,1)} async-done(((bf16[16,2,2,128,1024]{4,3,2,1,0:T(8,128)(2,1)}), bf16[16,2,2,128,1024]{4,3,2,1,0:T(8,128)(2,1)}, u32[]{:S(2)}, u32[]{:S(2)}) %all-to-all-start.1) | async-done | bytes 16777248 | tf_op jit(solution)/shard_map/all_to_all | solution.py:63
  341.8 10.5 %gather_fusion.1 = bf16[16,2,128,1024]{3,2,1,0:T(8,128)(2,1)} fusion(bf16[32,2,128,1024]{3,2,1,0:T(8,128)(2,1)} %bitcast.3, s32[1024]{0:T(1024)S(1)} %pad_clamp_fusion), kind=kCustom, calls=%fused_computation.1 | custom fusion | bytes 16777280 | tf_op jit(solution)/shard_map/gather | solution.py:64
  352.4 4.0 %fusion.60 = (bf16[2,8,1,128,1024]{4,3,2,1,0:T(8,128)(2,1)S(1)}, bf16[2,8,1,128,1024]{4,3,2,1,0:T(8,128)(2,1)S(1)}) fusion(bf16[2,8,2,128,1024]{4,3,2,1,0:T(8,128)(2,1)} %bitcast.79), kind=kLoop, calls=%fused_computation.81 | loop fusion | bytes 16777216 | tf_op jit(solution)/shard_map/slice | solution.py:66
  356.3 1.1 copy.58
  357.4 1.3 fusion.12
  358.8 2.3 fusion.66
  361.1 0.9 copy-done.2
  362.0 3.1 copy.59
  365.1 9.9 %fusion.19 = f32[2,128,8,128]{3,1,2,0:T(8,128)S(1)} fusion(bf16[2,1024,8,128]{3,2,1,0:T(8,128)(2,1)} %bitcast.83, f32[2,8,128]{2,1,0:T(8,128)S(1)} %fusion.66, f32[2,8,128,1024]{3,2,1,0:T(8,128)} %copy-done.2), kind=kOutput, calls=%fused_computation.28 | convolution fusion | flops 547359744 | bytes 13639680 | tf_op jit(solution)/shard_map/bhqk,bkhd->bqhd/dot_general | solution.py:73
  375.0 0.6 copy.48
  375.6 0.4 copy.49
  376.0 6.9 %fusion.26 = bf16[256,8,128]{0,2,1:T(8,128)(2,1)S(1)} fusion(bf16[1280,8,128]{0,2,1:T(8,128)(2,1)} %bitcast.85, f32[8,256,1280]{2,1,0:T(8,128)} %get-tuple-element.14, f32[8,256]{1,0:T(8,128)S(1)} %get-tuple-element.13, f32[256,8,128]{0,2,1:T(8,128)S(1)} %copy.49, f32[8]{0:T(128)S(1)} %get-tuple-element.5, f32[8]{0:T(128)S(1)} %get-tuple-element.6), kind=kOutput, calls=%fused_computation.37 | convolution fusion | flops 677380096 | bytes 14688320 | tf_op jit(solution)/shard_map/hqk,khd->qhd/dot_general | solution.py:39
  382.9 2.2 fusion.18
  (29 shorter events, 0.5 us)
Async XLA Ops:
  6.5 9.3 %copy-start = (bf16[1,256,2048]{2,1,0:T(8,128)(2,1)S(1)}, bf16[1,256,2048]{2,1,0:T(8,128)(2,1)}, u32[]{:S(2)}) copy-start(bf16[1,256,2048]{2,1,0:T(8,128)(2,1)} %param.8) | copy-start | bytes 3145732
  8.5 10.8 %all-to-all-start = ((s32[16,1,2]{2,1,0:T(1,128)}), s32[16,1,2]{2,1,0:T(1,128)S(1)}, u32[]{:S(2)}, u32[]{:S(2)}) async-start(s32[16,1,2]{2,1,0:T(1,128)} %bitcast), calls=%async_computation | async-start | bytes 16384 | tf_op jit(solution)/shard_map/all_to_all | solution.py:60
  30.0 311.8 %all-to-all-start.1 = ((bf16[16,2,2,128,1024]{4,3,2,1,0:T(8,128)(2,1)}), bf16[16,2,2,128,1024]{4,3,2,1,0:T(8,128)(2,1)}, u32[]{:S(2)}, u32[]{:S(2)}) async-start(bf16[16,2,2,128,1024]{4,3,2,1,0:T(8,128)(2,1)} %bitcast.78), calls=%async_computation.1 | async-start | bytes 33554432 | tf_op jit(solution)/shard_map/all_to_all | solution.py:63
  39.0 4.6 %copy-start.4 = (s32[1,2,8]{2,1,0:T(2,128)S(1)}, s32[1,2,8]{2,1,0:T(2,128)}, u32[]{:S(2)}) copy-start(s32[1,2,8]{2,1,0:T(2,128)} %param.9) | copy-start | bytes 196
  39.0 55.1 %all-gather.2.cloned.1.call-start = ((), (), s32[]{:S(2)}) async-start(), calls=%async_computation.2 | async-start | bytes 9437184 | tf_op jit(solution)/shard_map/all_gather | solution.py:22
  43.6 3.7 copy-start.5
  358.8 3.2 copy-start.2
  376.0 6.9 %copy-start.3 = (bf16[1024,2048]{1,0:T(8,128)(2,1)S(1)}, bf16[1024,2048]{1,0:T(8,128)(2,1)}, u32[]{:S(2)}) copy-start(bf16[1024,2048]{1,0:T(8,128)(2,1)} %param.14) | copy-start | bytes 12582916
  376.0 9.2 %copy-start.1 = (bf16[1,256,2048]{2,1,0:T(8,128)(2,1)S(1)}, bf16[1,256,2048]{2,1,0:T(8,128)(2,1)}, u32[]{:S(2)}) copy-start(bf16[1,256,2048]{2,1,0:T(8,128)(2,1)} %param.8) | copy-start | bytes 3145732
Sparse Core Ops, SparseCore 0:
  43.7 50.3 all-gather.1
where the time goes:
time: 393 us; the launch traced here: 392 us
  waiting for transfers between devices  273 us (69%)
  local copies, waits for them, and re-layouts  43.6 us (11%)
  matrix products  40.4 us (10%)
  starting transfers between devices  16.4 us (4%)
  between operations  13.6 us (3%)
  other arithmetic  4.95 us (1%)
    all_to_all x1, waiting for transfers between devices, shards(): lax.all_to_all(outgoing, 'mem', split_axis=0, concat_axis=0, tiled=True)  227 us
    all_gather x1, waiting for transfers between devices, shards(): grouped = lax.all_gather(paired, 'seq', axis=1, tiled=True)  46.3 us
    unnamed x17, local copies, waits for them, and re-layouts  12.1 us
    gather x1, local copies, waits for them, and re-layouts, shards(): chosen = arrived.reshape((slots,) + tile_shape)[slot]  10.5 us
    dot_general x1, matrix products, shards(): jnp.einsum('bhqk,bkhd->bqhd', mprobs, mvalues, preferred_element_type=jnp...  9.91 us
    sub x1, matrix products, shards(): probs = jax.nn.softmax(scores, axis=-1).astype(jnp.bfloat16)  9.71 us
    gather x1, local copies, waits for them, and re-layouts, shards(): stored = memory[asked.reshape(slots)]  9.37 us
    all_to_all x1, starting transfers between devices, shards(): lax.all_to_all(outgoing, 'mem', split_axis=0, concat_axis=0, tiled=True)  8.99 us
  transfers between devices with their start and end apart: 3, of which 2 were waited for; matrix products, arithmetic and copies ran while one was open for 8% of the time, Pallas kernels for 0%

commit v1 on v0

v1 whole, which is shorter than its diff:
```python
import functools

import jax
import jax.numpy as jnp
from jax import lax
from jax.experimental import pallas as pl
from jax.experimental.pallas import tpu as pltpu
from jax.sharding import PartitionSpec as P

RING = 4
HD = 128
FEAT = 512
TOK = 256
CHIP = 512
BLK = 128
STAT = 16
SLAB = FEAT + STAT
NEG = -1e30
F32 = jnp.float32
BF16 = jnp.bfloat16
LOG2E = 1.4426950408889634
VMEM = 48 * 1024 * 1024


def index_of(x, y, z, c):
    return (y * 2 + c) * RING * RING + x * RING + z


def send(array, move):
    pairs = []
    for x in range(RING):
        for z in range(RING):
            for y in range(RING):
                for c in range(2):
                    to = move(x, y, z, c)
                    if to is not None:
                        pairs.append((index_of(x, y, z, c), index_of(*to)))
    return lax.ppermute(array, ("seq", "mem"), pairs)


def step(c):
    return 1 if c == 0 else -1


def x1(x, y, z, c):
    return ((x + step(c)) % RING, y, z, c)


def x2(x, y, z, c):
    return ((x - step(c)) % RING, y, z, c)


def z1(x, y, z, c):
    return (x, y, (z + step(c)) % RING, c)


def z2(x, y, z, c):
    return (x, y, (z - step(c)) % RING, c)


def y1(x, y, z, c):
    return (x, (y + step(c)) % RING, z, c)


def y2(x, y, z, c):
    return (x, (y - step(c)) % RING, z, c)


def yfar(x, y, z, c):
    return (x, (y + 2) % RING, z, c)


def later1(x, y, z, c):
    return (x, y + 1, z, c) if y + 1 < RING else None


def later2(x, y, z, c):
    return (x, y + 2, z, c) if y + 2 < RING else None


def core(x, y, z, c):
    return (x, y, z, 1 - c)


def params():
    return pltpu.CompilerParams(vmem_limit_bytes=VMEM)


def cost(flops, nbytes, trans=0):
    return pl.CostEstimate(flops=flops, bytes_accessed=nbytes, transcendentals=trans)


def any_specs(count):
    return [pl.BlockSpec(memory_space=pl.ANY)] * count


def dot(a, b, ca, cb):
    return lax.dot_general(a, b, (((ca,), (cb,)), ((), ())), preferred_element_type=F32)


def query_kernel(info, own, oth, w, ids, out):
    out[0:TOK, :] = dot(own[...], w[...], 1, 0).astype(BF16)
    out[TOK:CHIP, :] = dot(oth[...], w[...], 1, 0).astype(BF16)
    out[CHIP:, :] = ids[...]


def project_query(info, own, oth, w, ids):
    depth = own.shape[1]
    tile = 256
    steps = FEAT // tile
    whole = pl.BlockSpec((TOK, depth), lambda j, info: (0, 0))
    return pl.pallas_call(
        query_kernel,
        grid_spec=pltpu.PrefetchScalarGridSpec(
            num_scalar_prefetch=1,
            grid=(steps,),
            in_specs=[
                whole,
                whole,
                pl.BlockSpec((depth, tile), lambda j, info: (0, info[3] * steps + j)),
                pl.BlockSpec((STAT, tile), lambda j, info: (0, j)),
            ],
            out_specs=pl.BlockSpec((CHIP + STAT, tile), lambda j, info: (0, j)),
        ),
        out_shape=jax.ShapeDtypeStruct((CHIP + STAT, FEAT), BF16),
        compiler_params=params(),
        cost_estimate=cost(2 * CHIP * depth * FEAT, 2 * depth * (FEAT + CHIP)),
    )(info, own, oth, w, ids)


def keyvalue_kernel(info, own, oth, wk, wv, k, v):
    for w, out in ((wk, k), (wv, v)):
        out[0:TOK, :] = dot(own[...], w[...], 1, 0).astype(BF16)
        out[TOK:CHIP, :] = dot(oth[...], w[...], 1, 0).astype(BF16)


def project_keyvalue(info, own, oth, wk, wv):
    depth = own.shape[1]
    tile = 256
    steps = FEAT // tile
    whole = pl.BlockSpec((TOK, depth), lambda j, info: (0, 0))
    weight = pl.BlockSpec((depth, tile), lambda j, info: (0, info[3] * steps + j))
    result = pl.BlockSpec((CHIP, tile), lambda j, info: (0, j))
    return pl.pallas_call(
        keyvalue_kernel,
        grid_spec=pltpu.PrefetchScalarGridSpec(
            num_scalar_prefetch=1,
            grid=(steps,),
            in_specs=[whole, whole, weight, weight],
            out_specs=[result, result],
        ),
        out_shape=[jax.ShapeDtypeStruct((CHIP, FEAT), BF16)] * 2,
        compiler_params=params(),
        cost_estimate=cost(4 * CHIP * depth * FEAT, 2 * depth * (2 * FEAT + CHIP)),
    )(info, own, oth, wk, wv)


def split3(value):
    high = value.astype(BF16).astype(F32)
    rest = value - high
    mid = rest.astype(BF16).astype(F32)
    return high, mid, rest - mid


def pack_stats(values, width):
    row = lax.broadcasted_iota(jnp.int32, (STAT, width), 0)
    packed = jnp.zeros((STAT, width), F32)
    for h, value in enumerate(values):
        for i, part in enumerate(split3(value)):
            packed = jnp.where(row == 3 * h + i, part, packed)
    return packed.astype(BF16)


def local_kernel(info, qa, q1, q2, q3, k_hbm, v_hbm, o0, o1, o2, q, k, v, o, sem, osem):
    y = info[1]
    c = info[3]
    rows = pl.ds(0, CHIP)
    copies = [
        pltpu.make_async_copy(k_hbm, k, sem.at[0]),
        pltpu.make_async_copy(v_hbm, v, sem.at[1]),
        pltpu.make_async_copy(qa.at[rows], q.at[0], sem.at[2]),
        pltpu.make_async_copy(q3.at[rows], q.at[2], sem.at[3]),
    ]
    for copy in copies:
        copy.start()

    @pl.when(c == 0)
    def _():
        pltpu.make_async_copy(q2.at[rows], q.at[1], sem.at[4]).start()

    @pl.when(c != 0)
    def _():
        pltpu.make_async_copy(q1.at[rows], q.at[1], sem.at[4]).start()

    for copy in copies:
        copy.wait()
    pltpu.make_async_copy(q2.at[rows], q.at[1], sem.at[4]).wait()

    factor = HD ** -0.5 * LOG2E
    j = lax.broadcasted_iota(jnp.int32, (CHIP, TOK), 0)
    i = lax.broadcasted_iota(jnp.int32, (CHIP, TOK), 1)
    kpos = jnp.where(j < TOK, j + c * TOK, j - TOK + (1 - c) * TOK)

    def unit(t, carry):
        d = t // 2
        half = t % 2

        @pl.when(y + d < RING)
        def _():
            place = jnp.where(half == 0, c, 1 - c) * TOK
            diff = i - kpos + (place + d * CHIP)
            valid = (diff >= 0) & (diff < 2 * CHIP)
            start = pl.multiple_of(half * TOK, TOK)
            stats = []
            for h in range(FEAT // HD):
                cols = slice(h * HD, (h + 1) * HD)
                s = dot(k[:, cols], q[d, pl.ds(start, TOK), cols], 1, 1) * factor
                s = jnp.where(valid, s, NEG)
                m = jnp.max(s, axis=0, keepdims=True)
                p = jnp.exp2(s - m)
                total = jnp.sum(p, axis=0, keepdims=True)
                out = dot(v[:, cols], p.astype(BF16), 0, 0) / total
                o[d, cols, pl.ds(start, TOK)] = out.astype(BF16)
                stats.append(m + jnp.log2(total))
            o[d, FEAT:, pl.ds(start, TOK)] = pack_stats(stats, TOK)

        return carry

    lax.fori_loop(0, 6, unit, 0)
    outs = [
        pltpu.make_async_copy(o.at[d], ref, osem.at[d])
        for d, ref in enumerate((o0, o1, o2))
    ]
    for copy in outs:
        copy.start()
    for copy in outs:
        copy.wait()


def local_attention(info, queries, k, v):
    slab = jax.ShapeDtypeStruct((SLAB, CHIP), BF16)
    return pl.pallas_call(
        local_kernel,
        grid_spec=pltpu.PrefetchScalarGridSpec(
            num_scalar_prefetch=1,
            grid=(1,),
            in_specs=any_specs(6),
            out_specs=any_specs(3),
            scratch_shapes=[
                pltpu.VMEM((3, CHIP, FEAT), BF16),
                pltpu.VMEM((CHIP, FEAT), BF16),
                pltpu.VMEM((CHIP, FEAT), BF16),
                pltpu.VMEM((3, SLAB, CHIP), BF16),
                pltpu.SemaphoreType.DMA((5,)),
                pltpu.SemaphoreType.DMA((3,)),
            ],
        ),
        out_shape=[slab] * 3,
        compiler_params=params(),
        cost_estimate=cost(12 * CHIP * CHIP * FEAT, 8 * 2 * CHIP * FEAT, 12 * CHIP * CHIP),
    )(info, *queries, k, v)


def memory_kernel(info, ids, *refs):
    queries, parts_a, parts_b, outs = refs[:4], refs[4:8], refs[8:12], refs[12:16]
    q, mem, o, slots, sem, osem = refs[16:]
    x, y, z, c = info[0], info[1], info[2], info[3]
    copies = [
        pltpu.make_async_copy(ref.at[pl.ds(0, CHIP)], q.at[s], sem.at[s])
        for s, ref in enumerate(queries)
    ]
    for s in range(RING):
        for first, parts in ((0, parts_a), (16, parts_b)):
            copies.append(
                pltpu.make_async_copy(
                    parts[s],
                    mem.at[pl.ds(first + 4 * s, 4)],
                    sem.at[4 + s + first // 4],
                )
            )
    for copy in copies:
        copy.start()
    for copy in copies:
        copy.wait()

    factor = HD ** -0.5 * LOG2E

    def arrival(relative):
        near = jnp.where((relative == 3) == (c == 0), 1, 2)
        return jnp.where(relative == 0, 0, jnp.where(relative == 2, 3, near))

    def block(n, carry):
        s = n // 4
        start = pl.multiple_of((n % 4) * BLK, BLK)

        def look(t, count):
            ident = ids[n * 8 + t]
            mine = ((ident >> 1) & 3) == y
            ax = arrival(((ident >> 5) - x) & 3)
            az = arrival((((ident >> 3) & 3) - z) & 3)
            slot = jnp.where((ident & 1) == 0, az * 4 + ax, 16 + ax * 4 + az)
            slots[count] = slot
            return count + mine.astype(jnp.int32)

        for t in range(8):
            slots[t] = 0
        count = lax.fori_loop(0, 8, look, 0)
        pairs = (count + 1) // 2

        @pl.when(pairs == 0)
        def _():
            o[s, 0:FEAT, pl.ds(start, BLK)] = jnp.zeros((FEAT, BLK), BF16)
            low = jnp.full((1, BLK), NEG, F32)
            o[s, FEAT:, pl.ds(start, BLK)] = pack_stats([low] * (FEAT // HD), BLK)

        def attend(size):
            chosen = [slots[t] for t in range(size)]
            stats = []
            for h in range(FEAT // HD):
                cols = slice(h * HD, (h + 1) * HD)
                qh = q[s, pl.ds(start, BLK), cols]
                scores = [dot(mem[t, 0, :, cols], qh, 1, 1) * factor for t in chosen]
                scores[-1] = jnp.where(count == size, scores[-1], NEG)
                m = functools.reduce(jnp.maximum, scores)
                m = jnp.max(m, axis=0, keepdims=True)
                probs = [jnp.exp2(score - m) for score in scores]
                total = jnp.sum(functools.reduce(jnp.add, probs), axis=0, keepdims=True)
                out = functools.reduce(
                    jnp.add,
                    [
                        dot(mem[t, 1, :, cols], p.astype(BF16), 0, 0)
                        for t, p in zip(chosen, probs)
                    ],
                )
                o[s, cols, pl.ds(start, BLK)] = (out / total).astype(BF16)
                stats.append(m + jnp.log2(total))
            o[s, FEAT:, pl.ds(start, BLK)] = pack_stats(stats, BLK)

        for size in range(1, 5):
            pl.when(pairs == size)(functools.partial(attend, 2 * size))
        return carry

    lax.fori_loop(0, 16, block, 0)
    backs = [
        pltpu.make_async_copy(o.at[s], ref, osem.at[s]) for s, ref in enumerate(outs)
    ]
    for copy in backs:
        copy.start()
    for copy in backs:
        copy.wait()


def memory_attention(info, ids, queries, parts_a, parts_b):
    slab = jax.ShapeDtypeStruct((SLAB, CHIP), BF16)
    return pl.pallas_call(
        memory_kernel,
        grid_spec=pltpu.PrefetchScalarGridSpec(
            num_scalar_prefetch=2,
            grid=(1,),
            in_specs=any_specs(12),
            out_specs=any_specs(4),
            scratch_shapes=[
                pltpu.VMEM((4, CHIP, FEAT), BF16),
                pltpu.VMEM((32, 2, BLK, FEAT), BF16),
                pltpu.VMEM((4, SLAB, CHIP), BF16),
                pltpu.SMEM((16,), jnp.int32),
                pltpu.SemaphoreType.DMA((12,)),
                pltpu.SemaphoreType.DMA((4,)),
            ],
        ),
        out_shape=[slab] * 4,
        compiler_params=params(),
        cost_estimate=cost(32 * 4 * BLK * BLK * FEAT, 12 * 2**20, 32 * 4 * BLK * BLK),
    )(info, ids, *queries, *parts_a, *parts_b)


def merge_kernel(info, gate, m0, m1, m2, m3, l0, l1, l2, own, oth):
    y = info[1]
    heads = FEAT // HD

    def merged(refs, shown, h, share):
        logs = []
        for ref, show in zip(refs, shown):
            rows = ref[FEAT:, :].astype(F32)
            log = rows[3 * h : 3 * h + 1] + rows[3 * h + 1 : 3 * h + 2]
            log = log + rows[3 * h + 2 : 3 * h + 3]
            logs.append(log if show is None else jnp.where(show, log, NEG))
        top = functools.reduce(jnp.maximum, logs)
        weights = [jnp.exp2(log - top) for log in logs]
        scale = share / functools.reduce(jnp.add, weights)
        total = None
        for ref, weight in zip(refs, weights):
            term = ref[h * HD : (h + 1) * HD, :].astype(F32) * (weight * scale)
            total = term if total is None else total + term
        return total

    for h in range(heads):
        g = jax.nn.sigmoid(jnp.full((1, CHIP), gate[info[3] * heads + h], F32))
        mix = merged((m0, m1, m2, m3), (None,) * 4, h, g)
        mix = mix + merged((l0, l1, l2), (None, y >= 1, y >= 2), h, 1.0 - g)
        mix = mix.astype(BF16)
        own[h * HD : (h + 1) * HD, :] = mix[:, :TOK]
        oth[h * HD : (h + 1) * HD, :] = mix[:, TOK:]


def merge(info, gate, slabs):
    whole = pl.BlockSpec((SLAB, CHIP), lambda j, info, gate: (0, 0))
    half = pl.BlockSpec((FEAT, TOK), lambda j, info, gate: (0, 0))
    return pl.pallas_call(
        merge_kernel,
        grid_spec=pltpu.PrefetchScalarGridSpec(
            num_scalar_prefetch=2,
            grid=(1,),
            in_specs=[whole] * 7,
            out_specs=[half] * 2,
        ),
        out_shape=[jax.ShapeDtypeStruct((FEAT, TOK), BF16)] * 2,
        compiler_params=params(),
        cost_estimate=cost(20 * SLAB * CHIP, 8 * 2 * SLAB * CHIP),
    )(info, gate, *slabs)


def output_kernel(info, own, oth, w_own, w_oth, out):
    total = dot(own[...], w_own[...], 0, 0) + dot(oth[...], w_oth[...], 0, 0)
    out[...] = total.astype(BF16)


def project_output(info, own, oth, w):
    width = w.shape[1]
    tile = 512
    half = pl.BlockSpec((FEAT, TOK), lambda j, info: (0, 0))
    return pl.pallas_call(
        output_kernel,
        grid_spec=pltpu.PrefetchScalarGridSpec(
            num_scalar_prefetch=1,
            grid=(width // tile,),
            in_specs=[
                half,
                half,
                pl.BlockSpec((FEAT, tile), lambda j, info: (info[3], j)),
                pl.BlockSpec((FEAT, tile), lambda j, info: (1 - info[3], j)),
            ],
            out_specs=pl.BlockSpec((TOK, tile), lambda j, info: (0, j)),
        ),
        out_shape=jax.ShapeDtypeStruct((TOK, width), BF16),
        compiler_params=params(),
        cost_estimate=cost(4 * TOK * FEAT * width, 4 * FEAT * width),
    )(info, own, oth, w, w)


def ring(array, first, second):
    near = send(array, first)
    other = send(array, second)
    return [array, near, other, send(near, first)]


def shards(tokens, block_ids, memory, w_query, w_key, w_value, w_out, gate_bias):
    mem = lax.axis_index("mem")
    seq = lax.axis_index("seq")
    y, c = seq // 2, seq % 2
    info = jnp.stack([mem // RING, y, mem % RING, c]).astype(jnp.int32)

    part = lax.dynamic_slice(memory, (2 * y, 0, 0, c * FEAT), (2, 2, BLK, FEAT))
    gathered_a = jnp.concatenate(ring(part[0:1], x1, x2))
    gathered_b = jnp.concatenate(ring(part[1:2], z1, z2))
    parts_a = ring(gathered_a, z1, z2)
    parts_b = ring(gathered_b, x1, x2)

    own = tokens[0]
    oth = send(own, core)
    ids_own = block_ids.reshape(1, 16)
    ids_chip = jnp.concatenate([ids_own, send(ids_own, core)], axis=1)
    ids_rows = jnp.zeros((STAT, FEAT), BF16).at[0:1, 0:32].set(ids_chip.astype(BF16))
    query = project_query(info, own, oth, w_query, ids_rows)
    queries = ring(query, y1, y2)
    k, v = project_keyvalue(info, own, oth, w_key, w_value)
    ids = jnp.concatenate([q[CHIP, 0:32] for q in queries]).astype(jnp.int32)

    local0, local1, local2 = local_attention(info, queries, k, v)
    local1 = send(local1, later1)
    local2 = send(local2, later2)

    part0, part1, part2, part3 = memory_attention(info, ids, queries, parts_a, parts_b)
    slabs = [part0, send(part1, y2), send(part2, y1), send(part3, yfar)]
    mix_own, mix_oth = merge(info, gate_bias, slabs + [local0, local1, local2])
    mix_oth = send(mix_oth, core)
    return project_output(info, mix_own, mix_oth, w_out)[None]


def solution(mesh):
    in_specs = (
        P("mem", "seq", None),
        P("mem", "seq", None),
        P("mem", None, None, None),
        P(),
        P(),
        P(),
        P(),
        P(),
    )
    out_specs = P("mem", "seq", None)
    return jax.shard_map(shards, mesh=mesh, in_specs=in_specs, out_specs=out_specs, check_vma=False)
```

time: 393 us -> 132 us (0.34)
  the two profiles are of different devices: /device:TPU:76 before, /device:TPU:1 now
where the time goes in v1:
time: 132 us; the launch traced here: 131 us
  Pallas kernels  48.7 us (37%)
  starting transfers between devices  47.4 us (36%)
  waiting for transfers between devices  30.5 us (23%)
  local copies, waits for them, and re-layouts  2.59 us (2%)
  other arithmetic  1.47 us (1%)
    ppermute x23, starting transfers between devices, send(): return lax.ppermute(array, ('seq', 'mem'), pairs)  47.4 us
    ppermute x23, waiting for transfers between devices, send(): return lax.ppermute(array, ('seq', 'mem'), pairs)  30.5 us
    pallas_call x1, Pallas kernels, memory_attention(): pl.pallas_call(memory_kernel, grid_spec=pltpu.PrefetchScalarGridSpec(num_...  23.4 us
    pallas_call x1, Pallas kernels, local_attention(): pl.pallas_call(local_kernel, grid_spec=pltpu.PrefetchScalarGridSpec(num_s...  12.1 us
    pallas_call x1, Pallas kernels, project_keyvalue(): pl.pallas_call(keyvalue_kernel, grid_spec=pltpu.PrefetchScalarGridSpec(nu...  4.72 us
    pallas_call x1, Pallas kernels, project_output(): pl.pallas_call(output_kernel, grid_spec=pltpu.PrefetchScalarGridSpec(num_...  3.64 us
    pallas_call x1, Pallas kernels, project_query(): pl.pallas_call(query_kernel, grid_spec=pltpu.PrefetchScalarGridSpec(num_s...  3.25 us
  transfers between devices with their start and end apart: 23, of which 10 were waited for; matrix products, arithmetic and copies ran while one was open for 1% of the time, Pallas kernels for 33%

profile of v1, /device:TPU:1, one launch (start us, length us, event | category | flops | bytes accessed | tf_op | source)
XLA Modules:
  0.0 130.8 jit_solution(12084144487386925827)
XLA Ops:
  0.0 1.2 constant_dynamic-slice_fusion.1
  1.2 3.4 %collective-permute-start.5 = (bf16[1,2,128,512]{3,2,1,0:T(8,128)(2,1)S(1)}, bf16[1,2,128,512]{3,2,1,0:T(8,128)(2,1)S(1)}, u32[]{:S(2)}, u32[]{:S(2)}) collective-permute-start(bf16[1,2,128,512]{3,2,1,0:T(8,128)(2,1)S(1)} %get-tuple-element.40), channel_id=1, source_target_pairs={{0,4},{16,28},{32,36},{48,60},{64,68},{80,92},{96,100},{112,124},{... | collective-permute-start | bytes 786440 | tf_op jit(solution)/shard_map/ppermute | solution.py:38
  4.6 3.8 %collective-permute-start.11 = (bf16[1,2,128,512]{3,2,1,0:T(8,128)(2,1)S(1)}, bf16[1,2,128,512]{3,2,1,0:T(8,128)(2,1)S(1)}, u32[]{:S(2)}, u32[]{:S(2)}) collective-permute-start(bf16[1,2,128,512]{3,2,1,0:T(8,128)(2,1)S(1)} %get-tuple-element.39), channel_id=1, source_target_pairs={{0,1},{16,19},{32,33},{48,51},{64,65},{80,83},{96,97},{112,115},{1... | collective-permute-start | bytes 786440 | tf_op jit(solution)/shard_map/ppermute | solution.py:38
  8.3 3.0 %collective-permute-start.7 = (bf16[1,2,128,512]{3,2,1,0:T(8,128)(2,1)S(1)}, bf16[1,2,128,512]{3,2,1,0:T(8,128)(2,1)S(1)}, u32[]{:S(2)}, u32[]{:S(2)}) collective-permute-start(bf16[1,2,128,512]{3,2,1,0:T(8,128)(2,1)S(1)} %collective-permute-done.5), channel_id=1, source_target_pairs={{0,4},{16,28},{32,36},{48,60},{64,68},{80,92},{96,100},{112,124},{... | collective-permute-start | bytes 786440 | tf_op jit(solution)/shard_map/ppermute | solution.py:38
  11.3 1.3 %collective-permute-start.12 = (bf16[1,2,128,512]{3,2,1,0:T(8,128)(2,1)S(1)}, bf16[1,2,128,512]{3,2,1,0:T(8,128)(2,1)S(1)}, u32[]{:S(2)}, u32[]{:S(2)}) collective-permute-start(bf16[1,2,128,512]{3,2,1,0:T(8,128)(2,1)S(1)} %get-tuple-element.39), channel_id=1, source_target_pairs={{0,3},{16,17},{32,35},{48,49},{64,67},{80,81},{96,99},{112,113},{1... | collective-permute-start | bytes 786440 | tf_op jit(solution)/shard_map/ppermute | solution.py:38
  12.6 3.5 %collective-permute-start.13 = (bf16[1,2,128,512]{3,2,1,0:T(8,128)(2,1)S(1)}, bf16[1,2,128,512]{3,2,1,0:T(8,128)(2,1)S(1)}, u32[]{:S(2)}, u32[]{:S(2)}) collective-permute-start(bf16[1,2,128,512]{3,2,1,0:T(8,128)(2,1)S(1)} %collective-permute-done.11), channel_id=1, source_target_pairs={{0,1},{16,19},{32,33},{48,51},{64,65},{80,83},{96,97},{112,115},{1... | collective-permute-start | bytes 786440 | tf_op jit(solution)/shard_map/ppermute | solution.py:38
  16.3 3.4 %collective-permute-start.8 = (bf16[4,2,128,512]{3,2,1,0:T(8,128)(2,1)S(1)}, bf16[4,2,128,512]{3,2,1,0:T(8,128)(2,1)}, u32[]{:S(2)}, u32[]{:S(2)}) collective-permute-start(bf16[4,2,128,512]{3,2,1,0:T(8,128)(2,1)S(1)} %pad_maximum_fusion.refs_4_), channel_id=1, source_target_pairs={{0,1},{16,19},{32,33},{48,51},{64,65},{80,83},{96,97},{112,115},{1... | collective-permute-start | bytes 3145736 | tf_op jit(solution)/shard_map/ppermute | solution.py:38
  19.9 2.0 %collective-permute-done.13 = bf16[1,2,128,512]{3,2,1,0:T(8,128)(2,1)S(1)} collective-permute-done((bf16[1,2,128,512]{3,2,1,0:T(8,128)(2,1)S(1)}, bf16[1,2,128,512]{3,2,1,0:T(8,128)(2,1)S(1)}, u32[]{:S(2)}, u32[]{:S(2)}) %collective-permute-start.13) | collective-permute-done | bytes 262176 | tf_op jit(solution)/shard_map/ppermute | solution.py:38
  23.0 1.2 collective-permute-start.14
  24.3 2.8 %collective-permute-start.1 = (s32[1,16]{1,0:T(1,128)S(1)}, s32[1,16]{1,0:T(1,128)S(1)}, u32[]{:S(2)}, u32[]{:S(2)}) collective-permute-start(s32[1,16]{1,0:T(1,128)S(1)} %concatenate.25), channel_id=1, source_target_pairs={{0,16},{16,0},{32,48},{48,32},{64,80},{80,64},{96,112},{112,96},{1... | collective-permute-start | bytes 200 | tf_op jit(solution)/shard_map/ppermute | solution.py:38
  27.9 3.3 %shard_map.82.refs_0_.qa = bf16[528,512]{1,0:T(8,128)(2,1)S(1)} custom-call(s32[4]{0:T(128)S(1)} %pad_add_fusion.info, bf16[256,2048]{1,0:T(8,128)(2,1)S(1)} %bitcast.15, bf16[256,2048]{1,0:T(8,128)(2,1)S(1)} %collective-permute-done.oth, bf16[2048,1024]{1,0:T(8,128)(2,1)} %w.1, bf16[16,512]{1,0:T(8,128)(2,1)S(1)} %fusion.5.ids), custom_call_target="tpu_custom_call" | custom-call | flops 1073741824 | bytes 4194304 | tf_op jit(solution)/shard_map/pallas_call | solution.py:112
  31.2 1.4 %collective-permute-start.3 = (bf16[528,512]{1,0:T(8,128)(2,1)S(1)}, bf16[528,512]{1,0:T(8,128)(2,1)S(1)}, u32[]{:S(2)}, u32[]{:S(2)}) collective-permute-start(bf16[528,512]{1,0:T(8,128)(2,1)S(1)} %shard_map.82.refs_0_.qa), channel_id=1, source_target_pairs={{0,96},{16,48},{32,0},{48,80},{64,32},{80,112},{96,64},{112,16},{1... | collective-permute-start | bytes 1622024 | tf_op jit(solution)/shard_map/ppermute | solution.py:38
  32.6 1.5 %collective-permute-start.2 = (bf16[528,512]{1,0:T(8,128)(2,1)S(1)}, bf16[528,512]{1,0:T(8,128)(2,1)S(1)}, u32[]{:S(2)}, u32[]{:S(2)}) collective-permute-start(bf16[528,512]{1,0:T(8,128)(2,1)S(1)} %shard_map.82.refs_0_.qa), channel_id=1, source_target_pairs={{0,32},{16,112},{32,64},{48,16},{64,96},{80,48},{96,0},{112,80},{1... | collective-permute-start | bytes 1622024 | tf_op jit(solution)/shard_map/ppermute | solution.py:38
  34.1 1.7 %collective-permute-start.15 = (bf16[4,2,128,512]{3,2,1,0:T(8,128)(2,1)}, bf16[4,2,128,512]{3,2,1,0:T(8,128)(2,1)S(1)}, u32[]{:S(2)}, u32[]{:S(2)}) collective-permute-start(bf16[4,2,128,512]{3,2,1,0:T(8,128)(2,1)} %pad_maximum_fusion.1.refs_8_), channel_id=1, source_target_pairs={{0,12},{16,20},{32,44},{48,52},{64,76},{80,84},{96,108},{112,116},... | collective-permute-start | bytes 3145736 | tf_op jit(solution)/shard_map/ppermute | solution.py:38
  35.8 1.5 %collective-permute-done.14.refs_9_ = bf16[4,2,128,512]{3,2,1,0:T(8,128)(2,1)} collective-permute-done((bf16[4,2,128,512]{3,2,1,0:T(8,128)(2,1)}, bf16[4,2,128,512]{3,2,1,0:T(8,128)(2,1)}, u32[]{:S(2)}, u32[]{:S(2)}) %collective-permute-start.14) | collective-permute-done | bytes 1048608 | tf_op jit(solution)/shard_map/ppermute | solution.py:38
  37.2 3.4 %collective-permute-start.10 = (bf16[4,2,128,512]{3,2,1,0:T(8,128)(2,1)}, bf16[4,2,128,512]{3,2,1,0:T(8,128)(2,1)S(1)}, u32[]{:S(2)}, u32[]{:S(2)}) collective-permute-start(bf16[4,2,128,512]{3,2,1,0:T(8,128)(2,1)} %collective-permute-done.8.refs_5_), channel_id=1, source_target_pairs={{0,1},{16,19},{32,33},{48,51},{64,65},{80,83},{96,97},{112,115},{1... | collective-permute-start | bytes 3145736 | tf_op jit(solution)/shard_map/ppermute | solution.py:38
  40.7 2.5 %collective-permute-done.3.refs_2_.q2 = bf16[528,512]{1,0:T(8,128)(2,1)S(1)} collective-permute-done((bf16[528,512]{1,0:T(8,128)(2,1)S(1)}, bf16[528,512]{1,0:T(8,128)(2,1)S(1)}, u32[]{:S(2)}, u32[]{:S(2)}) %collective-permute-start.3) | collective-permute-done | bytes 540704 | tf_op jit(solution)/shard_map/ppermute | solution.py:38
  44.2 2.1 %collective-permute-done.2.refs_1_.q1 = bf16[528,512]{1,0:T(8,128)(2,1)S(1)} collective-permute-done((bf16[528,512]{1,0:T(8,128)(2,1)S(1)}, bf16[528,512]{1,0:T(8,128)(2,1)S(1)}, u32[]{:S(2)}, u32[]{:S(2)}) %collective-permute-start.2) | collective-permute-done | bytes 540704 | tf_op jit(solution)/shard_map/ppermute | solution.py:38
  46.3 2.6 %collective-permute-start.4 = (bf16[528,512]{1,0:T(8,128)(2,1)S(1)}, bf16[528,512]{1,0:T(8,128)(2,1)S(1)}, u32[]{:S(2)}, u32[]{:S(2)}) collective-permute-start(bf16[528,512]{1,0:T(8,128)(2,1)S(1)} %collective-permute-done.2.refs_1_.q1), channel_id=1, source_target_pairs={{0,32},{16,112},{32,64},{48,16},{64,96},{80,48},{96,0},{112,80},{1... | collective-permute-start | bytes 1622024 | tf_op jit(solution)/shard_map/ppermute | solution.py:38
  49.0 4.7 %shard_map.84 = (bf16[512,512]{1,0:T(8,128)(2,1)S(1)}, bf16[512,512]{1,0:T(8,128)(2,1)S(1)}) custom-call(s32[4]{0:T(128)S(1)} %pad_add_fusion.info, bf16[256,2048]{1,0:T(8,128)(2,1)S(1)} %bitcast.16, bf16[256,2048]{1,0:T(8,128)(2,1)S(1)} %collective-permute-done.oth, bf16[2048,1024]{1,0:T(8,128)(2,1)} %wk.1, bf16[2048,1024]{1,0:T(8,128)(2,1)} %wv.1), custom_call_target="tpu_custom_call" | custom-call | flops 2147483648 | bytes 6291456 | tf_op jit(solution)/shard_map/pallas_call | solution.py:144
  53.7 1.6 %collective-permute-done.4.refs_3_.q3 = bf16[528,512]{1,0:T(8,128)(2,1)S(1)} collective-permute-done((bf16[528,512]{1,0:T(8,128)(2,1)S(1)}, bf16[528,512]{1,0:T(8,128)(2,1)S(1)}, u32[]{:S(2)}, u32[]{:S(2)}) %collective-permute-start.4) | collective-permute-done | bytes 540704 | tf_op jit(solution)/shard_map/ppermute | solution.py:38
  55.3 12.1 %shard_map.85 = (bf16[528,512]{1,0:T(8,128)(2,1)S(1)}, bf16[528,512]{1,0:T(8,128)(2,1)S(1)}, bf16[528,512]{1,0:T(8,128)(2,1)S(1)}) custom-call(s32[4]{0:T(128)S(1)} %pad_add_fusion.info, bf16[528,512]{1,0:T(8,128)(2,1)S(1)} %shard_map.82.refs_0_.qa, bf16[528,512]{1,0:T(8,128)(2,1)S(1)} %collective-permute-done.2.refs_1_.q1, ...), custom_call_target="tpu_custom_call" | custom-call | flops 1610612736 | bytes 4194304 | tf_op jit(solution)/shard_map/pallas_call | solution.py:242
  67.4 2.9 %collective-permute-start.20 = (bf16[528,512]{1,0:T(8,128)(2,1)S(1)}, bf16[528,512]{1,0:T(8,128)(2,1)S(1)}, u32[]{:S(2)}, u32[]{:S(2)}) collective-permute-start(bf16[528,512]{1,0:T(8,128)(2,1)S(1)} %get-tuple-element.35), channel_id=1, source_target_pairs={{0,32},{16,48},{32,64},{48,80},{64,96},{80,112},{1,33},{17,49},{33... | collective-permute-start | bytes 1622024 | tf_op jit(solution)/shard_map/ppermute | solution.py:38
  70.4 1.6 %collective-permute-start.21 = (bf16[528,512]{1,0:T(8,128)(2,1)S(1)}, bf16[528,512]{1,0:T(8,128)(2,1)S(1)}, u32[]{:S(2)}, u32[]{:S(2)}) collective-permute-start(bf16[528,512]{1,0:T(8,128)(2,1)S(1)} %get-tuple-element.36), channel_id=1, source_target_pairs={{0,64},{16,80},{32,96},{48,112},{1,65},{17,81},{33,97},{49,113},{2... | collective-permute-start | bytes 1622024 | tf_op jit(solution)/shard_map/ppermute | solution.py:38
  73.4 23.4 %shard_map.83 = (bf16[528,512]{1,0:T(8,128)(2,1)S(1)}, bf16[528,512]{1,0:T(8,128)(2,1)S(1)}, bf16[528,512]{1,0:T(8,128)(2,1)S(1)}, bf16[528,512]{1,0:T(8,128)(2,1)S(1)}) custom-call(s32[4]{0:T(128)S(1)} %pad_add_fusion.info, s32[128]{0:T(128)S(1)} %maximum_convert_fusion.ids, bf16[528,512]{1,0:T(8,128)(2,1)S(1)} %shard_map.82.refs_0_.qa, ...), custom_call_target="tpu_custom_call" | custom-call | flops 1073741824 | bytes 12582912 | tf_op jit(solution)/shard_map/pallas_call | solution.py:355
  96.9 2.4 %collective-permute-start.17 = (bf16[528,512]{1,0:T(8,128)(2,1)S(1)}, bf16[528,512]{1,0:T(8,128)(2,1)S(1)}, u32[]{:S(2)}, u32[]{:S(2)}) collective-permute-start(bf16[528,512]{1,0:T(8,128)(2,1)S(1)} %get-tuple-element.29), channel_id=1, source_target_pairs={{0,96},{16,48},{32,0},{48,80},{64,32},{80,112},{96,64},{112,16},{1... | collective-permute-start | bytes 1622024 | tf_op jit(solution)/shard_map/ppermute | solution.py:38
  99.6 1.5 %collective-permute-start.19 = (bf16[528,512]{1,0:T(8,128)(2,1)S(1)}, bf16[528,512]{1,0:T(8,128)(2,1)S(1)}, u32[]{:S(2)}, u32[]{:S(2)}) collective-permute-start(bf16[528,512]{1,0:T(8,128)(2,1)S(1)} %get-tuple-element.31), channel_id=1, source_target_pairs={{0,64},{16,80},{32,96},{48,112},{64,0},{80,16},{96,32},{112,48},{1... | collective-permute-start | bytes 1622024 | tf_op jit(solution)/shard_map/ppermute | solution.py:38
  101.2 14.0 %collective-permute-done.17.m1 = bf16[528,512]{1,0:T(8,128)(2,1)S(1)} collective-permute-done((bf16[528,512]{1,0:T(8,128)(2,1)S(1)}, bf16[528,512]{1,0:T(8,128)(2,1)S(1)}, u32[]{:S(2)}, u32[]{:S(2)}) %collective-permute-start.17) | collective-permute-done | bytes 540704 | tf_op jit(solution)/shard_map/ppermute | solution.py:38
  115.1 4.7 %collective-permute-done.19.m3 = bf16[528,512]{1,0:T(8,128)(2,1)S(1)} collective-permute-done((bf16[528,512]{1,0:T(8,128)(2,1)S(1)}, bf16[528,512]{1,0:T(8,128)(2,1)S(1)}, u32[]{:S(2)}, u32[]{:S(2)}) %collective-permute-start.19) | collective-permute-done | bytes 540704 | tf_op jit(solution)/shard_map/ppermute | solution.py:38
  119.8 1.5 %shard_map.86 = (bf16[512,256]{1,0:T(8,128)(2,1)S(1)}, bf16[512,256]{1,0:T(8,128)(2,1)S(1)}) custom-call(s32[4]{0:T(128)S(1)} %pad_add_fusion.info, f32[8]{0:T(128)S(1)} %copy-done.2, bf16[528,512]{1,0:T(8,128)(2,1)S(1)} %get-tuple-element.28.m0, bf16[528,512]{1,0:T(8,128)(2,1)S(1)} %collective-permute-done.17.m1, ...), custom_call_target="tpu_custom_call" | custom-call | flops 5406720 | bytes 4325376 | tf_op jit(solution)/shard_map/pallas_call | solution.py:409
  121.3 4.7 %collective-permute-start.22 = (bf16[512,256]{1,0:T(8,128)(2,1)S(1)}, bf16[512,256]{1,0:T(8,128)(2,1)S(1)}, u32[]{:S(2)}, u32[]{:S(2)}) collective-permute-start(bf16[512,256]{1,0:T(8,128)(2,1)S(1)} %get-tuple-element.38), channel_id=1, source_target_pairs={{0,16},{16,0},{32,48},{48,32},{64,80},{80,64},{96,112},{112,96},{1... | collective-permute-start | bytes 786440 | tf_op jit(solution)/shard_map/ppermute | solution.py:38
  127.2 3.6 %shard_map.87 = bf16[256,2048]{1,0:T(8,128)(2,1)} custom-call(s32[4]{0:T(128)S(1)} %pad_add_fusion.info, bf16[512,256]{1,0:T(8,128)(2,1)S(1)} %get-tuple-element.37.own, bf16[512,256]{1,0:T(8,128)(2,1)S(1)} %collective-permute-done.22.oth, bf16[1024,2048]{1,0:T(8,128)(2,1)S(1)} %copy-done, bf16[1024,2048]{1,0:T(8,128)(2,1)S(1)} %copy-done), custom_call_target="tpu_custom_call" | custom-call | flops 1073741824 | bytes 4194304 | tf_op jit(solution)/shard_map/pallas_call | solution.py:432
  (47 shorter events, 6.5 us)
Async XLA Ops:
  0.0 27.9 %copy-start.1 = (bf16[1,256,2048]{2,1,0:T(8,128)(2,1)S(1)}, bf16[1,256,2048]{2,1,0:T(8,128)(2,1)}, u32[]{:S(2)}) copy-start(bf16[1,256,2048]{2,1,0:T(8,128)(2,1)} %param.10) | copy-start | bytes 3145732
  0.0 24.2 %copy-start.6 = (s32[1,2,8]{2,1,0:T(2,128)S(1)}, s32[1,2,8]{2,1,0:T(2,128)}, u32[]{:S(2)}) copy-start(s32[1,2,8]{2,1,0:T(2,128)} %param.11) | copy-start | bytes 196
  1.2 7.1 %collective-permute-start.5 = (bf16[1,2,128,512]{3,2,1,0:T(8,128)(2,1)S(1)}, bf16[1,2,128,512]{3,2,1,0:T(8,128)(2,1)S(1)}, u32[]{:S(2)}, u32[]{:S(2)}) collective-permute-start(bf16[1,2,128,512]{3,2,1,0:T(8,128)(2,1)S(1)} %get-tuple-element.40), channel_id=1, source_target_pairs={{0,4},{16,28},{32,36},{48,60},{64,68},{80,92},{96,100},{112,124},{... | collective-permute-start | bytes 786440 | tf_op jit(solution)/shard_map/ppermute | solution.py:38
  4.6 8.1 %collective-permute-start.11 = (bf16[1,2,128,512]{3,2,1,0:T(8,128)(2,1)S(1)}, bf16[1,2,128,512]{3,2,1,0:T(8,128)(2,1)S(1)}, u32[]{:S(2)}, u32[]{:S(2)}) collective-permute-start(bf16[1,2,128,512]{3,2,1,0:T(8,128)(2,1)S(1)} %get-tuple-element.39), channel_id=1, source_target_pairs={{0,1},{16,19},{32,33},{48,51},{64,65},{80,83},{96,97},{112,115},{1... | collective-permute-start | bytes 786440 | tf_op jit(solution)/shard_map/ppermute | solution.py:38
  8.3 19.6 %collective-permute-start = (bf16[256,2048]{1,0:T(8,128)(2,1)}, bf16[256,2048]{1,0:T(8,128)(2,1)S(1)}, u32[]{:S(2)}, u32[]{:S(2)}) collective-permute-start(bf16[256,2048]{1,0:T(8,128)(2,1)} %bitcast.14), channel_id=1, source_target_pairs={{0,16},{16,0},{32,48},{48,32},{64,80},{80,64},{96,112},{112,96},{1... | collective-permute-start | bytes 3145736 | tf_op jit(solution)/shard_map/ppermute | solution.py:38
  8.3 7.8 %collective-permute-start.6 = (bf16[1,2,128,512]{3,2,1,0:T(8,128)(2,1)S(1)}, bf16[1,2,128,512]{3,2,1,0:T(8,128)(2,1)S(1)}, u32[]{:S(2)}, u32[]{:S(2)}) collective-permute-start(bf16[1,2,128,512]{3,2,1,0:T(8,128)(2,1)S(1)} %get-tuple-element.40), channel_id=1, source_target_pairs={{0,12},{16,20},{32,44},{48,52},{64,76},{80,84},{96,108},{112,116},... | collective-permute-start | bytes 786440 | tf_op jit(solution)/shard_map/ppermute | solution.py:38
  8.3 7.8 %collective-permute-start.7 = (bf16[1,2,128,512]{3,2,1,0:T(8,128)(2,1)S(1)}, bf16[1,2,128,512]{3,2,1,0:T(8,128)(2,1)S(1)}, u32[]{:S(2)}, u32[]{:S(2)}) collective-permute-start(bf16[1,2,128,512]{3,2,1,0:T(8,128)(2,1)S(1)} %collective-permute-done.5), channel_id=1, source_target_pairs={{0,4},{16,28},{32,36},{48,60},{64,68},{80,92},{96,100},{112,124},{... | collective-permute-start | bytes 786440 | tf_op jit(solution)/shard_map/ppermute | solution.py:38
  11.3 8.6 %collective-permute-start.12 = (bf16[1,2,128,512]{3,2,1,0:T(8,128)(2,1)S(1)}, bf16[1,2,128,512]{3,2,1,0:T(8,128)(2,1)S(1)}, u32[]{:S(2)}, u32[]{:S(2)}) collective-permute-start(bf16[1,2,128,512]{3,2,1,0:T(8,128)(2,1)S(1)} %get-tuple-element.39), channel_id=1, source_target_pairs={{0,3},{16,17},{32,35},{48,49},{64,67},{80,81},{96,99},{112,113},{1... | collective-permute-start | bytes 786440 | tf_op jit(solution)/shard_map/ppermute | solution.py:38
  12.6 9.3 %collective-permute-start.13 = (bf16[1,2,128,512]{3,2,1,0:T(8,128)(2,1)S(1)}, bf16[1,2,128,512]{3,2,1,0:T(8,128)(2,1)S(1)}, u32[]{:S(2)}, u32[]{:S(2)}) collective-permute-start(bf16[1,2,128,512]{3,2,1,0:T(8,128)(2,1)S(1)} %collective-permute-done.11), channel_id=1, source_target_pairs={{0,1},{16,19},{32,33},{48,51},{64,65},{80,83},{96,97},{112,115},{1... | collective-permute-start | bytes 786440 | tf_op jit(solution)/shard_map/ppermute | solution.py:38
  16.3 17.8 %collective-permute-start.8 = (bf16[4,2,128,512]{3,2,1,0:T(8,128)(2,1)S(1)}, bf16[4,2,128,512]{3,2,1,0:T(8,128)(2,1)}, u32[]{:S(2)}, u32[]{:S(2)}) collective-permute-start(bf16[4,2,128,512]{3,2,1,0:T(8,128)(2,1)S(1)} %pad_maximum_fusion.refs_4_), channel_id=1, source_target_pairs={{0,1},{16,19},{32,33},{48,51},{64,65},{80,83},{96,97},{112,115},{1... | collective-permute-start | bytes 3145736 | tf_op jit(solution)/shard_map/ppermute | solution.py:38
  23.0 14.3 %collective-permute-start.14 = (bf16[4,2,128,512]{3,2,1,0:T(8,128)(2,1)}, bf16[4,2,128,512]{3,2,1,0:T(8,128)(2,1)}, u32[]{:S(2)}, u32[]{:S(2)}) collective-permute-start(bf16[4,2,128,512]{3,2,1,0:T(8,128)(2,1)} %pad_maximum_fusion.1.refs_8_), channel_id=1, source_target_pairs={{0,4},{16,28},{32,36},{48,60},{64,68},{80,92},{96,100},{112,124},{... | collective-permute-start | bytes 3145736 | tf_op jit(solution)/shard_map/ppermute | solution.py:38
  24.3 3.6 %collective-permute-start.1 = (s32[1,16]{1,0:T(1,128)S(1)}, s32[1,16]{1,0:T(1,128)S(1)}, u32[]{:S(2)}, u32[]{:S(2)}) collective-permute-start(s32[1,16]{1,0:T(1,128)S(1)} %concatenate.25), channel_id=1, source_target_pairs={{0,16},{16,0},{32,48},{48,32},{64,80},{80,64},{96,112},{112,96},{1... | collective-permute-start | bytes 200 | tf_op jit(solution)/shard_map/ppermute | solution.py:38
  31.2 12.0 %collective-permute-start.3 = (bf16[528,512]{1,0:T(8,128)(2,1)S(1)}, bf16[528,512]{1,0:T(8,128)(2,1)S(1)}, u32[]{:S(2)}, u32[]{:S(2)}) collective-permute-start(bf16[528,512]{1,0:T(8,128)(2,1)S(1)} %shard_map.82.refs_0_.qa), channel_id=1, source_target_pairs={{0,96},{16,48},{32,0},{48,80},{64,32},{80,112},{96,64},{112,16},{1... | collective-permute-start | bytes 1622024 | tf_op jit(solution)/shard_map/ppermute | solution.py:38
  32.6 13.8 %collective-permute-start.2 = (bf16[528,512]{1,0:T(8,128)(2,1)S(1)}, bf16[528,512]{1,0:T(8,128)(2,1)S(1)}, u32[]{:S(2)}, u32[]{:S(2)}) collective-permute-start(bf16[528,512]{1,0:T(8,128)(2,1)S(1)} %shard_map.82.refs_0_.qa), channel_id=1, source_target_pairs={{0,32},{16,112},{32,64},{48,16},{64,96},{80,48},{96,0},{112,80},{1... | collective-permute-start | bytes 1622024 | tf_op jit(solution)/shard_map/ppermute | solution.py:38
  34.1 36.3 %collective-permute-start.9 = (bf16[4,2,128,512]{3,2,1,0:T(8,128)(2,1)S(1)}, bf16[4,2,128,512]{3,2,1,0:T(8,128)(2,1)S(1)}, u32[]{:S(2)}, u32[]{:S(2)}) collective-permute-start(bf16[4,2,128,512]{3,2,1,0:T(8,128)(2,1)S(1)} %pad_maximum_fusion.refs_4_), channel_id=1, source_target_pairs={{0,3},{16,17},{32,35},{48,49},{64,67},{80,81},{96,99},{112,113},{1... | collective-permute-start | bytes 3145736 | tf_op jit(solution)/shard_map/ppermute | solution.py:38
  34.1 38.0 %collective-permute-start.15 = (bf16[4,2,128,512]{3,2,1,0:T(8,128)(2,1)}, bf16[4,2,128,512]{3,2,1,0:T(8,128)(2,1)S(1)}, u32[]{:S(2)}, u32[]{:S(2)}) collective-permute-start(bf16[4,2,128,512]{3,2,1,0:T(8,128)(2,1)} %pad_maximum_fusion.1.refs_8_), channel_id=1, source_target_pairs={{0,12},{16,20},{32,44},{48,52},{64,76},{80,84},{96,108},{112,116},... | collective-permute-start | bytes 3145736 | tf_op jit(solution)/shard_map/ppermute | solution.py:38
  37.2 34.9 %collective-permute-start.10 = (bf16[4,2,128,512]{3,2,1,0:T(8,128)(2,1)}, bf16[4,2,128,512]{3,2,1,0:T(8,128)(2,1)S(1)}, u32[]{:S(2)}, u32[]{:S(2)}) collective-permute-start(bf16[4,2,128,512]{3,2,1,0:T(8,128)(2,1)} %collective-permute-done.8.refs_5_), channel_id=1, source_target_pairs={{0,1},{16,19},{32,33},{48,51},{64,65},{80,83},{96,97},{112,115},{1... | collective-permute-start | bytes 3145736 | tf_op jit(solution)/shard_map/ppermute | solution.py:38
  43.2 30.0 %collective-permute-start.16 = (bf16[4,2,128,512]{3,2,1,0:T(8,128)(2,1)}, bf16[4,2,128,512]{3,2,1,0:T(8,128)(2,1)}, u32[]{:S(2)}, u32[]{:S(2)}) collective-permute-start(bf16[4,2,128,512]{3,2,1,0:T(8,128)(2,1)} %collective-permute-done.14.refs_9_), channel_id=1, source_target_pairs={{0,4},{16,28},{32,36},{48,60},{64,68},{80,92},{96,100},{112,124},{... | collective-permute-start | bytes 3145736 | tf_op jit(solution)/shard_map/ppermute | solution.py:38
  46.3 8.9 %collective-permute-start.4 = (bf16[528,512]{1,0:T(8,128)(2,1)S(1)}, bf16[528,512]{1,0:T(8,128)(2,1)S(1)}, u32[]{:S(2)}, u32[]{:S(2)}) collective-permute-start(bf16[528,512]{1,0:T(8,128)(2,1)S(1)} %collective-permute-done.2.refs_1_.q1), channel_id=1, source_target_pairs={{0,32},{16,112},{32,64},{48,16},{64,96},{80,48},{96,0},{112,80},{1... | collective-permute-start | bytes 1622024 | tf_op jit(solution)/shard_map/ppermute | solution.py:38
  67.4 33.7 %collective-permute-start.20 = (bf16[528,512]{1,0:T(8,128)(2,1)S(1)}, bf16[528,512]{1,0:T(8,128)(2,1)S(1)}, u32[]{:S(2)}, u32[]{:S(2)}) collective-permute-start(bf16[528,512]{1,0:T(8,128)(2,1)S(1)} %get-tuple-element.35), channel_id=1, source_target_pairs={{0,32},{16,48},{32,64},{48,80},{64,96},{80,112},{1,33},{17,49},{33... | collective-permute-start | bytes 1622024 | tf_op jit(solution)/shard_map/ppermute | solution.py:38
  70.4 2.7 %copy-start.3 = (bf16[4,2,128,512]{3,2,1,0:T(8,128)(2,1)}, bf16[4,2,128,512]{3,2,1,0:T(8,128)(2,1)S(1)}, u32[]{:S(2)}) copy-start(bf16[4,2,128,512]{3,2,1,0:T(8,128)(2,1)S(1)} %collective-permute-done.9.refs_6_) | copy-start | bytes 3145732
  70.4 49.4 %copy-start.2 = (f32[8]{0:T(128)S(1)}, f32[8]{0:T(128)}, u32[]{:S(2)}) copy-start(f32[8]{0:T(128)} %gate.1) | copy-start | bytes 100
  70.4 30.7 %collective-permute-start.21 = (bf16[528,512]{1,0:T(8,128)(2,1)S(1)}, bf16[528,512]{1,0:T(8,128)(2,1)S(1)}, u32[]{:S(2)}, u32[]{:S(2)}) collective-permute-start(bf16[528,512]{1,0:T(8,128)(2,1)S(1)} %get-tuple-element.36), channel_id=1, source_target_pairs={{0,64},{16,80},{32,96},{48,112},{1,65},{17,81},{33,97},{49,113},{2... | collective-permute-start | bytes 1622024 | tf_op jit(solution)/shard_map/ppermute | solution.py:38
  72.1 1.3 %copy-start.4 = (bf16[4,2,128,512]{3,2,1,0:T(8,128)(2,1)}, bf16[4,2,128,512]{3,2,1,0:T(8,128)(2,1)S(1)}, u32[]{:S(2)}) copy-start(bf16[4,2,128,512]{3,2,1,0:T(8,128)(2,1)S(1)} %collective-permute-done.15.refs_10_) | copy-start | bytes 3145732
  72.1 1.0 copy-start.5
  73.4 53.7 %copy-start = (bf16[1024,2048]{1,0:T(8,128)(2,1)S(1)}, bf16[1024,2048]{1,0:T(8,128)(2,1)}, u32[]{:S(2)}) copy-start(bf16[1024,2048]{1,0:T(8,128)(2,1)} %w_oth.1) | copy-start | bytes 12582916
  96.9 18.2 %collective-permute-start.17 = (bf16[528,512]{1,0:T(8,128)(2,1)S(1)}, bf16[528,512]{1,0:T(8,128)(2,1)S(1)}, u32[]{:S(2)}, u32[]{:S(2)}) collective-permute-start(bf16[528,512]{1,0:T(8,128)(2,1)S(1)} %get-tuple-element.29), channel_id=1, source_target_pairs={{0,96},{16,48},{32,0},{48,80},{64,32},{80,112},{96,64},{112,16},{1... | collective-permute-start | bytes 1622024 | tf_op jit(solution)/shard_map/ppermute | solution.py:38
  99.3 15.8 %collective-permute-start.18 = (bf16[528,512]{1,0:T(8,128)(2,1)S(1)}, bf16[528,512]{1,0:T(8,128)(2,1)S(1)}, u32[]{:S(2)}, u32[]{:S(2)}) collective-permute-start(bf16[528,512]{1,0:T(8,128)(2,1)S(1)} %get-tuple-element.30), channel_id=1, source_target_pairs={{0,32},{16,112},{32,64},{48,16},{64,96},{80,48},{96,0},{112,80},{1... | collective-permute-start | bytes 1622024 | tf_op jit(solution)/shard_map/ppermute | solution.py:38
  99.6 20.2 %collective-permute-start.19 = (bf16[528,512]{1,0:T(8,128)(2,1)S(1)}, bf16[528,512]{1,0:T(8,128)(2,1)S(1)}, u32[]{:S(2)}, u32[]{:S(2)}) collective-permute-start(bf16[528,512]{1,0:T(8,128)(2,1)S(1)} %get-tuple-element.31), channel_id=1, source_target_pairs={{0,64},{16,80},{32,96},{48,112},{64,0},{80,16},{96,32},{112,48},{1... | collective-permute-start | bytes 1622024 | tf_op jit(solution)/shard_map/ppermute | solution.py:38
  121.3 5.9 %collective-permute-start.22 = (bf16[512,256]{1,0:T(8,128)(2,1)S(1)}, bf16[512,256]{1,0:T(8,128)(2,1)S(1)}, u32[]{:S(2)}, u32[]{:S(2)}) collective-permute-start(bf16[512,256]{1,0:T(8,128)(2,1)S(1)} %get-tuple-element.38), channel_id=1, source_target_pairs={{0,16},{16,0},{32,48},{48,32},{64,80},{80,64},{96,112},{112,96},{1... | collective-permute-start | bytes 786440 | tf_op jit(solution)/shard_map/ppermute | solution.py:38

commit v2 on v1

v2 whole, which is shorter than its diff:
```python
import functools

import jax
import jax.numpy as jnp
from jax import lax
from jax.experimental import pallas as pl
from jax.experimental.pallas import tpu as pltpu
from jax.sharding import PartitionSpec as P

RING = 4
HD = 128
FEAT = 512
HEADS = FEAT // HD
GROUP = 2
UNROLL = 4
TOK = 256
CHIP = 512
BLK = 128
STAT = 16
SLAB = FEAT + STAT
NEG = -1e30
F32 = jnp.float32
BF16 = jnp.bfloat16
LOG2E = 1.4426950408889634
VMEM = 24 * 1024 * 1024
WIDE_VMEM = 60 * 1024 * 1024


def index_of(x, y, z, c):
    return (y * 2 + c) * RING * RING + x * RING + z


def send(array, move):
    pairs = []
    for x in range(RING):
        for z in range(RING):
            for y in range(RING):
                for c in range(2):
                    to = move(x, y, z, c)
                    if to is not None:
                        pairs.append((index_of(x, y, z, c), index_of(*to)))
    return lax.ppermute(array, ("seq", "mem"), pairs)


def gather_move(phase, distance):
    def move(x, y, z, c):
        if (phase == 0) == (c == 0):
            return ((x + distance) % RING, y, z, c)
        return (x, y, (z + distance) % RING, c)

    return move


def around(distance):
    def move(x, y, z, c):
        return (x, (y + (distance if c == 0 else -distance)) % RING, z, c)

    return move


def later1(x, y, z, c):
    return (x, y + 1, z, c) if y + 1 < RING else None


def later2(x, y, z, c):
    return (x, y + 2, z, c) if y + 2 < RING else None


def core(x, y, z, c):
    return (x, y, z, 1 - c)


def params(limit=VMEM):
    return pltpu.CompilerParams(vmem_limit_bytes=limit)


def after(value, *earlier):
    return lax.optimization_barrier((value, earlier))[0]


def cost(flops, nbytes, trans=0):
    return pl.CostEstimate(flops=flops, bytes_accessed=nbytes, transcendentals=trans)


def any_specs(count):
    return [pl.BlockSpec(memory_space=pl.ANY)] * count


def dot(a, b, ca, cb):
    return lax.dot_general(a, b, (((ca,), (cb,)), ((), ())), preferred_element_type=F32)


def query_kernel(info, own, oth, w, ids, out):
    out[0:TOK, :] = dot(own[...], w[...], 1, 0).astype(BF16)
    out[TOK:CHIP, :] = dot(oth[...], w[...], 1, 0).astype(BF16)
    out[CHIP:, :] = ids[...]


def project_query(info, own, oth, w, ids):
    depth = own.shape[1]
    tile = 256
    steps = FEAT // tile
    whole = pl.BlockSpec((TOK, depth), lambda j, info: (0, 0))
    return pl.pallas_call(
        query_kernel,
        grid_spec=pltpu.PrefetchScalarGridSpec(
            num_scalar_prefetch=1,
            grid=(steps,),
            in_specs=[
                whole,
                whole,
                pl.BlockSpec((depth, tile), lambda j, info: (0, info[3] * steps + j)),
                pl.BlockSpec((STAT, tile), lambda j, info: (0, j)),
            ],
            out_specs=pl.BlockSpec((CHIP + STAT, tile), lambda j, info: (0, j)),
        ),
        out_shape=jax.ShapeDtypeStruct((CHIP + STAT, FEAT), BF16),
        compiler_params=params(WIDE_VMEM),
        cost_estimate=cost(2 * CHIP * depth * FEAT, 2 * depth * (FEAT + CHIP)),
    )(info, own, oth, w, ids)


def keyvalue_kernel(info, own, oth, wk, wv, k, v):
    for tok, place in ((own, slice(0, TOK)), (oth, slice(TOK, CHIP))):
        k[place, :] = dot(tok[...], wk[...], 1, 0).astype(BF16)
        v[:, place] = dot(tok[...], wv[...], 1, 0).astype(BF16).T


def project_keyvalue(info, own, oth, wk, wv):
    depth = own.shape[1]
    tile = 256
    steps = FEAT // tile
    whole = pl.BlockSpec((TOK, depth), lambda j, info: (0, 0))
    weight = pl.BlockSpec((depth, tile), lambda j, info: (0, info[3] * steps + j))
    result = pl.BlockSpec((CHIP, tile), lambda j, info: (0, j))
    return pl.pallas_call(
        keyvalue_kernel,
        grid_spec=pltpu.PrefetchScalarGridSpec(
            num_scalar_prefetch=1,
            grid=(steps,),
            in_specs=[whole, whole, weight, weight],
            out_specs=[result, pl.BlockSpec((tile, CHIP), lambda j, info: (j, 0))],
        ),
        out_shape=[jax.ShapeDtypeStruct((CHIP, FEAT), BF16)] * 2,
        compiler_params=params(WIDE_VMEM),
        cost_estimate=cost(4 * CHIP * depth * FEAT, 2 * depth * (2 * FEAT + CHIP)),
    )(info, own, oth, wk, wv)


def split3(value):
    high = value.astype(BF16).astype(F32)
    rest = value - high
    mid = rest.astype(BF16).astype(F32)
    return high, mid, rest - mid


def pack_stats(values, width):
    row = lax.broadcasted_iota(jnp.int32, (STAT, width), 0)
    packed = jnp.zeros((STAT, width), F32)
    for h, value in enumerate(values):
        for i, part in enumerate(split3(value)):
            packed = jnp.where(row == 3 * h + i, part, packed)
    return packed.astype(BF16)


def local_block(distance, info, q, k, v, out):
    c = info[3]
    factor = HD ** -0.5 * LOG2E
    key = lax.broadcasted_iota(jnp.int32, (TOK, TOK), 0)
    ask = lax.broadcasted_iota(jnp.int32, (TOK, TOK), 1)
    valid = {0: ask >= key, 1: None, 2: ask < key}[distance]

    def half(place, halves):
        rows = slice(place * TOK, (place + 1) * TOK)
        stats = []
        for h in range(HEADS):
            cols = slice(h * HD, (h + 1) * HD)
            scores = []
            for i in halves:
                s = dot(k[i * TOK : (i + 1) * TOK, cols], q[rows, cols], 1, 1) * factor
                if i == place and valid is not None:
                    s = jnp.where(valid, s, NEG)
                scores.append(s)
            m = jnp.max(functools.reduce(jnp.maximum, scores), axis=0, keepdims=True)
            probs = [jnp.exp2(s - m) for s in scores]
            total = jnp.sum(functools.reduce(jnp.add, probs), axis=0, keepdims=True)
            parts = [
                dot(v[cols, i * TOK : (i + 1) * TOK], p.astype(BF16), 1, 0)
                for i, p in zip(halves, probs)
            ]
            mix = functools.reduce(jnp.add, parts)
            out[cols, rows] = (mix * (1.0 / total)).astype(BF16)
            stats.append(m + jnp.log2(total))
        out[FEAT:, rows] = pack_stats(stats, TOK)

    for place in range(2):
        if distance == 1:
            half(place, (0, 1))
            continue
        later = (place + c) == 1
        both = later if distance == 0 else jnp.logical_not(later)
        pl.when(both)(functools.partial(half, place, (0, 1)))
        pl.when(jnp.logical_not(both))(functools.partial(half, place, (place,)))


def same_kernel(info, q, k, v, out):
    local_block(0, info, q, k, v, out)


def next_kernel(info, q1, q2, q3, k, v, out1, out2):
    y, c = info[1], info[3]
    for near, here in ((q2, c == 0), (q1, c != 0)):

        @pl.when((y + 1 < RING) & here)
        def _():
            local_block(1, info, near, k, v, out1)

    @pl.when(y + 2 < RING)
    def _():
        local_block(2, info, q3, k, v, out2)


def local_attention(kernel, info, queries, k, v, count):
    slab = jax.ShapeDtypeStruct((SLAB, CHIP), BF16)

    def whole(array):
        return pl.BlockSpec(array.shape, lambda j, info: (0, 0))

    return pl.pallas_call(
        kernel,
        grid_spec=pltpu.PrefetchScalarGridSpec(
            num_scalar_prefetch=1,
            grid=(1,),
            in_specs=[whole(a) for a in (*queries, k, v)],
            out_specs=[whole(slab)] * count,
        ),
        out_shape=[slab] * count,
        compiler_params=params(),
        cost_estimate=cost(4 * count * CHIP * CHIP * FEAT, 8 * CHIP * FEAT, 4 * CHIP * CHIP),
    )(info, *queries, k, v)


def part_kernel(info, mem, out, held, sem):
    start = pl.multiple_of(info[3] * FEAT, FEAT)
    src = mem.at[pl.ds(2 * info[1], 2), :, :, pl.ds(start, FEAT)]
    copy = pltpu.make_async_copy(src, held, sem)
    copy.start()
    copy.wait()
    for block in range(2):
        for h in range(HEADS):
            cols = slice(h * HD, (h + 1) * HD)
            out[0, h // GROUP, block, 0, h % GROUP] = held[block, 0, :, cols]
            out[0, h // GROUP, block, 1, h % GROUP] = held[block, 1, :, cols].T


def take_part(info, memory):
    shape = (1, HEADS // GROUP, 2, 2, GROUP, BLK, HD)
    return pl.pallas_call(
        part_kernel,
        grid_spec=pltpu.PrefetchScalarGridSpec(
            num_scalar_prefetch=1,
            grid=(1,),
            in_specs=[pl.BlockSpec(memory_space=pltpu.HBM)],
            out_specs=pl.BlockSpec(shape, lambda j, info: (0,) * 7),
            scratch_shapes=[
                pltpu.VMEM((2, 2, BLK, FEAT), BF16),
                pltpu.SemaphoreType.DMA,
            ],
        ),
        out_shape=jax.ShapeDtypeStruct(shape, BF16),
        compiler_params=params(WIDE_VMEM),
        cost_estimate=cost(0, 2**20),
    )(info, memory)


def plan_kernel(info, ids, slots, blocks):
    x, y, z, c = info[0], info[1], info[2], info[3]
    order = 120
    shift_x = jnp.where(c == 0, 0, 2)

    def look(n, used):
        count = used
        for t in range(8):
            ident = ids[n * 8 + t]
            ax = (order >> ((((ident >> 5) - x) & 3) * 2)) & 3
            az = (order >> (((((ident >> 3) & 3) - z) & 3) * 2)) & 3
            slot = (ax << shift_x) + (az << (2 - shift_x))
            slots[count] = slot * 2 + (ident & 1)
            blocks[count >> 1] = n
            count = count + (((ident >> 1) & 3) == y).astype(jnp.int32)
        slots[count] = 32
        return count + (count & 1)

    used = lax.fori_loop(0, 16, look, 0)
    units = used >> 1
    for u in range(UNROLL - 1):
        blocks[units + u] = 16
        slots[used + 2 * u] = 0
        slots[used + 2 * u + 1] = 32
    blocks[79] = (units + UNROLL - 1) // UNROLL


def plan_units(info, ids):
    smem = pl.BlockSpec(memory_space=pltpu.SMEM)
    return pl.pallas_call(
        plan_kernel,
        in_specs=[smem] * 2,
        out_specs=[smem] * 2,
        out_shape=[
            jax.ShapeDtypeStruct((144,), jnp.int32),
            jax.ShapeDtypeStruct((80,), jnp.int32),
        ],
        compiler_params=params(),
        cost_estimate=cost(1000, 1000),
    )(info, ids)


def memory_kernel(group, slots, blocks, *refs):
    queries, parts, outs = refs[:4], refs[4:8], refs[8:12]
    q, mem, acc, top, low, o, sem, osem = refs[12:]
    wide = GROUP * HD
    copies = [
        pltpu.make_async_copy(ref, mem.at[pl.ds(4 * s, 4)], sem.at[4 + s])
        for s, ref in enumerate(parts)
    ]
    for s, ref in enumerate(queries):
        src = ref.at[pl.ds(0, CHIP), pl.ds(group * wide, wide)]
        copies.append(pltpu.make_async_copy(src, q.at[s], sem.at[s]))
    for copy in copies:
        copy.start()

    acc[...] = jnp.zeros_like(acc)
    top[...] = jnp.full_like(top, NEG)
    low[...] = jnp.zeros_like(low)
    for copy in copies:
        copy.wait()

    factor = HD ** -0.5 * LOG2E

    def pair(i, carry):
        work = []
        for u in [UNROLL * i + k for k in range(UNROLL)]:
            n = blocks[u]
            from_q = jnp.minimum(n, 15)
            start = pl.multiple_of((from_q & 3) * BLK, BLK)
            second = slots[2 * u + 1]
            work.append((n, from_q >> 2, start, slots[2 * u], second & 31, second < 32))
        scores = {}
        for j, (n, s, start, one, two, full) in enumerate(work):
            for h in range(GROUP):
                keys = jnp.concatenate([mem[one >> 1, one & 1, 0, h], mem[two >> 1, two & 1, 0, h]], axis=0)
                qh = q[s, pl.ds(start, BLK), h * HD : (h + 1) * HD]
                scores[j, h] = dot(keys, qh, 1, 1) * factor
        for j, (n, s, start, one, two, full) in enumerate(work):
            for h in range(GROUP):
                first, last = scores[j, h][:BLK], scores[j, h][BLK:]
                last = jnp.where(full, last, NEG)
                m_old = top[n, h]
                m = jnp.max(jnp.maximum(first, last), axis=0, keepdims=True)
                m = jnp.maximum(m_old, m)
                p = jnp.concatenate([jnp.exp2(first - m), jnp.exp2(last - m)], axis=0)
                alpha = jnp.exp2(m_old - m)
                top[n, h] = m
                low[n, h] = low[n, h] * alpha + jnp.sum(p, axis=0, keepdims=True)
                values = jnp.concatenate([mem[one >> 1, one & 1, 1, h], mem[two >> 1, two & 1, 1, h]], axis=1)
                acc[n, h] = acc[n, h] * alpha + dot(values, p.astype(BF16), 1, 0)
        return carry

    lax.fori_loop(0, blocks[79], pair, 0)

    backs = [
        pltpu.make_async_copy(o.at[s], ref, osem.at[s]) for s, ref in enumerate(outs)
    ]
    for s in (3, 1, 2, 0):
        for b in range(4):
            n = s * 4 + b
            cols = slice(b * BLK, (b + 1) * BLK)
            stats = []
            for h in range(GROUP):
                total = low[n, h]
                some = total > 0.0
                total = jnp.where(some, total, 1.0)
                o[s, h * HD : (h + 1) * HD, cols] = (acc[n, h] * (1.0 / total)).astype(BF16)
                stats.append(jnp.where(some, top[n, h] + jnp.log2(total), NEG))
            o[s, wide:, cols] = pack_stats(stats, BLK)
        backs[s].start()
    for copy in backs:
        copy.wait()


def memory_attention(group, plan, queries, parts):
    wide = GROUP * HD
    slab = jax.ShapeDtypeStruct((wide + STAT, CHIP), BF16)
    return pl.pallas_call(
        functools.partial(memory_kernel, group),
        grid_spec=pltpu.PrefetchScalarGridSpec(
            num_scalar_prefetch=2,
            grid=(1,),
            in_specs=any_specs(8),
            out_specs=any_specs(4),
            scratch_shapes=[
                pltpu.VMEM((4, CHIP, wide), BF16),
                pltpu.VMEM((16, 2, 2, GROUP, BLK, HD), BF16),
                pltpu.VMEM((17, GROUP, HD, BLK), F32),
                pltpu.VMEM((17, GROUP, 1, BLK), F32),
                pltpu.VMEM((17, GROUP, 1, BLK), F32),
                pltpu.VMEM((4, wide + STAT, CHIP), BF16),
                pltpu.SemaphoreType.DMA((8,)),
                pltpu.SemaphoreType.DMA((4,)),
            ],
        ),
        out_shape=[slab] * 4,
        compiler_params=params(),
        cost_estimate=cost(32 * 4 * BLK * BLK * wide, 24 * 1024 * wide, 32 * 4 * BLK * BLK),
    )(*plan, *queries, *parts)


def merge_kernel(info, gate, *refs):
    y = info[1]
    groups = HEADS // GROUP
    own, oth = refs[-2:]
    local = refs[4 * groups : 4 * groups + 3]

    def merged(refs, shown, h, stats, share):
        logs = []
        for ref, show in zip(refs, shown):
            rows = ref[stats:, :].astype(F32)
            log = rows[3 * h : 3 * h + 1] + rows[3 * h + 1 : 3 * h + 2]
            log = log + rows[3 * h + 2 : 3 * h + 3]
            logs.append(log if show is None else jnp.where(show, log, NEG))
        top = functools.reduce(jnp.maximum, logs)
        weights = [jnp.exp2(log - top) for log in logs]
        scale = share / functools.reduce(jnp.add, weights)
        total = None
        for ref, weight in zip(refs, weights):
            term = ref[h * HD : (h + 1) * HD, :].astype(F32) * (weight * scale)
            total = term if total is None else total + term
        return total

    for h in range(HEADS):
        g = jax.nn.sigmoid(jnp.full((1, CHIP), gate[info[3] * HEADS + h], F32))
        first = h // GROUP * 4
        mix = merged(refs[first : first + 4], (None,) * 4, h % GROUP, GROUP * HD, g)
        mix = mix + merged(local, (None, y >= 1, y >= 2), h, FEAT, 1.0 - g)
        mix = mix.astype(BF16)
        own[:, h * HD : (h + 1) * HD] = mix[:, :TOK].T
        oth[:, h * HD : (h + 1) * HD] = mix[:, TOK:].T


def merge(info, gate, slabs):
    half = pl.BlockSpec((TOK, FEAT), lambda j, info, gate: (0, 0))
    return pl.pallas_call(
        merge_kernel,
        grid_spec=pltpu.PrefetchScalarGridSpec(
            num_scalar_prefetch=2,
            grid=(1,),
            in_specs=[pl.BlockSpec(s.shape, lambda j, info, gate: (0, 0)) for s in slabs],
            out_specs=[half] * 2,
        ),
        out_shape=[jax.ShapeDtypeStruct((TOK, FEAT), BF16)] * 2,
        compiler_params=params(),
        cost_estimate=cost(20 * SLAB * CHIP, 8 * 2 * SLAB * CHIP),
    )(info, gate, *slabs)


def output_kernel(info, own, oth, w_own, w_oth, out):
    total = dot(own[...], w_own[...], 1, 0) + dot(oth[...], w_oth[...], 1, 0)
    out[...] = total.astype(BF16)


def project_output(info, own, oth, w):
    width = w.shape[1]
    tile = 512
    half = pl.BlockSpec((TOK, FEAT), lambda j, info: (0, 0))
    return pl.pallas_call(
        output_kernel,
        grid_spec=pltpu.PrefetchScalarGridSpec(
            num_scalar_prefetch=1,
            grid=(width // tile,),
            in_specs=[
                half,
                half,
                pl.BlockSpec((FEAT, tile), lambda j, info: (info[3], j)),
                pl.BlockSpec((FEAT, tile), lambda j, info: (1 - info[3], j)),
            ],
            out_specs=pl.BlockSpec((TOK, tile), lambda j, info: (0, j)),
        ),
        out_shape=jax.ShapeDtypeStruct((TOK, width), BF16),
        compiler_params=params(),
        cost_estimate=cost(4 * TOK * FEAT * width, 4 * FEAT * width),
    )(info, own, oth, w, w)


def shards(tokens, block_ids, memory, w_query, w_key, w_value, w_out, gate_bias):
    mem = lax.axis_index("mem")
    seq = lax.axis_index("seq")
    y, c = seq // 2, seq % 2
    info = jnp.stack([mem // RING, y, mem % RING, c]).astype(jnp.int32)

    own = tokens[0]
    oth = send(own, core)
    ids_own = block_ids.reshape(1, 16)
    ids_chip = jnp.concatenate([ids_own, send(ids_own, core)], axis=1)
    ids_rows = jnp.zeros((STAT, FEAT), BF16).at[0:1, 0:32].set(ids_chip.astype(BF16))

    groups = HEADS // GROUP
    part = take_part(info, memory)
    near = [part] + [send(part, gather_move(0, d)) for d in (1, -1, 2)]

    query = project_query(info, own, oth, w_query, ids_rows)
    query1 = send(query, around(1))
    query2 = send(query, around(-1))
    k, v = project_keyvalue(info, own, oth, w_key, w_value)
    query3 = send(query1, around(1))
    queries = [query, query1, query2, query3]
    near = after(near, query, k)

    parts = []
    for g in range(groups):
        mine = jnp.concatenate([part[:, g] for part in near])
        below = send(mine, gather_move(1, 1))
        above = send(mine, gather_move(1, -1))
        far = send(below, gather_move(1, 1)) if g % 2 == 0 else send(above, gather_move(1, -1))
        parts.append((mine, below, above, far))

    (local0,) = local_attention(same_kernel, info, [query], k, v, 1)
    ids = jnp.concatenate([q[CHIP, 0:32] for q in queries]).astype(jnp.int32)
    plan = plan_units(info, ids)
    local1, local2 = local_attention(next_kernel, info, queries[1:], k, v, 2)
    local1 = send(local1, later1)
    local2 = send(local2, later2)

    slabs = []
    for g in range(groups):
        mine, one, two, far = memory_attention(g, plan, queries, parts[g])
        slabs += [mine, send(one, around(-1)), send(two, around(1)), send(far, around(2))]
    mix_own, mix_oth = merge(info, gate_bias, slabs + [local0, local1, local2])
    mix_oth = send(mix_oth, core)
    return project_output(info, mix_own, mix_oth, w_out)[None]


def solution(mesh):
    in_specs = (
        P("mem", "seq", None),
        P("mem", "seq", None),
        P("mem", None, None, None),
        P(),
        P(),
        P(),
        P(),
        P(),
    )
    out_specs = P("mem", "seq", None)
    return jax.shard_map(shards, mesh=mesh, in_specs=in_specs, out_specs=out_specs, check_vma=False)
```

time: 132 us -> 114 us (0.86)
  starting transfers between devices: 47.4 us -> 34.1 us
  Pallas kernels: 48.7 us -> 43.3 us
    ppermute x23, starting transfers between devices: 47.4 us -> 34.1 us  [send(): return lax.ppermute(array, ('seq', 'mem'), pairs)]
    pallas_call x2 -> x6, Pallas kernels: 35.6 us -> 26.9 us  [the longest x2 11.3 us: memory_attention(): pl.pallas_call(functools.partial(memory_kernel, group), grid_spec=pltpu.P...]
    pallas_call x1, Pallas kernels: 4.72 us -> 6.44 us  [project_keyvalue(): pl.pallas_call(keyvalue_kernel, grid_spec=pltpu.PrefetchScalarGridSpec(nu...]
    pallas_call x1, Pallas kernels: 3.25 us -> 4.78 us  [project_query(): pl.pallas_call(query_kernel, grid_spec=pltpu.PrefetchScalarGridSpec(num_s...]
  transfers between devices with their start and end apart: 23 -> 23, of which waited for: 10 -> 9; matrix products, arithmetic and copies ran while one was open for 1% -> 1% of each run, Pallas kernels for 33% -> 34%
where the time goes in v2:
time: 114 us; the launch traced here: 112 us
  Pallas kernels  43.3 us (38%)
  starting transfers between devices  34.1 us (30%)
  waiting for transfers between devices  31.5 us (28%)
  other arithmetic  1.63 us (1%)
  local copies, waits for them, and re-layouts  1.28 us (1%)
    ppermute x23, starting transfers between devices, send(): return lax.ppermute(array, ('seq', 'mem'), pairs)  34.1 us
    ppermute x23, waiting for transfers between devices, send(): return lax.ppermute(array, ('seq', 'mem'), pairs)  31.5 us
    pallas_call x2, Pallas kernels, memory_attention(): pl.pallas_call(functools.partial(memory_kernel, group), grid_spec=pltpu.P...  11.3 us
    pallas_call x2, Pallas kernels, local_attention(): pl.pallas_call(kernel, grid_spec=pltpu.PrefetchScalarGridSpec(num_scalar_...  10.6 us
    pallas_call x1, Pallas kernels, project_keyvalue(): pl.pallas_call(keyvalue_kernel, grid_spec=pltpu.PrefetchScalarGridSpec(nu...  6.44 us
    pallas_call x1, Pallas kernels, project_query(): pl.pallas_call(query_kernel, grid_spec=pltpu.PrefetchScalarGridSpec(num_s...  4.78 us
    pallas_call x1, Pallas kernels, project_output(): pl.pallas_call(output_kernel, grid_spec=pltpu.PrefetchScalarGridSpec(num_...  3.57 us
    pallas_call x1, Pallas kernels, take_part(): pl.pallas_call(part_kernel, grid_spec=pltpu.PrefetchScalarGridSpec(num_sc...  2.64 us
  transfers between devices with their start and end apart: 23, of which 9 were waited for; matrix products, arithmetic and copies ran while one was open for 1% of the time, Pallas kernels for 34%

profile of v2, /device:TPU:1, one launch (start us, length us, event | category | flops | bytes accessed | tf_op | source)
XLA Modules:
  0.0 112.0 jit_solution(14923727255004463032)
XLA Ops:
  0.0 1.4 %collective-permute-start = (bf16[256,2048]{1,0:T(8,128)(2,1)}, bf16[256,2048]{1,0:T(8,128)(2,1)S(1)}, u32[]{:S(2)}, u32[]{:S(2)}) collective-permute-start(bf16[256,2048]{1,0:T(8,128)(2,1)} %bitcast.30), channel_id=1, source_target_pairs={{0,16},{16,0},{32,48},{48,32},{64,80},{80,64},{96,112},{112,96},{1... | collective-permute-start | bytes 3145736 | tf_op jit(solution)/shard_map/ppermute | solution.py:42
  2.0 2.6 %shard_map.84 = bf16[1,2,2,2,2,128,128]{6,5,4,3,2,1,0:T(8,128)(2,1)} custom-call(s32[4]{0:T(128)} %pad_add_fusion.info, bf16[8,2,128,1024]{3,2,1,0:T(8,128)(2,1)} %mem.1), custom_call_target="tpu_custom_call" | custom-call | bytes 1048576 | tf_op jit(solution)/shard_map/pallas_call | solution.py:258
  4.7 1.8 %collective-permute-start.5 = (bf16[1,2,2,2,2,128,128]{6,5,4,3,2,1,0:T(8,128)(2,1)}, bf16[1,2,2,2,2,128,128]{6,5,4,3,2,1,0:T(8,128)(2,1)S(1)}, u32[]{:S(2)}, u32[]{:S(2)}) collective-permute-start(bf16[1,2,2,2,2,128,128]{6,5,4,3,2,1,0:T(8,128)(2,1)} %shard_map.84), channel_id=1, source_target_pairs={{0,4},{16,17},{32,36},{48,49},{64,68},{80,81},{96,100},{112,113},{... | collective-permute-start | bytes 1572872 | tf_op jit(solution)/shard_map/ppermute | solution.py:42
  6.5 2.2 %collective-permute-start.6 = (bf16[1,2,2,2,2,128,128]{6,5,4,3,2,1,0:T(8,128)(2,1)}, bf16[1,2,2,2,2,128,128]{6,5,4,3,2,1,0:T(8,128)(2,1)S(1)}, u32[]{:S(2)}, u32[]{:S(2)}) collective-permute-start(bf16[1,2,2,2,2,128,128]{6,5,4,3,2,1,0:T(8,128)(2,1)} %shard_map.84), channel_id=1, source_target_pairs={{0,12},{16,19},{32,44},{48,51},{64,76},{80,83},{96,108},{112,115},... | collective-permute-start | bytes 1572872 | tf_op jit(solution)/shard_map/ppermute | solution.py:42
  8.7 1.2 %collective-permute-start.7 = (bf16[1,2,2,2,2,128,128]{6,5,4,3,2,1,0:T(8,128)(2,1)}, bf16[1,2,2,2,2,128,128]{6,5,4,3,2,1,0:T(8,128)(2,1)S(1)}, u32[]{:S(2)}, u32[]{:S(2)}) collective-permute-start(bf16[1,2,2,2,2,128,128]{6,5,4,3,2,1,0:T(8,128)(2,1)} %shard_map.84), channel_id=1, source_target_pairs={{0,8},{16,18},{32,40},{48,50},{64,72},{80,82},{96,104},{112,114},{... | collective-permute-start | bytes 1572872 | tf_op jit(solution)/shard_map/ppermute | solution.py:42
  10.0 1.1 collective-permute-done.1
  11.8 1.0 copy-done.6
  12.8 4.8 %shard_map.82.refs_0_.q = bf16[528,512]{1,0:T(8,128)(2,1)} custom-call(s32[4]{0:T(128)} %pad_add_fusion.info, bf16[256,2048]{1,0:T(8,128)(2,1)} %bitcast.31, bf16[256,2048]{1,0:T(8,128)(2,1)} %copy-done.6, bf16[2048,1024]{1,0:T(8,128)(2,1)} %w.1, bf16[16,512]{1,0:T(8,128)(2,1)} %fusion.5.ids), custom_call_target="tpu_custom_call" | custom-call | flops 1073741824 | bytes 4194304 | tf_op jit(solution)/shard_map/pallas_call | solution.py:104
  17.5 6.4 %shard_map.85 = (bf16[512,512]{1,0:T(8,128)(2,1)}, bf16[512,512]{1,0:T(8,128)(2,1)}) custom-call(s32[4]{0:T(128)} %pad_add_fusion.info, bf16[256,2048]{1,0:T(8,128)(2,1)} %bitcast.32, bf16[256,2048]{1,0:T(8,128)(2,1)} %copy-done.6, bf16[2048,1024]{1,0:T(8,128)(2,1)} %wk.1, bf16[2048,1024]{1,0:T(8,128)(2,1)} %wv.1), custom_call_target="tpu_custom_call" | custom-call | flops 2147483648 | bytes 6291456 | tf_op jit(solution)/shard_map/pallas_call | solution.py:136
  24.4 2.5 %collective-permute-start.15 = (bf16[4,2,2,2,128,128]{5,4,3,2,1,0:T(8,128)(2,1)S(1)}, bf16[4,2,2,2,128,128]{5,4,3,2,1,0:T(8,128)(2,1)S(1)}, u32[]{:S(2)}, u32[]{:S(2)}) collective-permute-start(bf16[4,2,2,2,128,128]{5,4,3,2,1,0:T(8,128)(2,1)S(1)} %pad_maximum_fusion.1.refs_4_), channel_id=1, source_target_pairs={{0,3},{16,28},{32,35},{48,60},{64,67},{80,92},{96,99},{112,124},{1... | collective-permute-start | bytes 3145736 | tf_op jit(solution)/shard_map/ppermute | solution.py:42
  27.2 2.8 %collective-permute-start.2 = (bf16[528,512]{1,0:T(8,128)(2,1)S(1)}, bf16[528,512]{1,0:T(8,128)(2,1)S(1)}, u32[]{:S(2)}, u32[]{:S(2)}) collective-permute-start(bf16[528,512]{1,0:T(8,128)(2,1)S(1)} %copy-done.1), channel_id=1, source_target_pairs={{0,32},{16,112},{32,64},{48,16},{64,96},{80,48},{96,0},{112,80},{1... | collective-permute-start | bytes 1622024 | tf_op jit(solution)/shard_map/ppermute | solution.py:42
  30.1 9.7 %collective-permute-done.2.refs_1_.q1 = bf16[528,512]{1,0:T(8,128)(2,1)S(1)} collective-permute-done((bf16[528,512]{1,0:T(8,128)(2,1)S(1)}, bf16[528,512]{1,0:T(8,128)(2,1)S(1)}, u32[]{:S(2)}, u32[]{:S(2)}) %collective-permute-start.2) | collective-permute-done | bytes 540704 | tf_op jit(solution)/shard_map/ppermute | solution.py:42
  39.8 3.4 %collective-permute-start.4 = (bf16[528,512]{1,0:T(8,128)(2,1)S(1)}, bf16[528,512]{1,0:T(8,128)(2,1)S(1)}, u32[]{:S(2)}, u32[]{:S(2)}) collective-permute-start(bf16[528,512]{1,0:T(8,128)(2,1)S(1)} %collective-permute-done.2.refs_1_.q1), channel_id=1, source_target_pairs={{0,32},{16,112},{32,64},{48,16},{64,96},{80,48},{96,0},{112,80},{1... | collective-permute-start | bytes 1622024 | tf_op jit(solution)/shard_map/ppermute | solution.py:42
  43.2 4.4 %collective-permute-start.16 = (bf16[4,2,2,2,128,128]{5,4,3,2,1,0:T(8,128)(2,1)S(1)}, bf16[4,2,2,2,128,128]{5,4,3,2,1,0:T(8,128)(2,1)S(1)}, u32[]{:S(2)}, u32[]{:S(2)}) collective-permute-start(bf16[4,2,2,2,128,128]{5,4,3,2,1,0:T(8,128)(2,1)S(1)} %collective-permute-done.15.refs_6_), channel_id=1, source_target_pairs={{0,3},{16,28},{32,35},{48,60},{64,67},{80,92},{96,99},{112,124},{1... | collective-permute-start | bytes 3145736 | tf_op jit(solution)/shard_map/ppermute | solution.py:42
  47.7 1.4 %collective-permute-start.10 = (bf16[4,2,2,2,128,128]{5,4,3,2,1,0:T(8,128)(2,1)S(1)}, bf16[4,2,2,2,128,128]{5,4,3,2,1,0:T(8,128)(2,1)S(1)}, u32[]{:S(2)}, u32[]{:S(2)}) collective-permute-start(bf16[4,2,2,2,128,128]{5,4,3,2,1,0:T(8,128)(2,1)S(1)} %collective-permute-done.8.refs_5_), channel_id=1, source_target_pairs={{0,1},{16,20},{32,33},{48,52},{64,65},{80,84},{96,97},{112,116},{1... | collective-permute-start | bytes 3145736 | tf_op jit(solution)/shard_map/ppermute | solution.py:42
  49.5 6.9 %shard_map.89 = (bf16[528,512]{1,0:T(8,128)(2,1)S(1)}, bf16[528,512]{1,0:T(8,128)(2,1)S(1)}) custom-call(s32[4]{0:T(128)S(1)} %copy-done.4, bf16[528,512]{1,0:T(8,128)(2,1)S(1)} %collective-permute-done.2.refs_1_.q1, bf16[528,512]{1,0:T(8,128)(2,1)S(1)} %collective-permute-done.3.refs_2_.q2, bf16[528,512]{1,0:T(8,128)(2,1)S(1)} %collective-permute-done.4.refs_3_.q3, ...), custom_call_target="tpu_custom_call" | custom-call | flops 1073741824 | bytes 2097152 | tf_op jit(solution)/shard_map/pallas_call | solution.py:229
  56.4 1.3 %collective-permute-start.20 = (bf16[528,512]{1,0:T(8,128)(2,1)S(1)}, bf16[528,512]{1,0:T(8,128)(2,1)S(1)}, u32[]{:S(2)}, u32[]{:S(2)}) collective-permute-start(bf16[528,512]{1,0:T(8,128)(2,1)S(1)} %get-tuple-element.53), channel_id=1, source_target_pairs={{0,32},{16,48},{32,64},{48,80},{64,96},{80,112},{1,33},{17,49},{33... | collective-permute-start | bytes 1622024 | tf_op jit(solution)/shard_map/ppermute | solution.py:42
  57.8 1.5 %collective-permute-start.21 = (bf16[528,512]{1,0:T(8,128)(2,1)S(1)}, bf16[528,512]{1,0:T(8,128)(2,1)S(1)}, u32[]{:S(2)}, u32[]{:S(2)}) collective-permute-start(bf16[528,512]{1,0:T(8,128)(2,1)S(1)} %get-tuple-element.54), channel_id=1, source_target_pairs={{0,64},{16,80},{32,96},{48,112},{1,65},{17,81},{33,97},{49,113},{2... | collective-permute-start | bytes 1622024 | tf_op jit(solution)/shard_map/ppermute | solution.py:42
  59.4 2.4 %shard_map.83 = (s32[144]{0:T(256)S(1)}, s32[80]{0:T(128)S(1)}) custom-call(s32[4]{0:T(128)S(1)} %copy-done.4, s32[128]{0:T(128)S(1)} %maximum_convert_fusion.ids), custom_call_target="tpu_custom_call" | custom-call | flops 1000 | bytes 1000 | tf_op jit(solution)/shard_map/pallas_call | solution.py:305
  61.8 5.7 %shard_map.87 = (bf16[272,512]{1,0:T(8,128)(2,1)S(1)}, bf16[272,512]{1,0:T(8,128)(2,1)S(1)}, bf16[272,512]{1,0:T(8,128)(2,1)S(1)}, bf16[272,512]{1,0:T(8,128)(2,1)S(1)}) custom-call(s32[144]{0:T(256)S(1)} %get-tuple-element.37.slots, s32[80]{0:T(128)S(1)} %get-tuple-element.38.blocks, bf16[528,512]{1,0:T(8,128)(2,1)S(1)} %copy-done.1, ...), custom_call_target="tpu_custom_call" | custom-call | flops 536870912 | bytes 6291456 | tf_op jit(solution)/shard_map/pallas_call | solution.py:394
  67.5 3.1 %collective-permute-done.9.refs_6_ = bf16[4,2,2,2,128,128]{5,4,3,2,1,0:T(8,128)(2,1)S(1)} collective-permute-done((bf16[4,2,2,2,128,128]{5,4,3,2,1,0:T(8,128)(2,1)S(1)}, bf16[4,2,2,2,128,128]{5,4,3,2,1,0:T(8,128)(2,1)S(1)}, u32[]{:S(2)}, u32[]{:S(2)}) %collective-permute-start.9) | collective-permute-done | bytes 1048608 | tf_op jit(solution)/shard_map/ppermute | solution.py:42
  70.7 5.7 %shard_map.86 = (bf16[272,512]{1,0:T(8,128)(2,1)S(1)}, bf16[272,512]{1,0:T(8,128)(2,1)S(1)}, bf16[272,512]{1,0:T(8,128)(2,1)S(1)}, bf16[272,512]{1,0:T(8,128)(2,1)S(1)}) custom-call(s32[144]{0:T(256)S(1)} %get-tuple-element.37.slots, s32[80]{0:T(128)S(1)} %get-tuple-element.38.blocks, bf16[528,512]{1,0:T(8,128)(2,1)S(1)} %copy-done.1, ...), custom_call_target="tpu_custom_call" | custom-call | flops 536870912 | bytes 6291456 | tf_op jit(solution)/shard_map/pallas_call | solution.py:394
  77.2 2.5 %collective-permute-start.12 = (bf16[272,512]{1,0:T(8,128)(2,1)S(1)}, bf16[272,512]{1,0:T(8,128)(2,1)S(1)}, u32[]{:S(2)}, u32[]{:S(2)}) collective-permute-start(bf16[272,512]{1,0:T(8,128)(2,1)S(1)} %get-tuple-element.46), channel_id=1, source_target_pairs={{0,32},{16,112},{32,64},{48,16},{64,96},{80,48},{96,0},{112,80},{1... | collective-permute-start | bytes 835592 | tf_op jit(solution)/shard_map/ppermute | solution.py:42
  79.7 1.9 %collective-permute-done.17.refs_5_ = bf16[272,512]{1,0:T(8,128)(2,1)S(1)} collective-permute-done((bf16[272,512]{1,0:T(8,128)(2,1)S(1)}, bf16[272,512]{1,0:T(8,128)(2,1)S(1)}, u32[]{:S(2)}, u32[]{:S(2)}) %collective-permute-start.17) | collective-permute-done | bytes 278560 | tf_op jit(solution)/shard_map/ppermute | solution.py:42
  81.7 3.6 %shard_map.88.refs_8_ = bf16[528,512]{1,0:T(8,128)(2,1)S(1)} custom-call(s32[4]{0:T(128)S(1)} %copy-done.4, bf16[528,512]{1,0:T(8,128)(2,1)S(1)} %copy-done.1, bf16[512,512]{1,0:T(8,128)(2,1)S(1)} %copy-done.2, bf16[512,512]{1,0:T(8,128)(2,1)S(1)} %copy-done.3), custom_call_target="tpu_custom_call" | custom-call | flops 536870912 | bytes 2097152 | tf_op jit(solution)/shard_map/pallas_call | solution.py:229
  85.3 2.2 %collective-permute-done.19.refs_7_ = bf16[272,512]{1,0:T(8,128)(2,1)S(1)} collective-permute-done((bf16[272,512]{1,0:T(8,128)(2,1)S(1)}, bf16[272,512]{1,0:T(8,128)(2,1)S(1)}, u32[]{:S(2)}, u32[]{:S(2)}) %collective-permute-start.19) | collective-permute-done | bytes 278560 | tf_op jit(solution)/shard_map/ppermute | solution.py:42
  87.5 6.0 %collective-permute-done.11.refs_1_ = bf16[272,512]{1,0:T(8,128)(2,1)S(1)} collective-permute-done((bf16[272,512]{1,0:T(8,128)(2,1)S(1)}, bf16[272,512]{1,0:T(8,128)(2,1)S(1)}, u32[]{:S(2)}, u32[]{:S(2)}) %collective-permute-start.11) | collective-permute-done | bytes 278560 | tf_op jit(solution)/shard_map/ppermute | solution.py:42
  93.5 6.0 %collective-permute-done.13.refs_3_ = bf16[272,512]{1,0:T(8,128)(2,1)S(1)} collective-permute-done((bf16[272,512]{1,0:T(8,128)(2,1)S(1)}, bf16[272,512]{1,0:T(8,128)(2,1)S(1)}, u32[]{:S(2)}, u32[]{:S(2)}) %collective-permute-start.13) | collective-permute-done | bytes 278560 | tf_op jit(solution)/shard_map/ppermute | solution.py:42
  99.5 1.5 %shard_map.90 = (bf16[256,512]{1,0:T(8,128)(2,1)S(1)}, bf16[256,512]{1,0:T(8,128)(2,1)S(1)}) custom-call(s32[4]{0:T(128)S(1)} %copy-done.4, f32[8]{0:T(128)S(1)} %copy-done.5, bf16[272,512]{1,0:T(8,128)(2,1)S(1)} %get-tuple-element.44.refs_0_, bf16[272,512]{1,0:T(8,128)(2,1)S(1)} %collective-permute-done.11.refs_1_, ...), custom_call_target="tpu_custom_call" | custom-call | flops 5406720 | bytes 4325376 | tf_op jit(solution)/shard_map/pallas_call | solution.py:452
  101.1 6.3 %collective-permute-start.22 = (bf16[256,512]{1,0:T(8,128)(2,1)S(1)}, bf16[256,512]{1,0:T(8,128)(2,1)S(1)}, u32[]{:S(2)}, u32[]{:S(2)}) collective-permute-start(bf16[256,512]{1,0:T(8,128)(2,1)S(1)} %get-tuple-element.56), channel_id=1, source_target_pairs={{0,16},{16,0},{32,48},{48,32},{64,80},{80,64},{96,112},{112,96},{1... | collective-permute-start | bytes 786440 | tf_op jit(solution)/shard_map/ppermute | solution.py:42
  107.3 1.2 %collective-permute-done.22.oth = bf16[256,512]{1,0:T(8,128)(2,1)S(1)} collective-permute-done((bf16[256,512]{1,0:T(8,128)(2,1)S(1)}, bf16[256,512]{1,0:T(8,128)(2,1)S(1)}, u32[]{:S(2)}, u32[]{:S(2)}) %collective-permute-start.22) | collective-permute-done | bytes 262176 | tf_op jit(solution)/shard_map/ppermute | solution.py:42
  108.5 3.6 %shard_map.91 = bf16[256,2048]{1,0:T(8,128)(2,1)} custom-call(s32[4]{0:T(128)S(1)} %copy-done.4, bf16[256,512]{1,0:T(8,128)(2,1)S(1)} %get-tuple-element.55.own, bf16[256,512]{1,0:T(8,128)(2,1)S(1)} %collective-permute-done.22.oth, bf16[1024,2048]{1,0:T(8,128)(2,1)S(1)} %copy-done, bf16[1024,2048]{1,0:T(8,128)(2,1)S(1)} %copy-done), custom_call_target="tpu_custom_call" | custom-call | flops 1073741824 | bytes 4194304 | tf_op jit(solution)/shard_map/pallas_call | solution.py:475
  (56 shorter events, 3.7 us)
Async XLA Ops:
  0.0 9.9 %copy-start.8 = (s32[1,2,8]{2,1,0:T(2,128)S(1)}, s32[1,2,8]{2,1,0:T(2,128)}, u32[]{:S(2)}) copy-start(s32[1,2,8]{2,1,0:T(2,128)} %param.11) | copy-start | bytes 196
  0.0 11.8 %collective-permute-start = (bf16[256,2048]{1,0:T(8,128)(2,1)}, bf16[256,2048]{1,0:T(8,128)(2,1)S(1)}, u32[]{:S(2)}, u32[]{:S(2)}) collective-permute-start(bf16[256,2048]{1,0:T(8,128)(2,1)} %bitcast.30), channel_id=1, source_target_pairs={{0,16},{16,0},{32,48},{48,32},{64,80},{80,64},{96,112},{112,96},{1... | collective-permute-start | bytes 3145736 | tf_op jit(solution)/shard_map/ppermute | solution.py:42
  4.7 19.3 %collective-permute-start.5 = (bf16[1,2,2,2,2,128,128]{6,5,4,3,2,1,0:T(8,128)(2,1)}, bf16[1,2,2,2,2,128,128]{6,5,4,3,2,1,0:T(8,128)(2,1)S(1)}, u32[]{:S(2)}, u32[]{:S(2)}) collective-permute-start(bf16[1,2,2,2,2,128,128]{6,5,4,3,2,1,0:T(8,128)(2,1)} %shard_map.84), channel_id=1, source_target_pairs={{0,4},{16,17},{32,36},{48,49},{64,68},{80,81},{96,100},{112,113},{... | collective-permute-start | bytes 1572872 | tf_op jit(solution)/shard_map/ppermute | solution.py:42
  6.5 17.5 %collective-permute-start.6 = (bf16[1,2,2,2,2,128,128]{6,5,4,3,2,1,0:T(8,128)(2,1)}, bf16[1,2,2,2,2,128,128]{6,5,4,3,2,1,0:T(8,128)(2,1)S(1)}, u32[]{:S(2)}, u32[]{:S(2)}) collective-permute-start(bf16[1,2,2,2,2,128,128]{6,5,4,3,2,1,0:T(8,128)(2,1)} %shard_map.84), channel_id=1, source_target_pairs={{0,12},{16,19},{32,44},{48,51},{64,76},{80,83},{96,108},{112,115},... | collective-permute-start | bytes 1572872 | tf_op jit(solution)/shard_map/ppermute | solution.py:42
  8.7 15.3 %collective-permute-start.7 = (bf16[1,2,2,2,2,128,128]{6,5,4,3,2,1,0:T(8,128)(2,1)}, bf16[1,2,2,2,2,128,128]{6,5,4,3,2,1,0:T(8,128)(2,1)S(1)}, u32[]{:S(2)}, u32[]{:S(2)}) collective-permute-start(bf16[1,2,2,2,2,128,128]{6,5,4,3,2,1,0:T(8,128)(2,1)} %shard_map.84), channel_id=1, source_target_pairs={{0,8},{16,18},{32,40},{48,50},{64,72},{80,82},{96,104},{112,114},{... | collective-permute-start | bytes 1572872 | tf_op jit(solution)/shard_map/ppermute | solution.py:42
  10.0 1.1 %collective-permute-start.1 = (s32[1,16]{1,0:T(1,128)S(1)}, s32[1,16]{1,0:T(1,128)S(1)}, u32[]{:S(2)}, u32[]{:S(2)}) collective-permute-start(s32[1,16]{1,0:T(1,128)S(1)} %concatenate.25), channel_id=1, source_target_pairs={{0,16},{16,0},{32,48},{48,32},{64,80},{80,64},{96,112},{112,96},{1... | collective-permute-start | bytes 200 | tf_op jit(solution)/shard_map/ppermute | solution.py:42
  11.8 1.0 copy-start.6
  17.5 6.5 %copy-start.7 = (bf16[1,2,2,2,2,128,128]{6,5,4,3,2,1,0:T(8,128)(2,1)S(1)}, bf16[1,2,2,2,2,128,128]{6,5,4,3,2,1,0:T(8,128)(2,1)}, u32[]{:S(2)}) copy-start(bf16[1,2,2,2,2,128,128]{6,5,4,3,2,1,0:T(8,128)(2,1)} %shard_map.84) | copy-start | bytes 1572868
  24.0 3.2 %copy-start.1 = (bf16[528,512]{1,0:T(8,128)(2,1)S(1)}, bf16[528,512]{1,0:T(8,128)(2,1)}, u32[]{:S(2)}) copy-start(bf16[528,512]{1,0:T(8,128)(2,1)} %shard_map.82.refs_0_.q) | copy-start | bytes 1622020
  24.0 25.5 %copy-start.2 = (bf16[512,512]{1,0:T(8,128)(2,1)S(1)}, bf16[512,512]{1,0:T(8,128)(2,1)}, u32[]{:S(2)}) copy-start(bf16[512,512]{1,0:T(8,128)(2,1)} %get-tuple-element.39.k) | copy-start | bytes 1572868
  24.0 25.5 %copy-start.3 = (bf16[512,512]{1,0:T(8,128)(2,1)S(1)}, bf16[512,512]{1,0:T(8,128)(2,1)}, u32[]{:S(2)}) copy-start(bf16[512,512]{1,0:T(8,128)(2,1)} %get-tuple-element.52.v) | copy-start | bytes 1572868
  24.0 25.4 %copy-start.4 = (s32[4]{0:T(128)S(1)}, s32[4]{0:T(128)}, u32[]{:S(2)}) copy-start(s32[4]{0:T(128)} %pad_add_fusion.info) | copy-start | bytes 52
  24.4 18.8 %collective-permute-start.15 = (bf16[4,2,2,2,128,128]{5,4,3,2,1,0:T(8,128)(2,1)S(1)}, bf16[4,2,2,2,128,128]{5,4,3,2,1,0:T(8,128)(2,1)S(1)}, u32[]{:S(2)}, u32[]{:S(2)}) collective-permute-start(bf16[4,2,2,2,128,128]{5,4,3,2,1,0:T(8,128)(2,1)S(1)} %pad_maximum_fusion.1.refs_4_), channel_id=1, source_target_pairs={{0,3},{16,28},{32,35},{48,60},{64,67},{80,92},{96,99},{112,124},{1... | collective-permute-start | bytes 3145736 | tf_op jit(solution)/shard_map/ppermute | solution.py:42
  27.1 20.6 %collective-permute-start.8 = (bf16[4,2,2,2,128,128]{5,4,3,2,1,0:T(8,128)(2,1)S(1)}, bf16[4,2,2,2,128,128]{5,4,3,2,1,0:T(8,128)(2,1)S(1)}, u32[]{:S(2)}, u32[]{:S(2)}) collective-permute-start(bf16[4,2,2,2,128,128]{5,4,3,2,1,0:T(8,128)(2,1)S(1)} %pad_maximum_fusion.refs_4_), channel_id=1, source_target_pairs={{0,1},{16,20},{32,33},{48,52},{64,65},{80,84},{96,97},{112,116},{1... | collective-permute-start | bytes 3145736 | tf_op jit(solution)/shard_map/ppermute | solution.py:42
  27.2 12.6 %collective-permute-start.2 = (bf16[528,512]{1,0:T(8,128)(2,1)S(1)}, bf16[528,512]{1,0:T(8,128)(2,1)S(1)}, u32[]{:S(2)}, u32[]{:S(2)}) collective-permute-start(bf16[528,512]{1,0:T(8,128)(2,1)S(1)} %copy-done.1), channel_id=1, source_target_pairs={{0,32},{16,112},{32,64},{48,16},{64,96},{80,48},{96,0},{112,80},{1... | collective-permute-start | bytes 1622024 | tf_op jit(solution)/shard_map/ppermute | solution.py:42
  30.0 17.7 %collective-permute-start.3 = (bf16[528,512]{1,0:T(8,128)(2,1)S(1)}, bf16[528,512]{1,0:T(8,128)(2,1)S(1)}, u32[]{:S(2)}, u32[]{:S(2)}) collective-permute-start(bf16[528,512]{1,0:T(8,128)(2,1)S(1)} %copy-done.1), channel_id=1, source_target_pairs={{0,96},{16,48},{32,0},{48,80},{64,32},{80,112},{96,64},{112,16},{1... | collective-permute-start | bytes 1622024 | tf_op jit(solution)/shard_map/ppermute | solution.py:42
  30.0 27.8 %collective-permute-start.14 = (bf16[4,2,2,2,128,128]{5,4,3,2,1,0:T(8,128)(2,1)S(1)}, bf16[4,2,2,2,128,128]{5,4,3,2,1,0:T(8,128)(2,1)S(1)}, u32[]{:S(2)}, u32[]{:S(2)}) collective-permute-start(bf16[4,2,2,2,128,128]{5,4,3,2,1,0:T(8,128)(2,1)S(1)} %pad_maximum_fusion.1.refs_4_), channel_id=1, source_target_pairs={{0,1},{16,20},{32,33},{48,52},{64,65},{80,84},{96,97},{112,116},{1... | collective-permute-start | bytes 3145736 | tf_op jit(solution)/shard_map/ppermute | solution.py:42
  39.8 9.7 %collective-permute-start.4 = (bf16[528,512]{1,0:T(8,128)(2,1)S(1)}, bf16[528,512]{1,0:T(8,128)(2,1)S(1)}, u32[]{:S(2)}, u32[]{:S(2)}) collective-permute-start(bf16[528,512]{1,0:T(8,128)(2,1)S(1)} %collective-permute-done.2.refs_1_.q1), channel_id=1, source_target_pairs={{0,32},{16,112},{32,64},{48,16},{64,96},{80,48},{96,0},{112,80},{1... | collective-permute-start | bytes 1622024 | tf_op jit(solution)/shard_map/ppermute | solution.py:42
  43.2 18.6 %collective-permute-start.16 = (bf16[4,2,2,2,128,128]{5,4,3,2,1,0:T(8,128)(2,1)S(1)}, bf16[4,2,2,2,128,128]{5,4,3,2,1,0:T(8,128)(2,1)S(1)}, u32[]{:S(2)}, u32[]{:S(2)}) collective-permute-start(bf16[4,2,2,2,128,128]{5,4,3,2,1,0:T(8,128)(2,1)S(1)} %collective-permute-done.15.refs_6_), channel_id=1, source_target_pairs={{0,3},{16,28},{32,35},{48,60},{64,67},{80,92},{96,99},{112,124},{1... | collective-permute-start | bytes 3145736 | tf_op jit(solution)/shard_map/ppermute | solution.py:42
  47.6 23.0 %collective-permute-start.9 = (bf16[4,2,2,2,128,128]{5,4,3,2,1,0:T(8,128)(2,1)S(1)}, bf16[4,2,2,2,128,128]{5,4,3,2,1,0:T(8,128)(2,1)S(1)}, u32[]{:S(2)}, u32[]{:S(2)}) collective-permute-start(bf16[4,2,2,2,128,128]{5,4,3,2,1,0:T(8,128)(2,1)S(1)} %pad_maximum_fusion.refs_4_), channel_id=1, source_target_pairs={{0,3},{16,28},{32,35},{48,60},{64,67},{80,92},{96,99},{112,124},{1... | collective-permute-start | bytes 3145736 | tf_op jit(solution)/shard_map/ppermute | solution.py:42
  47.7 22.9 %collective-permute-start.10 = (bf16[4,2,2,2,128,128]{5,4,3,2,1,0:T(8,128)(2,1)S(1)}, bf16[4,2,2,2,128,128]{5,4,3,2,1,0:T(8,128)(2,1)S(1)}, u32[]{:S(2)}, u32[]{:S(2)}) collective-permute-start(bf16[4,2,2,2,128,128]{5,4,3,2,1,0:T(8,128)(2,1)S(1)} %collective-permute-done.8.refs_5_), channel_id=1, source_target_pairs={{0,1},{16,20},{32,33},{48,52},{64,65},{80,84},{96,97},{112,116},{1... | collective-permute-start | bytes 3145736 | tf_op jit(solution)/shard_map/ppermute | solution.py:42
  56.4 20.0 %collective-permute-start.20 = (bf16[528,512]{1,0:T(8,128)(2,1)S(1)}, bf16[528,512]{1,0:T(8,128)(2,1)S(1)}, u32[]{:S(2)}, u32[]{:S(2)}) collective-permute-start(bf16[528,512]{1,0:T(8,128)(2,1)S(1)} %get-tuple-element.53), channel_id=1, source_target_pairs={{0,32},{16,48},{32,64},{48,80},{64,96},{80,112},{1,33},{17,49},{33... | collective-permute-start | bytes 1622024 | tf_op jit(solution)/shard_map/ppermute | solution.py:42
  57.8 19.4 %collective-permute-start.21 = (bf16[528,512]{1,0:T(8,128)(2,1)S(1)}, bf16[528,512]{1,0:T(8,128)(2,1)S(1)}, u32[]{:S(2)}, u32[]{:S(2)}) collective-permute-start(bf16[528,512]{1,0:T(8,128)(2,1)S(1)} %get-tuple-element.54), channel_id=1, source_target_pairs={{0,64},{16,80},{32,96},{48,112},{1,65},{17,81},{33,97},{49,113},{2... | collective-permute-start | bytes 1622024 | tf_op jit(solution)/shard_map/ppermute | solution.py:42
  67.5 14.1 %collective-permute-start.17 = (bf16[272,512]{1,0:T(8,128)(2,1)S(1)}, bf16[272,512]{1,0:T(8,128)(2,1)S(1)}, u32[]{:S(2)}, u32[]{:S(2)}) collective-permute-start(bf16[272,512]{1,0:T(8,128)(2,1)S(1)} %get-tuple-element.49), channel_id=1, source_target_pairs={{0,96},{16,48},{32,0},{48,80},{64,32},{80,112},{96,64},{112,16},{1... | collective-permute-start | bytes 835592 | tf_op jit(solution)/shard_map/ppermute | solution.py:42
  70.6 14.7 %collective-permute-start.18 = (bf16[272,512]{1,0:T(8,128)(2,1)S(1)}, bf16[272,512]{1,0:T(8,128)(2,1)S(1)}, u32[]{:S(2)}, u32[]{:S(2)}) collective-permute-start(bf16[272,512]{1,0:T(8,128)(2,1)S(1)} %get-tuple-element.50), channel_id=1, source_target_pairs={{0,32},{16,112},{32,64},{48,16},{64,96},{80,48},{96,0},{112,80},{1... | collective-permute-start | bytes 835592 | tf_op jit(solution)/shard_map/ppermute | solution.py:42
  70.6 28.9 %copy-start.5 = (f32[8]{0:T(128)S(1)}, f32[8]{0:T(128)}, u32[]{:S(2)}) copy-start(f32[8]{0:T(128)} %gate.1) | copy-start | bytes 100
  70.6 16.9 %collective-permute-start.19 = (bf16[272,512]{1,0:T(8,128)(2,1)S(1)}, bf16[272,512]{1,0:T(8,128)(2,1)S(1)}, u32[]{:S(2)}, u32[]{:S(2)}) collective-permute-start(bf16[272,512]{1,0:T(8,128)(2,1)S(1)} %get-tuple-element.51), channel_id=1, source_target_pairs={{0,64},{16,80},{32,96},{48,112},{64,0},{80,16},{96,32},{112,48},{1... | collective-permute-start | bytes 835592 | tf_op jit(solution)/shard_map/ppermute | solution.py:42
  76.4 32.1 %copy-start = (bf16[1024,2048]{1,0:T(8,128)(2,1)S(1)}, bf16[1024,2048]{1,0:T(8,128)(2,1)}, u32[]{:S(2)}) copy-start(bf16[1024,2048]{1,0:T(8,128)(2,1)} %w_oth.1) | copy-start | bytes 12582916
  76.4 17.1 %collective-permute-start.11 = (bf16[272,512]{1,0:T(8,128)(2,1)S(1)}, bf16[272,512]{1,0:T(8,128)(2,1)S(1)}, u32[]{:S(2)}, u32[]{:S(2)}) collective-permute-start(bf16[272,512]{1,0:T(8,128)(2,1)S(1)} %get-tuple-element.45), channel_id=1, source_target_pairs={{0,96},{16,48},{32,0},{48,80},{64,32},{80,112},{96,64},{112,16},{1... | collective-permute-start | bytes 835592 | tf_op jit(solution)/shard_map/ppermute | solution.py:42
  77.2 16.3 %collective-permute-start.12 = (bf16[272,512]{1,0:T(8,128)(2,1)S(1)}, bf16[272,512]{1,0:T(8,128)(2,1)S(1)}, u32[]{:S(2)}, u32[]{:S(2)}) collective-permute-start(bf16[272,512]{1,0:T(8,128)(2,1)S(1)} %get-tuple-element.46), channel_id=1, source_target_pairs={{0,32},{16,112},{32,64},{48,16},{64,96},{80,48},{96,0},{112,80},{1... | collective-permute-start | bytes 835592 | tf_op jit(solution)/shard_map/ppermute | solution.py:42
  81.6 17.9 %collective-permute-start.13 = (bf16[272,512]{1,0:T(8,128)(2,1)S(1)}, bf16[272,512]{1,0:T(8,128)(2,1)S(1)}, u32[]{:S(2)}, u32[]{:S(2)}) collective-permute-start(bf16[272,512]{1,0:T(8,128)(2,1)S(1)} %get-tuple-element.47), channel_id=1, source_target_pairs={{0,64},{16,80},{32,96},{48,112},{64,0},{80,16},{96,32},{112,48},{1... | collective-permute-start | bytes 835592 | tf_op jit(solution)/shard_map/ppermute | solution.py:42
  101.1 7.4 %collective-permute-start.22 = (bf16[256,512]{1,0:T(8,128)(2,1)S(1)}, bf16[256,512]{1,0:T(8,128)(2,1)S(1)}, u32[]{:S(2)}, u32[]{:S(2)}) collective-permute-start(bf16[256,512]{1,0:T(8,128)(2,1)S(1)} %get-tuple-element.56), channel_id=1, source_target_pairs={{0,16},{16,0},{32,48},{48,32},{64,80},{80,64},{96,112},{112,96},{1... | collective-permute-start | bytes 786440 | tf_op jit(solution)/shard_map/ppermute | solution.py:42

commit v3 on v2

--- a/solution.py
+++ b/solution.py
@@ -74,10 +74,6 @@
     return pltpu.CompilerParams(vmem_limit_bytes=limit)
 
 
-def after(value, *earlier):
-    return lax.optimization_barrier((value, earlier))[0]
-
-
 def cost(flops, nbytes, trans=0):
     return pl.CostEstimate(flops=flops, bytes_accessed=nbytes, transcendentals=trans)
 
@@ -90,13 +86,13 @@
     return lax.dot_general(a, b, (((ca,), (cb,)), ((), ())), preferred_element_type=F32)
 
 
-def query_kernel(info, own, oth, w, ids, out):
+def query_kernel(info, own, oth, w, ids, _, out):
     out[0:TOK, :] = dot(own[...], w[...], 1, 0).astype(BF16)
     out[TOK:CHIP, :] = dot(oth[...], w[...], 1, 0).astype(BF16)
     out[CHIP:, :] = ids[...]
 
 
-def project_query(info, own, oth, w, ids):
+def project_query(info, own, oth, w, ids, earlier):
     depth = own.shape[1]
     tile = 256
     steps = FEAT // tile
@@ -111,22 +107,23 @@
                 whole,
                 pl.BlockSpec((depth, tile), lambda j, info: (0, info[3] * steps + j)),
                 pl.BlockSpec((STAT, tile), lambda j, info: (0, j)),
+                pl.BlockSpec(memory_space=pl.ANY),
             ],
             out_specs=pl.BlockSpec((CHIP + STAT, tile), lambda j, info: (0, j)),
         ),
         out_shape=jax.ShapeDtypeStruct((CHIP + STAT, FEAT), BF16),
         compiler_params=params(WIDE_VMEM),
         cost_estimate=cost(2 * CHIP * depth * FEAT, 2 * depth * (FEAT + CHIP)),
-    )(info, own, oth, w, ids)
-
-
-def keyvalue_kernel(info, own, oth, wk, wv, k, v):
+    )(info, own, oth, w, ids, earlier)
+
+
+def keyvalue_kernel(info, own, oth, wk, wv, _, k, v):
     for tok, place in ((own, slice(0, TOK)), (oth, slice(TOK, CHIP))):
         k[place, :] = dot(tok[...], wk[...], 1, 0).astype(BF16)
         v[:, place] = dot(tok[...], wv[...], 1, 0).astype(BF16).T
 
 
-def project_keyvalue(info, own, oth, wk, wv):
+def project_keyvalue(info, own, oth, wk, wv, earlier):
     depth = own.shape[1]
     tile = 256
     steps = FEAT // tile
@@ -138,13 +135,13 @@
         grid_spec=pltpu.PrefetchScalarGridSpec(
             num_scalar_prefetch=1,
             grid=(steps,),
-            in_specs=[whole, whole, weight, weight],
+            in_specs=[whole, whole, weight, weight, pl.BlockSpec(memory_space=pl.ANY)],
             out_specs=[result, pl.BlockSpec((tile, CHIP), lambda j, info: (j, 0))],
         ),
         out_shape=[jax.ShapeDtypeStruct((CHIP, FEAT), BF16)] * 2,
         compiler_params=params(WIDE_VMEM),
         cost_estimate=cost(4 * CHIP * depth * FEAT, 2 * depth * (2 * FEAT + CHIP)),
-    )(info, own, oth, wk, wv)
+    )(info, own, oth, wk, wv, earlier)
 
 
 def split3(value):
@@ -220,27 +217,27 @@
         local_block(2, info, q3, k, v, out2)
 
 
+def held_specs(count):
+    return [pl.BlockSpec(memory_space=pltpu.VMEM)] * count
+
+
+def scalars(count):
+    return [pl.BlockSpec(memory_space=pltpu.SMEM)] * count
+
+
 def local_attention(kernel, info, queries, k, v, count):
     slab = jax.ShapeDtypeStruct((SLAB, CHIP), BF16)
-
-    def whole(array):
-        return pl.BlockSpec(array.shape, lambda j, info: (0, 0))
-
     return pl.pallas_call(
         kernel,
-        grid_spec=pltpu.PrefetchScalarGridSpec(
-            num_scalar_prefetch=1,
-            grid=(1,),
-            in_specs=[whole(a) for a in (*queries, k, v)],
-            out_specs=[whole(slab)] * count,
-        ),
+        in_specs=scalars(1) + held_specs(len(queries) + 2),
+        out_specs=held_specs(count),
         out_shape=[slab] * count,
         compiler_params=params(),
         cost_estimate=cost(4 * count * CHIP * CHIP * FEAT, 8 * CHIP * FEAT, 4 * CHIP * CHIP),
     )(info, *queries, k, v)
 
 
-def part_kernel(info, mem, out, held, sem):
+def part_kernel(info, mem, out, flag, held, sem):
     start = pl.multiple_of(info[3] * FEAT, FEAT)
     src = mem.at[pl.ds(2 * info[1], 2), :, :, pl.ds(start, FEAT)]
     copy = pltpu.make_async_copy(src, held, sem)
@@ -251,6 +248,7 @@
             cols = slice(h * HD, (h + 1) * HD)
             out[0, h // GROUP, block, 0, h % GROUP] = held[block, 0, :, cols]
             out[0, h // GROUP, block, 1, h % GROUP] = held[block, 1, :, cols].T
+    flag[...] = jnp.zeros_like(flag)
 
 
 def take_part(info, memory):
@@ -261,16 +259,47 @@
             num_scalar_prefetch=1,
             grid=(1,),
             in_specs=[pl.BlockSpec(memory_space=pltpu.HBM)],
-            out_specs=pl.BlockSpec(shape, lambda j, info: (0,) * 7),
+            out_specs=[
+                pl.BlockSpec(shape, lambda j, info: (0,) * 7),
+                pl.BlockSpec((8, HD), lambda j, info: (0, 0)),
+            ],
             scratch_shapes=[
                 pltpu.VMEM((2, 2, BLK, FEAT), BF16),
                 pltpu.SemaphoreType.DMA,
             ],
         ),
-        out_shape=jax.ShapeDtypeStruct(shape, BF16),
+        out_shape=[
+            jax.ShapeDtypeStruct(shape, BF16),
+            jax.ShapeDtypeStruct((8, HD), F32),
+        ],
         compiler_params=params(WIDE_VMEM),
         cost_estimate=cost(0, 2**20),
     )(info, memory)
+
+
+def join_kernel(group, *refs):
+    near, out, sem = refs[:RING], refs[-2], refs[-1]
+    copies = [
+        pltpu.make_async_copy(ref.at[:, group], out.at[pl.ds(s, 1)], sem.at[s])
+        for s, ref in enumerate(near)
+    ]
+    for copy in copies:
+        copy.start()
+    for copy in copies:
+        copy.wait()
+
+
+def join(group, near, *earlier):
+    shape = (RING, *near[0].shape[2:])
+    return pl.pallas_call(
+        functools.partial(join_kernel, group),
+        in_specs=any_specs(len(near) + len(earlier)),
+        out_specs=pl.BlockSpec(memory_space=pl.ANY),
+        out_shape=jax.ShapeDtypeStruct(shape, BF16),
+        scratch_shapes=[pltpu.SemaphoreType.DMA((RING,))],
+        compiler_params=params(),
+        cost_estimate=cost(0, 2**20),
+    )(*near, *earlier)
 
 
 def plan_kernel(info, ids, slots, blocks):
@@ -448,47 +477,44 @@
 
 
 def merge(info, gate, slabs):
-    half = pl.BlockSpec((TOK, FEAT), lambda j, info, gate: (0, 0))
     return pl.pallas_call(
         merge_kernel,
-        grid_spec=pltpu.PrefetchScalarGridSpec(
-            num_scalar_prefetch=2,
-            grid=(1,),
-            in_specs=[pl.BlockSpec(s.shape, lambda j, info, gate: (0, 0)) for s in slabs],
-            out_specs=[half] * 2,
-        ),
+        in_specs=scalars(2) + held_specs(len(slabs)),
+        out_specs=held_specs(2),
         out_shape=[jax.ShapeDtypeStruct((TOK, FEAT), BF16)] * 2,
         compiler_params=params(),
         cost_estimate=cost(20 * SLAB * CHIP, 8 * 2 * SLAB * CHIP),
     )(info, gate, *slabs)
 
 
-def output_kernel(info, own, oth, w_own, w_oth, out):
-    total = dot(own[...], w_own[...], 1, 0) + dot(oth[...], w_oth[...], 1, 0)
-    out[...] = total.astype(BF16)
+def output_kernel(info, own, oth, w, out):
+    c = info[3]
+    mine = pl.ds(pl.multiple_of(c * FEAT, FEAT), FEAT)
+    other = pl.ds(pl.multiple_of((1 - c) * FEAT, FEAT), FEAT)
+    tile = 512
+    for j in range(out.shape[1] // tile):
+        cols = slice(j * tile, (j + 1) * tile)
+        total = dot(own[...], w[mine, cols], 1, 0) + dot(oth[...], w[other, cols], 1, 0)
+        out[:, cols] = total.astype(BF16)
 
 
 def project_output(info, own, oth, w):
-    width = w.shape[1]
-    tile = 512
-    half = pl.BlockSpec((TOK, FEAT), lambda j, info: (0, 0))
+    def whole(array):
+        return pl.BlockSpec(array.shape, lambda j, info: (0, 0))
+
+    result = jax.ShapeDtypeStruct((TOK, w.shape[1]), BF16)
     return pl.pallas_call(
         output_kernel,
         grid_spec=pltpu.PrefetchScalarGridSpec(
             num_scalar_prefetch=1,
-            grid=(width // tile,),
-            in_specs=[
-                half,
-                half,
-                pl.BlockSpec((FEAT, tile), lambda j, info: (info[3], j)),
-                pl.BlockSpec((FEAT, tile), lambda j, info: (1 - info[3], j)),
-            ],
-            out_specs=pl.BlockSpec((TOK, tile), lambda j, info: (0, j)),
+            grid=(1,),
+            in_specs=[whole(own), whole(oth), whole(w)],
+            out_specs=whole(result),
         ),
-        out_shape=jax.ShapeDtypeStruct((TOK, width), BF16),
+        out_shape=result,
         compiler_params=params(),
-        cost_estimate=cost(4 * TOK * FEAT * width, 4 * FEAT * width),
-    )(info, own, oth, w, w)
+        cost_estimate=cost(4 * TOK * FEAT * w.shape[1], 4 * FEAT * w.shape[1]),
+    )(info, own, oth, w)
 
 
 def shards(tokens, block_ids, memory, w_query, w_key, w_value, w_out, gate_bias):
@@ -504,20 +530,19 @@
     ids_rows = jnp.zeros((STAT, FEAT), BF16).at[0:1, 0:32].set(ids_chip.astype(BF16))
 
     groups = HEADS // GROUP
-    part = take_part(info, memory)
+    part, taken = take_part(info, memory)
     near = [part] + [send(part, gather_move(0, d)) for d in (1, -1, 2)]
 
-    query = project_query(info, own, oth, w_query, ids_rows)
+    query = project_query(info, own, oth, w_query, ids_rows, taken)
     query1 = send(query, around(1))
     query2 = send(query, around(-1))
-    k, v = project_keyvalue(info, own, oth, w_key, w_value)
+    k, v = project_keyvalue(info, own, oth, w_key, w_value, query)
     query3 = send(query1, around(1))
     queries = [query, query1, query2, query3]
-    near = after(near, query, k)
 
     parts = []
     for g in range(groups):
-        mine = jnp.concatenate([part[:, g] for part in near])
+        mine = join(g, near, *((query1, k) if g == 1 else ()))
         below = send(mine, gather_move(1, 1))
         above = send(mine, gather_move(1, -1))
         far = send(below, gather_move(1, 1)) if g % 2 == 0 else send(above, gather_move(1, -1))

time: 114 us -> 112 us (0.982); the launches traced: 112 us -> 112 us
    pallas_call x3 -> x5, Pallas kernels: 12.1 us -> 12.2 us  [the longest x2 10.4 us: local_attention(): pl.pallas_call(kernel, in_specs=scalars(1) + held_specs(len(queries) + 2)...]
  transfers between devices with their start and end apart: 23 -> 23, of which waited for: 9 -> 11; matrix products, arithmetic and copies ran while one was open for 1% -> 1% of each run, Pallas kernels for 34% -> 35%
where the time goes in v3:
time: 112 us
  Pallas kernels  43.3 us (39%)
  starting transfers between devices  34.4 us (31%)
  waiting for transfers between devices  31.5 us (28%)
  other arithmetic  1.36 us (1%)
  local copies, waits for them, and re-layouts  1.21 us (1%)
    ppermute x23, starting transfers between devices, send(): return lax.ppermute(array, ('seq', 'mem'), pairs)  34.4 us
    ppermute x23, waiting for transfers between devices, send(): return lax.ppermute(array, ('seq', 'mem'), pairs)  31.5 us
    pallas_call x2, Pallas kernels, memory_attention(): pl.pallas_call(functools.partial(memory_kernel, group), grid_spec=pltpu.P...  12.1 us
    pallas_call x2, Pallas kernels, local_attention(): pl.pallas_call(kernel, in_specs=scalars(1) + held_specs(len(queries) + 2)...  10.4 us
    pallas_call x1, Pallas kernels, project_keyvalue(): pl.pallas_call(keyvalue_kernel, grid_spec=pltpu.PrefetchScalarGridSpec(nu...  6.45 us
    pallas_call x1, Pallas kernels, project_query(): pl.pallas_call(query_kernel, grid_spec=pltpu.PrefetchScalarGridSpec(num_s...  4.74 us
    pallas_call x1, Pallas kernels, project_output(): pl.pallas_call(output_kernel, grid_spec=pltpu.PrefetchScalarGridSpec(num_...  2.77 us
    pallas_call x1, Pallas kernels, take_part(): pl.pallas_call(part_kernel, grid_spec=pltpu.PrefetchScalarGridSpec(num_sc...  2.64 us
  transfers between devices with their start and end apart: 23, of which 11 were waited for; matrix products, arithmetic and copies ran while one was open for 1% of the time, Pallas kernels for 35%

profile of v3, /device:TPU:1, one launch (start us, length us, event | category | flops | bytes accessed | tf_op | source)
XLA Modules:
  0.0 112.1 jit_solution(8535122580269989144)
XLA Ops:
  0.0 1.4 %collective-permute-start = (bf16[256,2048]{1,0:T(8,128)(2,1)}, bf16[256,2048]{1,0:T(8,128)(2,1)}, u32[]{:S(2)}, u32[]{:S(2)}) collective-permute-start(bf16[256,2048]{1,0:T(8,128)(2,1)} %bitcast.14), channel_id=1, source_target_pairs={{0,16},{16,0},{32,48},{48,32},{64,80},{80,64},{96,112},{112,96},{1... | collective-permute-start | bytes 3145736 | tf_op jit(solution)/shard_map/ppermute | solution.py:42
  2.0 2.6 %shard_map.82 = (bf16[1,2,2,2,2,128,128]{6,5,4,3,2,1,0:T(8,128)(2,1)}, f32[8,128]{1,0:T(8,128)}) custom-call(s32[4]{0:T(128)} %pad_add_fusion.info, bf16[8,2,128,1024]{3,2,1,0:T(8,128)(2,1)} %mem.1), custom_call_target="tpu_custom_call" | custom-call | bytes 1048576 | tf_op jit(solution)/shard_map/pallas_call | solution.py:256
  4.7 3.8 %collective-permute-start.7 = (bf16[1,2,2,2,2,128,128]{6,5,4,3,2,1,0:T(8,128)(2,1)}, bf16[1,2,2,2,2,128,128]{6,5,4,3,2,1,0:T(8,128)(2,1)S(1)}, u32[]{:S(2)}, u32[]{:S(2)}) collective-permute-start(bf16[1,2,2,2,2,128,128]{6,5,4,3,2,1,0:T(8,128)(2,1)} %get-tuple-element.38.refs_0_), channel_id=1, source_target_pairs={{0,8},{16,18},{32,40},{48,50},{64,72},{80,82},{96,104},{112,114},{... | collective-permute-start | bytes 1572872 | tf_op jit(solution)/shard_map/ppermute | solution.py:42
  11.8 4.7 %shard_map.83.refs_0_._.q = bf16[528,512]{1,0:T(8,128)(2,1)} custom-call(s32[4]{0:T(128)} %pad_add_fusion.info, bf16[256,2048]{1,0:T(8,128)(2,1)} %bitcast.15, bf16[256,2048]{1,0:T(8,128)(2,1)} %collective-permute-done.oth, bf16[2048,1024]{1,0:T(8,128)(2,1)} %w.2, bf16[16,512]{1,0:T(8,128)(2,1)} %fusion.5.ids, f32[8,128]{1,0:T(8,128)} %get-tuple-element.35._), custom_call_target="tpu_custom_call" | custom-call | flops 1073741824 | bytes 4194304 | tf_op jit(solution)/shard_map/pallas_call | solution.py:100
  16.5 2.7 %collective-permute-start.2 = (bf16[528,512]{1,0:T(8,128)(2,1)}, bf16[528,512]{1,0:T(8,128)(2,1)S(1)}, u32[]{:S(2)}, u32[]{:S(2)}) collective-permute-start(bf16[528,512]{1,0:T(8,128)(2,1)} %shard_map.83.refs_0_._.q), channel_id=1, source_target_pairs={{0,32},{16,112},{32,64},{48,16},{64,96},{80,48},{96,0},{112,80},{1... | collective-permute-start | bytes 1622024 | tf_op jit(solution)/shard_map/ppermute | solution.py:42
  19.3 2.6 %collective-permute-done.6.refs_2_ = bf16[1,2,2,2,2,128,128]{6,5,4,3,2,1,0:T(8,128)(2,1)S(1)} collective-permute-done((bf16[1,2,2,2,2,128,128]{6,5,4,3,2,1,0:T(8,128)(2,1)}, bf16[1,2,2,2,2,128,128]{6,5,4,3,2,1,0:T(8,128)(2,1)S(1)}, u32[]{:S(2)}, u32[]{:S(2)}) %collective-permute-start.6) | collective-permute-done | bytes 524320 | tf_op jit(solution)/shard_map/ppermute | solution.py:42
  22.0 1.3 %collective-permute-start.8 = (bf16[4,2,2,2,128,128]{5,4,3,2,1,0:T(8,128)(2,1)S(1)}, bf16[4,2,2,2,128,128]{5,4,3,2,1,0:T(8,128)(2,1)}, u32[]{:S(2)}, u32[]{:S(2)}) collective-permute-start(bf16[4,2,2,2,128,128]{5,4,3,2,1,0:T(8,128)(2,1)S(1)} %shard_map.85.refs_4_), channel_id=1, source_target_pairs={{0,1},{16,20},{32,33},{48,52},{64,65},{80,84},{96,97},{112,116},{1... | collective-permute-start | bytes 3145736 | tf_op jit(solution)/shard_map/ppermute | solution.py:42
  23.3 6.5 %shard_map.87 = (bf16[512,512]{1,0:T(8,128)(2,1)}, bf16[512,512]{1,0:T(8,128)(2,1)}) custom-call(s32[4]{0:T(128)} %pad_add_fusion.info, bf16[256,2048]{1,0:T(8,128)(2,1)} %bitcast.16, bf16[256,2048]{1,0:T(8,128)(2,1)} %collective-permute-done.oth, bf16[2048,1024]{1,0:T(8,128)(2,1)} %wk.1, bf16[2048,1024]{1,0:T(8,128)(2,1)} %wv.1, ...), custom_call_target="tpu_custom_call" | custom-call | flops 2147483648 | bytes 6291456 | tf_op jit(solution)/shard_map/pallas_call | solution.py:133
  31.0 1.5 %collective-permute-start.15 = (bf16[4,2,2,2,128,128]{5,4,3,2,1,0:T(8,128)(2,1)S(1)}, bf16[4,2,2,2,128,128]{5,4,3,2,1,0:T(8,128)(2,1)S(1)}, u32[]{:S(2)}, u32[]{:S(2)}) collective-permute-start(bf16[4,2,2,2,128,128]{5,4,3,2,1,0:T(8,128)(2,1)S(1)} %shard_map.88.refs_4_), channel_id=1, source_target_pairs={{0,3},{16,28},{32,35},{48,60},{64,67},{80,92},{96,99},{112,124},{1... | collective-permute-start | bytes 3145736 | tf_op jit(solution)/shard_map/ppermute | solution.py:42
  32.5 1.3 %collective-permute-start.3 = (bf16[528,512]{1,0:T(8,128)(2,1)S(1)}, bf16[528,512]{1,0:T(8,128)(2,1)S(1)}, u32[]{:S(2)}, u32[]{:S(2)}) collective-permute-start(bf16[528,512]{1,0:T(8,128)(2,1)S(1)} %copy-done), channel_id=1, source_target_pairs={{0,96},{16,48},{32,0},{48,80},{64,32},{80,112},{96,64},{112,16},{1... | collective-permute-start | bytes 1622024 | tf_op jit(solution)/shard_map/ppermute | solution.py:42
  33.8 1.3 %collective-permute-start.9 = (bf16[4,2,2,2,128,128]{5,4,3,2,1,0:T(8,128)(2,1)S(1)}, bf16[4,2,2,2,128,128]{5,4,3,2,1,0:T(8,128)(2,1)S(1)}, u32[]{:S(2)}, u32[]{:S(2)}) collective-permute-start(bf16[4,2,2,2,128,128]{5,4,3,2,1,0:T(8,128)(2,1)S(1)} %shard_map.85.refs_4_), channel_id=1, source_target_pairs={{0,3},{16,28},{32,35},{48,60},{64,67},{80,92},{96,99},{112,124},{1... | collective-permute-start | bytes 3145736 | tf_op jit(solution)/shard_map/ppermute | solution.py:42
  35.1 2.3 %collective-permute-done.8.refs_5_ = bf16[4,2,2,2,128,128]{5,4,3,2,1,0:T(8,128)(2,1)} collective-permute-done((bf16[4,2,2,2,128,128]{5,4,3,2,1,0:T(8,128)(2,1)S(1)}, bf16[4,2,2,2,128,128]{5,4,3,2,1,0:T(8,128)(2,1)}, u32[]{:S(2)}, u32[]{:S(2)}) %collective-permute-start.8) | collective-permute-done | bytes 1048608 | tf_op jit(solution)/shard_map/ppermute | solution.py:42
  37.4 2.7 %collective-permute-start.4 = (bf16[528,512]{1,0:T(8,128)(2,1)S(1)}, bf16[528,512]{1,0:T(8,128)(2,1)S(1)}, u32[]{:S(2)}, u32[]{:S(2)}) collective-permute-start(bf16[528,512]{1,0:T(8,128)(2,1)S(1)} %collective-permute-done.2.refs_1_.refs_4_.q1), channel_id=1, source_target_pairs={{0,32},{16,112},{32,64},{48,16},{64,96},{80,48},{96,0},{112,80},{1... | collective-permute-start | bytes 1622024 | tf_op jit(solution)/shard_map/ppermute | solution.py:42
  40.1 1.9 %collective-permute-done.3.refs_2_.q2 = bf16[528,512]{1,0:T(8,128)(2,1)S(1)} collective-permute-done((bf16[528,512]{1,0:T(8,128)(2,1)S(1)}, bf16[528,512]{1,0:T(8,128)(2,1)S(1)}, u32[]{:S(2)}, u32[]{:S(2)}) %collective-permute-start.3) | collective-permute-done | bytes 540704 | tf_op jit(solution)/shard_map/ppermute | solution.py:42
  42.0 3.0 %collective-permute-done.15.refs_6_ = bf16[4,2,2,2,128,128]{5,4,3,2,1,0:T(8,128)(2,1)S(1)} collective-permute-done((bf16[4,2,2,2,128,128]{5,4,3,2,1,0:T(8,128)(2,1)S(1)}, bf16[4,2,2,2,128,128]{5,4,3,2,1,0:T(8,128)(2,1)S(1)}, u32[]{:S(2)}, u32[]{:S(2)}) %collective-permute-start.15) | collective-permute-done | bytes 1048608 | tf_op jit(solution)/shard_map/ppermute | solution.py:42
  45.0 2.7 %collective-permute-start.16 = (bf16[4,2,2,2,128,128]{5,4,3,2,1,0:T(8,128)(2,1)S(1)}, bf16[4,2,2,2,128,128]{5,4,3,2,1,0:T(8,128)(2,1)S(1)}, u32[]{:S(2)}, u32[]{:S(2)}) collective-permute-start(bf16[4,2,2,2,128,128]{5,4,3,2,1,0:T(8,128)(2,1)S(1)} %collective-permute-done.15.refs_6_), channel_id=1, source_target_pairs={{0,3},{16,28},{32,35},{48,60},{64,67},{80,92},{96,99},{112,124},{1... | collective-permute-start | bytes 3145736 | tf_op jit(solution)/shard_map/ppermute | solution.py:42
  48.7 7.0 %shard_map.91 = (bf16[528,512]{1,0:T(8,128)(2,1)S(1)}, bf16[528,512]{1,0:T(8,128)(2,1)S(1)}) custom-call(s32[4]{0:T(128)S(1)} %copy-done.6, bf16[528,512]{1,0:T(8,128)(2,1)S(1)} %collective-permute-done.2.refs_1_.refs_4_.q1, bf16[528,512]{1,0:T(8,128)(2,1)S(1)} %collective-permute-done.3.refs_2_.q2, bf16[528,512]{1,0:T(8,128)(2,1)S(1)} %collective-permute-done.4.refs_3_.q3, ...), custom_call_target="tpu_custom_call" | custom-call | flops 1073741824 | bytes 2097152 | tf_op jit(solution)/shard_map/pallas_call | solution.py:230
  55.8 2.7 %collective-permute-start.20 = (bf16[528,512]{1,0:T(8,128)(2,1)S(1)}, bf16[528,512]{1,0:T(8,128)(2,1)S(1)}, u32[]{:S(2)}, u32[]{:S(2)}) collective-permute-start(bf16[528,512]{1,0:T(8,128)(2,1)S(1)} %get-tuple-element.49), channel_id=1, source_target_pairs={{0,32},{16,48},{32,64},{48,80},{64,96},{80,112},{1,33},{17,49},{33... | collective-permute-start | bytes 1622024 | tf_op jit(solution)/shard_map/ppermute | solution.py:42
  58.5 2.6 %collective-permute-start.21 = (bf16[528,512]{1,0:T(8,128)(2,1)S(1)}, bf16[528,512]{1,0:T(8,128)(2,1)S(1)}, u32[]{:S(2)}, u32[]{:S(2)}) collective-permute-start(bf16[528,512]{1,0:T(8,128)(2,1)S(1)} %get-tuple-element.50), channel_id=1, source_target_pairs={{0,64},{16,80},{32,96},{48,112},{1,65},{17,81},{33,97},{49,113},{2... | collective-permute-start | bytes 1622024 | tf_op jit(solution)/shard_map/ppermute | solution.py:42
  61.2 2.4 %shard_map.84 = (s32[144]{0:T(256)S(1)}, s32[80]{0:T(128)S(1)}) custom-call(s32[4]{0:T(128)S(1)} %copy-done.6, s32[128]{0:T(128)S(1)} %maximum_convert_fusion.ids), custom_call_target="tpu_custom_call" | custom-call | flops 1000 | bytes 1000 | tf_op jit(solution)/shard_map/pallas_call | solution.py:334
  63.6 6.4 %shard_map.86 = (bf16[272,512]{1,0:T(8,128)(2,1)S(1)}, bf16[272,512]{1,0:T(8,128)(2,1)S(1)}, bf16[272,512]{1,0:T(8,128)(2,1)S(1)}, bf16[272,512]{1,0:T(8,128)(2,1)S(1)}) custom-call(s32[144]{0:T(256)S(1)} %get-tuple-element.36.slots, s32[80]{0:T(128)S(1)} %get-tuple-element.37.blocks, bf16[528,512]{1,0:T(8,128)(2,1)S(1)} %copy-done, ...), custom_call_target="tpu_custom_call" | custom-call | flops 536870912 | bytes 6291456 | tf_op jit(solution)/shard_map/pallas_call | solution.py:423
  70.2 2.7 %collective-permute-start.12 = (bf16[272,512]{1,0:T(8,128)(2,1)S(1)}, bf16[272,512]{1,0:T(8,128)(2,1)S(1)}, u32[]{:S(2)}, u32[]{:S(2)}) collective-permute-start(bf16[272,512]{1,0:T(8,128)(2,1)S(1)} %get-tuple-element.41), channel_id=1, source_target_pairs={{0,32},{16,112},{32,64},{48,16},{64,96},{80,48},{96,0},{112,80},{1... | collective-permute-start | bytes 835592 | tf_op jit(solution)/shard_map/ppermute | solution.py:42
  72.8 5.7 %shard_map.89 = (bf16[272,512]{1,0:T(8,128)(2,1)S(1)}, bf16[272,512]{1,0:T(8,128)(2,1)S(1)}, bf16[272,512]{1,0:T(8,128)(2,1)S(1)}, bf16[272,512]{1,0:T(8,128)(2,1)S(1)}) custom-call(s32[144]{0:T(256)S(1)} %get-tuple-element.36.slots, s32[80]{0:T(128)S(1)} %get-tuple-element.37.blocks, bf16[528,512]{1,0:T(8,128)(2,1)S(1)} %copy-done, ...), custom_call_target="tpu_custom_call" | custom-call | flops 536870912 | bytes 6291456 | tf_op jit(solution)/shard_map/pallas_call | solution.py:423
  78.6 1.8 %collective-permute-done.21.refs_10_ = bf16[528,512]{1,0:T(8,128)(2,1)S(1)} collective-permute-done((bf16[528,512]{1,0:T(8,128)(2,1)S(1)}, bf16[528,512]{1,0:T(8,128)(2,1)S(1)}, u32[]{:S(2)}, u32[]{:S(2)}) %collective-permute-start.21) | collective-permute-done | bytes 540704 | tf_op jit(solution)/shard_map/ppermute | solution.py:42
  81.3 5.1 %collective-permute-done.11.refs_1_ = bf16[272,512]{1,0:T(8,128)(2,1)S(1)} collective-permute-done((bf16[272,512]{1,0:T(8,128)(2,1)S(1)}, bf16[272,512]{1,0:T(8,128)(2,1)S(1)}, u32[]{:S(2)}, u32[]{:S(2)}) %collective-permute-start.11) | collective-permute-done | bytes 278560 | tf_op jit(solution)/shard_map/ppermute | solution.py:42
  86.3 3.0 %collective-permute-start.19 = (bf16[272,512]{1,0:T(8,128)(2,1)S(1)}, bf16[272,512]{1,0:T(8,128)(2,1)S(1)}, u32[]{:S(2)}, u32[]{:S(2)}) collective-permute-start(bf16[272,512]{1,0:T(8,128)(2,1)S(1)} %get-tuple-element.47), channel_id=1, source_target_pairs={{0,64},{16,80},{32,96},{48,112},{64,0},{80,16},{96,32},{112,48},{1... | collective-permute-start | bytes 835592 | tf_op jit(solution)/shard_map/ppermute | solution.py:42
  89.3 3.4 %shard_map.90.refs_8_ = bf16[528,512]{1,0:T(8,128)(2,1)S(1)} custom-call(s32[4]{0:T(128)S(1)} %copy-done.6, bf16[528,512]{1,0:T(8,128)(2,1)S(1)} %copy-done, bf16[512,512]{1,0:T(8,128)(2,1)S(1)} %copy-done.3, bf16[512,512]{1,0:T(8,128)(2,1)S(1)} %copy-done.5), custom_call_target="tpu_custom_call" | custom-call | flops 536870912 | bytes 2097152 | tf_op jit(solution)/shard_map/pallas_call | solution.py:230
  92.7 5.6 %collective-permute-done.17.refs_5_ = bf16[272,512]{1,0:T(8,128)(2,1)S(1)} collective-permute-done((bf16[272,512]{1,0:T(8,128)(2,1)S(1)}, bf16[272,512]{1,0:T(8,128)(2,1)S(1)}, u32[]{:S(2)}, u32[]{:S(2)}) %collective-permute-start.17) | collective-permute-done | bytes 278560 | tf_op jit(solution)/shard_map/ppermute | solution.py:42
  98.3 6.0 %collective-permute-done.19.refs_7_ = bf16[272,512]{1,0:T(8,128)(2,1)S(1)} collective-permute-done((bf16[272,512]{1,0:T(8,128)(2,1)S(1)}, bf16[272,512]{1,0:T(8,128)(2,1)S(1)}, u32[]{:S(2)}, u32[]{:S(2)}) %collective-permute-start.19) | collective-permute-done | bytes 278560 | tf_op jit(solution)/shard_map/ppermute | solution.py:42
  104.3 1.6 %shard_map.92 = (bf16[256,512]{1,0:T(8,128)(2,1)S(1)}, bf16[256,512]{1,0:T(8,128)(2,1)S(1)}) custom-call(s32[4]{0:T(128)S(1)} %copy-done.6, f32[8]{0:T(128)S(1)} %copy-done.7, bf16[272,512]{1,0:T(8,128)(2,1)S(1)} %get-tuple-element.39.refs_0_, bf16[272,512]{1,0:T(8,128)(2,1)S(1)} %collective-permute-done.11.refs_1_, ...), custom_call_target="tpu_custom_call" | custom-call | flops 5406720 | bytes 4325376 | tf_op jit(solution)/shard_map/pallas_call | solution.py:480
  105.9 2.3 %collective-permute-start.22 = (bf16[256,512]{1,0:T(8,128)(2,1)S(1)}, bf16[256,512]{1,0:T(8,128)(2,1)S(1)}, u32[]{:S(2)}, u32[]{:S(2)}) collective-permute-start(bf16[256,512]{1,0:T(8,128)(2,1)S(1)} %get-tuple-element.52), channel_id=1, source_target_pairs={{0,16},{16,0},{32,48},{48,32},{64,80},{80,64},{96,112},{112,96},{1... | collective-permute-start | bytes 786440 | tf_op jit(solution)/shard_map/ppermute | solution.py:42
  109.3 2.8 %shard_map.93 = bf16[256,2048]{1,0:T(8,128)(2,1)} custom-call(s32[4]{0:T(128)S(1)} %copy-done.6, bf16[256,512]{1,0:T(8,128)(2,1)S(1)} %get-tuple-element.51.own, bf16[256,512]{1,0:T(8,128)(2,1)S(1)} %collective-permute-done.22.oth, bf16[1024,2048]{1,0:T(8,128)(2,1)S(1)} %copy-done.1), custom_call_target="tpu_custom_call" | custom-call | flops 1073741824 | bytes 4194304 | tf_op jit(solution)/shard_map/pallas_call | solution.py:506
  (54 shorter events, 8.7 us)
Async XLA Ops:
  0.0 9.9 %copy-start.8 = (s32[1,2,8]{2,1,0:T(2,128)S(1)}, s32[1,2,8]{2,1,0:T(2,128)}, u32[]{:S(2)}) copy-start(s32[1,2,8]{2,1,0:T(2,128)} %param.11) | copy-start | bytes 196
  0.0 11.8 %collective-permute-start = (bf16[256,2048]{1,0:T(8,128)(2,1)}, bf16[256,2048]{1,0:T(8,128)(2,1)}, u32[]{:S(2)}, u32[]{:S(2)}) collective-permute-start(bf16[256,2048]{1,0:T(8,128)(2,1)} %bitcast.14), channel_id=1, source_target_pairs={{0,16},{16,0},{32,48},{48,32},{64,80},{80,64},{96,112},{112,96},{1... | collective-permute-start | bytes 3145736 | tf_op jit(solution)/shard_map/ppermute | solution.py:42
  4.7 17.2 %copy-start.4 = (bf16[1,2,2,2,2,128,128]{6,5,4,3,2,1,0:T(8,128)(2,1)S(1)}, bf16[1,2,2,2,2,128,128]{6,5,4,3,2,1,0:T(8,128)(2,1)}, u32[]{:S(2)}) copy-start(bf16[1,2,2,2,2,128,128]{6,5,4,3,2,1,0:T(8,128)(2,1)} %get-tuple-element.38.refs_0_) | copy-start | bytes 1572868
  4.7 14.6 %collective-permute-start.7 = (bf16[1,2,2,2,2,128,128]{6,5,4,3,2,1,0:T(8,128)(2,1)}, bf16[1,2,2,2,2,128,128]{6,5,4,3,2,1,0:T(8,128)(2,1)S(1)}, u32[]{:S(2)}, u32[]{:S(2)}) collective-permute-start(bf16[1,2,2,2,2,128,128]{6,5,4,3,2,1,0:T(8,128)(2,1)} %get-tuple-element.38.refs_0_), channel_id=1, source_target_pairs={{0,8},{16,18},{32,40},{48,50},{64,72},{80,82},{96,104},{112,114},{... | collective-permute-start | bytes 1572872 | tf_op jit(solution)/shard_map/ppermute | solution.py:42
  8.4 13.5 %collective-permute-start.6 = (bf16[1,2,2,2,2,128,128]{6,5,4,3,2,1,0:T(8,128)(2,1)}, bf16[1,2,2,2,2,128,128]{6,5,4,3,2,1,0:T(8,128)(2,1)S(1)}, u32[]{:S(2)}, u32[]{:S(2)}) collective-permute-start(bf16[1,2,2,2,2,128,128]{6,5,4,3,2,1,0:T(8,128)(2,1)} %get-tuple-element.38.refs_0_), channel_id=1, source_target_pairs={{0,12},{16,19},{32,44},{48,51},{64,76},{80,83},{96,108},{112,115},... | collective-permute-start | bytes 1572872 | tf_op jit(solution)/shard_map/ppermute | solution.py:42
  8.9 13.0 %collective-permute-start.5 = (bf16[1,2,2,2,2,128,128]{6,5,4,3,2,1,0:T(8,128)(2,1)}, bf16[1,2,2,2,2,128,128]{6,5,4,3,2,1,0:T(8,128)(2,1)S(1)}, u32[]{:S(2)}, u32[]{:S(2)}) collective-permute-start(bf16[1,2,2,2,2,128,128]{6,5,4,3,2,1,0:T(8,128)(2,1)} %get-tuple-element.38.refs_0_), channel_id=1, source_target_pairs={{0,4},{16,17},{32,36},{48,49},{64,68},{80,81},{96,100},{112,113},{... | collective-permute-start | bytes 1572872 | tf_op jit(solution)/shard_map/ppermute | solution.py:42
  10.0 1.1 %collective-permute-start.1 = (s32[1,16]{1,0:T(1,128)S(1)}, s32[1,16]{1,0:T(1,128)S(1)}, u32[]{:S(2)}, u32[]{:S(2)}) collective-permute-start(s32[1,16]{1,0:T(1,128)S(1)} %concatenate.19), channel_id=1, source_target_pairs={{0,16},{16,0},{32,48},{48,32},{64,80},{80,64},{96,112},{112,96},{1... | collective-permute-start | bytes 200 | tf_op jit(solution)/shard_map/ppermute | solution.py:42
  16.5 13.2 %collective-permute-start.2 = (bf16[528,512]{1,0:T(8,128)(2,1)}, bf16[528,512]{1,0:T(8,128)(2,1)S(1)}, u32[]{:S(2)}, u32[]{:S(2)}) collective-permute-start(bf16[528,512]{1,0:T(8,128)(2,1)} %shard_map.83.refs_0_._.q), channel_id=1, source_target_pairs={{0,32},{16,112},{32,64},{48,16},{64,96},{80,48},{96,0},{112,80},{1... | collective-permute-start | bytes 1622024 | tf_op jit(solution)/shard_map/ppermute | solution.py:42
  22.0 15.3 %collective-permute-start.8 = (bf16[4,2,2,2,128,128]{5,4,3,2,1,0:T(8,128)(2,1)S(1)}, bf16[4,2,2,2,128,128]{5,4,3,2,1,0:T(8,128)(2,1)}, u32[]{:S(2)}, u32[]{:S(2)}) collective-permute-start(bf16[4,2,2,2,128,128]{5,4,3,2,1,0:T(8,128)(2,1)S(1)} %shard_map.85.refs_4_), channel_id=1, source_target_pairs={{0,1},{16,20},{32,33},{48,52},{64,65},{80,84},{96,97},{112,116},{1... | collective-permute-start | bytes 3145736 | tf_op jit(solution)/shard_map/ppermute | solution.py:42
  23.3 25.4 %copy-start.6 = (s32[4]{0:T(128)S(1)}, s32[4]{0:T(128)}, u32[]{:S(2)}) copy-start(s32[4]{0:T(128)} %pad_add_fusion.info) | copy-start | bytes 52
  29.8 2.8 %copy-start = (bf16[528,512]{1,0:T(8,128)(2,1)S(1)}, bf16[528,512]{1,0:T(8,128)(2,1)}, u32[]{:S(2)}) copy-start(bf16[528,512]{1,0:T(8,128)(2,1)} %shard_map.83.refs_0_._.q) | copy-start | bytes 1622020
  29.8 1.1 copy-start.2
  30.9 17.9 %copy-start.5 = (bf16[512,512]{1,0:T(8,128)(2,1)S(1)}, bf16[512,512]{1,0:T(8,128)(2,1)}, u32[]{:S(2)}) copy-start(bf16[512,512]{1,0:T(8,128)(2,1)} %get-tuple-element.48.v) | copy-start | bytes 1572868
  31.0 14.0 %collective-permute-start.15 = (bf16[4,2,2,2,128,128]{5,4,3,2,1,0:T(8,128)(2,1)S(1)}, bf16[4,2,2,2,128,128]{5,4,3,2,1,0:T(8,128)(2,1)S(1)}, u32[]{:S(2)}, u32[]{:S(2)}) collective-permute-start(bf16[4,2,2,2,128,128]{5,4,3,2,1,0:T(8,128)(2,1)S(1)} %shard_map.88.refs_4_), channel_id=1, source_target_pairs={{0,3},{16,28},{32,35},{48,60},{64,67},{80,92},{96,99},{112,124},{1... | collective-permute-start | bytes 3145736 | tf_op jit(solution)/shard_map/ppermute | solution.py:42
  32.5 9.5 %collective-permute-start.3 = (bf16[528,512]{1,0:T(8,128)(2,1)S(1)}, bf16[528,512]{1,0:T(8,128)(2,1)S(1)}, u32[]{:S(2)}, u32[]{:S(2)}) collective-permute-start(bf16[528,512]{1,0:T(8,128)(2,1)S(1)} %copy-done), channel_id=1, source_target_pairs={{0,96},{16,48},{32,0},{48,80},{64,32},{80,112},{96,64},{112,16},{1... | collective-permute-start | bytes 1622024 | tf_op jit(solution)/shard_map/ppermute | solution.py:42
  33.8 24.7 %collective-permute-start.9 = (bf16[4,2,2,2,128,128]{5,4,3,2,1,0:T(8,128)(2,1)S(1)}, bf16[4,2,2,2,128,128]{5,4,3,2,1,0:T(8,128)(2,1)S(1)}, u32[]{:S(2)}, u32[]{:S(2)}) collective-permute-start(bf16[4,2,2,2,128,128]{5,4,3,2,1,0:T(8,128)(2,1)S(1)} %shard_map.85.refs_4_), channel_id=1, source_target_pairs={{0,3},{16,28},{32,35},{48,60},{64,67},{80,92},{96,99},{112,124},{1... | collective-permute-start | bytes 3145736 | tf_op jit(solution)/shard_map/ppermute | solution.py:42
  37.4 26.2 %collective-permute-start.10 = (bf16[4,2,2,2,128,128]{5,4,3,2,1,0:T(8,128)(2,1)}, bf16[4,2,2,2,128,128]{5,4,3,2,1,0:T(8,128)(2,1)S(1)}, u32[]{:S(2)}, u32[]{:S(2)}) collective-permute-start(bf16[4,2,2,2,128,128]{5,4,3,2,1,0:T(8,128)(2,1)} %collective-permute-done.8.refs_5_), channel_id=1, source_target_pairs={{0,1},{16,20},{32,33},{48,52},{64,65},{80,84},{96,97},{112,116},{1... | collective-permute-start | bytes 3145736 | tf_op jit(solution)/shard_map/ppermute | solution.py:42
  37.4 11.4 %collective-permute-start.4 = (bf16[528,512]{1,0:T(8,128)(2,1)S(1)}, bf16[528,512]{1,0:T(8,128)(2,1)S(1)}, u32[]{:S(2)}, u32[]{:S(2)}) collective-permute-start(bf16[528,512]{1,0:T(8,128)(2,1)S(1)} %collective-permute-done.2.refs_1_.refs_4_.q1), channel_id=1, source_target_pairs={{0,32},{16,112},{32,64},{48,16},{64,96},{80,48},{96,0},{112,80},{1... | collective-permute-start | bytes 1622024 | tf_op jit(solution)/shard_map/ppermute | solution.py:42
  42.0 28.1 %collective-permute-start.14 = (bf16[4,2,2,2,128,128]{5,4,3,2,1,0:T(8,128)(2,1)S(1)}, bf16[4,2,2,2,128,128]{5,4,3,2,1,0:T(8,128)(2,1)S(1)}, u32[]{:S(2)}, u32[]{:S(2)}) collective-permute-start(bf16[4,2,2,2,128,128]{5,4,3,2,1,0:T(8,128)(2,1)S(1)} %shard_map.88.refs_4_), channel_id=1, source_target_pairs={{0,1},{16,20},{32,33},{48,52},{64,65},{80,84},{96,97},{112,116},{1... | collective-permute-start | bytes 3145736 | tf_op jit(solution)/shard_map/ppermute | solution.py:42
  45.0 27.8 %collective-permute-start.16 = (bf16[4,2,2,2,128,128]{5,4,3,2,1,0:T(8,128)(2,1)S(1)}, bf16[4,2,2,2,128,128]{5,4,3,2,1,0:T(8,128)(2,1)S(1)}, u32[]{:S(2)}, u32[]{:S(2)}) collective-permute-start(bf16[4,2,2,2,128,128]{5,4,3,2,1,0:T(8,128)(2,1)S(1)} %collective-permute-done.15.refs_6_), channel_id=1, source_target_pairs={{0,3},{16,28},{32,35},{48,60},{64,67},{80,92},{96,99},{112,124},{1... | collective-permute-start | bytes 3145736 | tf_op jit(solution)/shard_map/ppermute | solution.py:42
  55.8 22.7 %collective-permute-start.20 = (bf16[528,512]{1,0:T(8,128)(2,1)S(1)}, bf16[528,512]{1,0:T(8,128)(2,1)S(1)}, u32[]{:S(2)}, u32[]{:S(2)}) collective-permute-start(bf16[528,512]{1,0:T(8,128)(2,1)S(1)} %get-tuple-element.49), channel_id=1, source_target_pairs={{0,32},{16,48},{32,64},{48,80},{64,96},{80,112},{1,33},{17,49},{33... | collective-permute-start | bytes 1622024 | tf_op jit(solution)/shard_map/ppermute | solution.py:42
  58.5 21.9 %collective-permute-start.21 = (bf16[528,512]{1,0:T(8,128)(2,1)S(1)}, bf16[528,512]{1,0:T(8,128)(2,1)S(1)}, u32[]{:S(2)}, u32[]{:S(2)}) collective-permute-start(bf16[528,512]{1,0:T(8,128)(2,1)S(1)} %get-tuple-element.50), channel_id=1, source_target_pairs={{0,64},{16,80},{32,96},{48,112},{1,65},{17,81},{33,97},{49,113},{2... | collective-permute-start | bytes 1622024 | tf_op jit(solution)/shard_map/ppermute | solution.py:42
  70.1 19.2 %copy-start.3 = (bf16[512,512]{1,0:T(8,128)(2,1)S(1)}, bf16[512,512]{1,0:T(8,128)(2,1)}, u32[]{:S(2)}) copy-start(bf16[512,512]{1,0:T(8,128)(2,1)} %get-tuple-element.43.refs_5_.k) | copy-start | bytes 1572868
  70.1 16.3 %collective-permute-start.11 = (bf16[272,512]{1,0:T(8,128)(2,1)S(1)}, bf16[272,512]{1,0:T(8,128)(2,1)S(1)}, u32[]{:S(2)}, u32[]{:S(2)}) collective-permute-start(bf16[272,512]{1,0:T(8,128)(2,1)S(1)} %get-tuple-element.40), channel_id=1, source_target_pairs={{0,96},{16,48},{32,0},{48,80},{64,32},{80,112},{96,64},{112,16},{1... | collective-permute-start | bytes 835592 | tf_op jit(solution)/shard_map/ppermute | solution.py:42
  70.2 22.5 %collective-permute-start.12 = (bf16[272,512]{1,0:T(8,128)(2,1)S(1)}, bf16[272,512]{1,0:T(8,128)(2,1)S(1)}, u32[]{:S(2)}, u32[]{:S(2)}) collective-permute-start(bf16[272,512]{1,0:T(8,128)(2,1)S(1)} %get-tuple-element.41), channel_id=1, source_target_pairs={{0,32},{16,112},{32,64},{48,16},{64,96},{80,48},{96,0},{112,80},{1... | collective-permute-start | bytes 835592 | tf_op jit(solution)/shard_map/ppermute | solution.py:42
  72.8 31.5 %copy-start.7 = (f32[8]{0:T(128)S(1)}, f32[8]{0:T(128)}, u32[]{:S(2)}) copy-start(f32[8]{0:T(128)} %gate.1) | copy-start | bytes 100
  72.8 19.9 %collective-permute-start.13 = (bf16[272,512]{1,0:T(8,128)(2,1)S(1)}, bf16[272,512]{1,0:T(8,128)(2,1)S(1)}, u32[]{:S(2)}, u32[]{:S(2)}) collective-permute-start(bf16[272,512]{1,0:T(8,128)(2,1)S(1)} %get-tuple-element.42), channel_id=1, source_target_pairs={{0,64},{16,80},{32,96},{48,112},{64,0},{80,16},{96,32},{112,48},{1... | collective-permute-start | bytes 835592 | tf_op jit(solution)/shard_map/ppermute | solution.py:42
  78.5 30.8 %copy-start.1 = (bf16[1024,2048]{1,0:T(8,128)(2,1)S(1)}, bf16[1024,2048]{1,0:T(8,128)(2,1)}, u32[]{:S(2)}) copy-start(bf16[1024,2048]{1,0:T(8,128)(2,1)} %w.3) | copy-start | bytes 12582916
  78.5 19.8 %collective-permute-start.17 = (bf16[272,512]{1,0:T(8,128)(2,1)S(1)}, bf16[272,512]{1,0:T(8,128)(2,1)S(1)}, u32[]{:S(2)}, u32[]{:S(2)}) collective-permute-start(bf16[272,512]{1,0:T(8,128)(2,1)S(1)} %get-tuple-element.45), channel_id=1, source_target_pairs={{0,96},{16,48},{32,0},{48,80},{64,32},{80,112},{96,64},{112,16},{1... | collective-permute-start | bytes 835592 | tf_op jit(solution)/shard_map/ppermute | solution.py:42
  80.4 18.0 %collective-permute-start.18 = (bf16[272,512]{1,0:T(8,128)(2,1)S(1)}, bf16[272,512]{1,0:T(8,128)(2,1)S(1)}, u32[]{:S(2)}, u32[]{:S(2)}) collective-permute-start(bf16[272,512]{1,0:T(8,128)(2,1)S(1)} %get-tuple-element.46), channel_id=1, source_target_pairs={{0,32},{16,112},{32,64},{48,16},{64,96},{80,48},{96,0},{112,80},{1... | collective-permute-start | bytes 835592 | tf_op jit(solution)/shard_map/ppermute | solution.py:42
  86.3 17.9 %collective-permute-start.19 = (bf16[272,512]{1,0:T(8,128)(2,1)S(1)}, bf16[272,512]{1,0:T(8,128)(2,1)S(1)}, u32[]{:S(2)}, u32[]{:S(2)}) collective-permute-start(bf16[272,512]{1,0:T(8,128)(2,1)S(1)} %get-tuple-element.47), channel_id=1, source_target_pairs={{0,64},{16,80},{32,96},{48,112},{64,0},{80,16},{96,32},{112,48},{1... | collective-permute-start | bytes 835592 | tf_op jit(solution)/shard_map/ppermute | solution.py:42
  105.9 3.4 %collective-permute-start.22 = (bf16[256,512]{1,0:T(8,128)(2,1)S(1)}, bf16[256,512]{1,0:T(8,128)(2,1)S(1)}, u32[]{:S(2)}, u32[]{:S(2)}) collective-permute-start(bf16[256,512]{1,0:T(8,128)(2,1)S(1)} %get-tuple-element.52), channel_id=1, source_target_pairs={{0,16},{16,0},{32,48},{48,32},{64,80},{80,64},{96,112},{112,96},{1... | collective-permute-start | bytes 786440 | tf_op jit(solution)/shard_map/ppermute | solution.py:42

commit v4 on v3

--- a/solution.py
+++ b/solution.py
@@ -204,17 +204,19 @@
     local_block(0, info, q, k, v, out)
 
 
-def next_kernel(info, q1, q2, q3, k, v, out1, out2):
+def next_kernel(info, q1, q2, k, v, out):
     y, c = info[1], info[3]
     for near, here in ((q2, c == 0), (q1, c != 0)):
 
         @pl.when((y + 1 < RING) & here)
         def _():
-            local_block(1, info, near, k, v, out1)
-
-    @pl.when(y + 2 < RING)
+            local_block(1, info, near, k, v, out)
+
+
+def second_kernel(info, q3, k, v, _, out):
+    @pl.when(info[1] + 2 < RING)
     def _():
-        local_block(2, info, q3, k, v, out2)
+        local_block(2, info, q3, k, v, out)
 
 
 def held_specs(count):
@@ -225,16 +227,17 @@
     return [pl.BlockSpec(memory_space=pltpu.SMEM)] * count
 
 
-def local_attention(kernel, info, queries, k, v, count):
+def local_attention(kernel, info, queries, k, v, *earlier):
+    count = 1
     slab = jax.ShapeDtypeStruct((SLAB, CHIP), BF16)
     return pl.pallas_call(
         kernel,
-        in_specs=scalars(1) + held_specs(len(queries) + 2),
+        in_specs=scalars(1) + held_specs(len(queries) + 2) + any_specs(len(earlier)),
         out_specs=held_specs(count),
         out_shape=[slab] * count,
         compiler_params=params(),
         cost_estimate=cost(4 * count * CHIP * CHIP * FEAT, 8 * CHIP * FEAT, 4 * CHIP * CHIP),
-    )(info, *queries, k, v)
+    )(info, *queries, k, v, *earlier)
 
 
 def part_kernel(info, mem, out, flag, held, sem):
@@ -548,10 +551,11 @@
         far = send(below, gather_move(1, 1)) if g % 2 == 0 else send(above, gather_move(1, -1))
         parts.append((mine, below, above, far))
 
-    (local0,) = local_attention(same_kernel, info, [query], k, v, 1)
+    (local0,) = local_attention(same_kernel, info, [query], k, v)
     ids = jnp.concatenate([q[CHIP, 0:32] for q in queries]).astype(jnp.int32)
     plan = plan_units(info, ids)
-    local1, local2 = local_attention(next_kernel, info, queries[1:], k, v, 2)
+    (local1,) = local_attention(next_kernel, info, queries[1:3], k, v)
+    (local2,) = local_attention(second_kernel, info, queries[3:], k, v, local1)
     local1 = send(local1, later1)
     local2 = send(local2, later2)
 

time: 112 us -> 105 us (0.938)
  waiting for transfers between devices: 31.5 us -> 17.3 us
  starting transfers between devices: 34.4 us -> 42.3 us
    ppermute x23, waiting for transfers between devices: 31.5 us -> 17.3 us  [send(): return lax.ppermute(array, ('seq', 'mem'), pairs)]
    ppermute x23, starting transfers between devices: 34.4 us -> 42.3 us  [send(): return lax.ppermute(array, ('seq', 'mem'), pairs)]
    pallas_call x2, Pallas kernels: 12.1 us -> 10.8 us  [memory_attention(): pl.pallas_call(functools.partial(memory_kernel, group), grid_spec=pltpu.P...]
    pallas_call x2 -> x3, Pallas kernels: 10.4 us -> 11 us  [local_attention(): pl.pallas_call(kernel, in_specs=scalars(1) + held_specs(len(queries) + 2)...]
  transfers between devices with their start and end apart: 23 -> 23, of which waited for: 11 -> 9; matrix products, arithmetic and copies ran while one was open for 1% -> 1% of each run, Pallas kernels for 35% -> 36%
where the time goes in v4:
time: 105 us
  Pallas kernels  42.5 us (40%)
  starting transfers between devices  42.3 us (40%)
  waiting for transfers between devices  17.3 us (16%)
  other arithmetic  1.32 us (1%)
  local copies, waits for them, and re-layouts  1.21 us (1%)
    ppermute x23, starting transfers between devices, send(): return lax.ppermute(array, ('seq', 'mem'), pairs)  42.3 us
    ppermute x23, waiting for transfers between devices, send(): return lax.ppermute(array, ('seq', 'mem'), pairs)  17.3 us
    pallas_call x3, Pallas kernels, local_attention(): pl.pallas_call(kernel, in_specs=scalars(1) + held_specs(len(queries) + 2)...  11 us
    pallas_call x2, Pallas kernels, memory_attention(): pl.pallas_call(functools.partial(memory_kernel, group), grid_spec=pltpu.P...  10.8 us
    pallas_call x1, Pallas kernels, project_keyvalue(): pl.pallas_call(keyvalue_kernel, grid_spec=pltpu.PrefetchScalarGridSpec(nu...  6.47 us
    pallas_call x1, Pallas kernels, project_query(): pl.pallas_call(query_kernel, grid_spec=pltpu.PrefetchScalarGridSpec(num_s...  4.74 us
    pallas_call x1, Pallas kernels, project_output(): pl.pallas_call(output_kernel, grid_spec=pltpu.PrefetchScalarGridSpec(num_...  2.77 us
    pallas_call x1, Pallas kernels, take_part(): pl.pallas_call(part_kernel, grid_spec=pltpu.PrefetchScalarGridSpec(num_sc...  2.63 us
  transfers between devices with their start and end apart: 23, of which 9 were waited for; matrix products, arithmetic and copies ran while one was open for 1% of the time, Pallas kernels for 36%

profile of v4, /device:TPU:1, one launch (start us, length us, event | category | flops | bytes accessed | tf_op | source)
XLA Modules:
  0.0 105.0 jit_solution(10427044480709124114)
XLA Ops:
  0.0 1.4 %collective-permute-start = (bf16[256,2048]{1,0:T(8,128)(2,1)}, bf16[256,2048]{1,0:T(8,128)(2,1)}, u32[]{:S(2)}, u32[]{:S(2)}) collective-permute-start(bf16[256,2048]{1,0:T(8,128)(2,1)} %bitcast.14), channel_id=1, source_target_pairs={{0,16},{16,0},{32,48},{48,32},{64,80},{80,64},{96,112},{112,96},{1... | collective-permute-start | bytes 3145736 | tf_op jit(solution)/shard_map/ppermute | solution.py:42
  2.0 2.6 %shard_map.82 = (bf16[1,2,2,2,2,128,128]{6,5,4,3,2,1,0:T(8,128)(2,1)}, f32[8,128]{1,0:T(8,128)}) custom-call(s32[4]{0:T(128)} %pad_add_fusion.info, bf16[8,2,128,1024]{3,2,1,0:T(8,128)(2,1)} %mem.1), custom_call_target="tpu_custom_call" | custom-call | bytes 1048576 | tf_op jit(solution)/shard_map/pallas_call | solution.py:259
  4.6 3.8 %collective-permute-start.7 = (bf16[1,2,2,2,2,128,128]{6,5,4,3,2,1,0:T(8,128)(2,1)}, bf16[1,2,2,2,2,128,128]{6,5,4,3,2,1,0:T(8,128)(2,1)S(1)}, u32[]{:S(2)}, u32[]{:S(2)}) collective-permute-start(bf16[1,2,2,2,2,128,128]{6,5,4,3,2,1,0:T(8,128)(2,1)} %get-tuple-element.36.refs_0_), channel_id=1, source_target_pairs={{0,8},{16,18},{32,40},{48,50},{64,72},{80,82},{96,104},{112,114},{... | collective-permute-start | bytes 1572872 | tf_op jit(solution)/shard_map/ppermute | solution.py:42
  11.7 4.7 %shard_map.83.refs_0_._.q = bf16[528,512]{1,0:T(8,128)(2,1)} custom-call(s32[4]{0:T(128)} %pad_add_fusion.info, bf16[256,2048]{1,0:T(8,128)(2,1)} %bitcast.15, bf16[256,2048]{1,0:T(8,128)(2,1)} %collective-permute-done.oth, bf16[2048,1024]{1,0:T(8,128)(2,1)} %w.2, bf16[16,512]{1,0:T(8,128)(2,1)} %fusion.5.ids, f32[8,128]{1,0:T(8,128)} %get-tuple-element.33._), custom_call_target="tpu_custom_call" | custom-call | flops 1073741824 | bytes 4194304 | tf_op jit(solution)/shard_map/pallas_call | solution.py:100
  16.5 2.7 %collective-permute-start.2 = (bf16[528,512]{1,0:T(8,128)(2,1)}, bf16[528,512]{1,0:T(8,128)(2,1)S(1)}, u32[]{:S(2)}, u32[]{:S(2)}) collective-permute-start(bf16[528,512]{1,0:T(8,128)(2,1)} %shard_map.83.refs_0_._.q), channel_id=1, source_target_pairs={{0,32},{16,112},{32,64},{48,16},{64,96},{80,48},{96,0},{112,80},{1... | collective-permute-start | bytes 1622024 | tf_op jit(solution)/shard_map/ppermute | solution.py:42
  19.2 2.6 %collective-permute-done.6.refs_2_ = bf16[1,2,2,2,2,128,128]{6,5,4,3,2,1,0:T(8,128)(2,1)S(1)} collective-permute-done((bf16[1,2,2,2,2,128,128]{6,5,4,3,2,1,0:T(8,128)(2,1)}, bf16[1,2,2,2,2,128,128]{6,5,4,3,2,1,0:T(8,128)(2,1)S(1)}, u32[]{:S(2)}, u32[]{:S(2)}) %collective-permute-start.6) | collective-permute-done | bytes 524320 | tf_op jit(solution)/shard_map/ppermute | solution.py:42
  22.0 1.3 %collective-permute-start.8 = (bf16[4,2,2,2,128,128]{5,4,3,2,1,0:T(8,128)(2,1)S(1)}, bf16[4,2,2,2,128,128]{5,4,3,2,1,0:T(8,128)(2,1)}, u32[]{:S(2)}, u32[]{:S(2)}) collective-permute-start(bf16[4,2,2,2,128,128]{5,4,3,2,1,0:T(8,128)(2,1)S(1)} %shard_map.85.refs_4_), channel_id=1, source_target_pairs={{0,1},{16,20},{32,33},{48,52},{64,65},{80,84},{96,97},{112,116},{1... | collective-permute-start | bytes 3145736 | tf_op jit(solution)/shard_map/ppermute | solution.py:42
  23.3 6.5 %shard_map.87 = (bf16[512,512]{1,0:T(8,128)(2,1)}, bf16[512,512]{1,0:T(8,128)(2,1)}) custom-call(s32[4]{0:T(128)} %pad_add_fusion.info, bf16[256,2048]{1,0:T(8,128)(2,1)} %bitcast.16, bf16[256,2048]{1,0:T(8,128)(2,1)} %collective-permute-done.oth, bf16[2048,1024]{1,0:T(8,128)(2,1)} %wk.1, bf16[2048,1024]{1,0:T(8,128)(2,1)} %wv.1, ...), custom_call_target="tpu_custom_call" | custom-call | flops 2147483648 | bytes 6291456 | tf_op jit(solution)/shard_map/pallas_call | solution.py:133
  31.0 1.5 %collective-permute-start.15 = (bf16[4,2,2,2,128,128]{5,4,3,2,1,0:T(8,128)(2,1)S(1)}, bf16[4,2,2,2,128,128]{5,4,3,2,1,0:T(8,128)(2,1)S(1)}, u32[]{:S(2)}, u32[]{:S(2)}) collective-permute-start(bf16[4,2,2,2,128,128]{5,4,3,2,1,0:T(8,128)(2,1)S(1)} %shard_map.88.refs_4_), channel_id=1, source_target_pairs={{0,3},{16,28},{32,35},{48,60},{64,67},{80,92},{96,99},{112,124},{1... | collective-permute-start | bytes 3145736 | tf_op jit(solution)/shard_map/ppermute | solution.py:42
  32.5 1.3 %collective-permute-start.3 = (bf16[528,512]{1,0:T(8,128)(2,1)S(1)}, bf16[528,512]{1,0:T(8,128)(2,1)S(1)}, u32[]{:S(2)}, u32[]{:S(2)}) collective-permute-start(bf16[528,512]{1,0:T(8,128)(2,1)S(1)} %copy-done), channel_id=1, source_target_pairs={{0,96},{16,48},{32,0},{48,80},{64,32},{80,112},{96,64},{112,16},{1... | collective-permute-start | bytes 1622024 | tf_op jit(solution)/shard_map/ppermute | solution.py:42
  33.8 1.3 %collective-permute-start.9 = (bf16[4,2,2,2,128,128]{5,4,3,2,1,0:T(8,128)(2,1)S(1)}, bf16[4,2,2,2,128,128]{5,4,3,2,1,0:T(8,128)(2,1)S(1)}, u32[]{:S(2)}, u32[]{:S(2)}) collective-permute-start(bf16[4,2,2,2,128,128]{5,4,3,2,1,0:T(8,128)(2,1)S(1)} %shard_map.85.refs_4_), channel_id=1, source_target_pairs={{0,3},{16,28},{32,35},{48,60},{64,67},{80,92},{96,99},{112,124},{1... | collective-permute-start | bytes 3145736 | tf_op jit(solution)/shard_map/ppermute | solution.py:42
  35.1 2.2 %collective-permute-done.8.refs_5_ = bf16[4,2,2,2,128,128]{5,4,3,2,1,0:T(8,128)(2,1)} collective-permute-done((bf16[4,2,2,2,128,128]{5,4,3,2,1,0:T(8,128)(2,1)S(1)}, bf16[4,2,2,2,128,128]{5,4,3,2,1,0:T(8,128)(2,1)}, u32[]{:S(2)}, u32[]{:S(2)}) %collective-permute-start.8) | collective-permute-done | bytes 1048608 | tf_op jit(solution)/shard_map/ppermute | solution.py:42
  37.3 2.7 %collective-permute-start.4 = (bf16[528,512]{1,0:T(8,128)(2,1)S(1)}, bf16[528,512]{1,0:T(8,128)(2,1)S(1)}, u32[]{:S(2)}, u32[]{:S(2)}) collective-permute-start(bf16[528,512]{1,0:T(8,128)(2,1)S(1)} %collective-permute-done.2.refs_1_.refs_4_.q1), channel_id=1, source_target_pairs={{0,32},{16,112},{32,64},{48,16},{64,96},{80,48},{96,0},{112,80},{1... | collective-permute-start | bytes 1622024 | tf_op jit(solution)/shard_map/ppermute | solution.py:42
  40.1 1.9 %collective-permute-done.3.refs_2_.q2 = bf16[528,512]{1,0:T(8,128)(2,1)S(1)} collective-permute-done((bf16[528,512]{1,0:T(8,128)(2,1)S(1)}, bf16[528,512]{1,0:T(8,128)(2,1)S(1)}, u32[]{:S(2)}, u32[]{:S(2)}) %collective-permute-start.3) | collective-permute-done | bytes 540704 | tf_op jit(solution)/shard_map/ppermute | solution.py:42
  42.0 3.7 %shard_map.91._ = bf16[528,512]{1,0:T(8,128)(2,1)S(1)} custom-call(s32[4]{0:T(128)S(1)} %copy-done.6, bf16[528,512]{1,0:T(8,128)(2,1)S(1)} %collective-permute-done.2.refs_1_.refs_4_.q1, bf16[528,512]{1,0:T(8,128)(2,1)S(1)} %collective-permute-done.3.refs_2_.q2, bf16[512,512]{1,0:T(8,128)(2,1)S(1)} %copy-done.2, bf16[512,512]{1,0:T(8,128)(2,1)S(1)} %copy-done.3), custom_call_target="tpu_custom_call" | custom-call | flops 536870912 | bytes 2097152 | tf_op jit(solution)/shard_map/pallas_call | solution.py:233
  45.8 2.7 %collective-permute-start.16 = (bf16[4,2,2,2,128,128]{5,4,3,2,1,0:T(8,128)(2,1)S(1)}, bf16[4,2,2,2,128,128]{5,4,3,2,1,0:T(8,128)(2,1)S(1)}, u32[]{:S(2)}, u32[]{:S(2)}) collective-permute-start(bf16[4,2,2,2,128,128]{5,4,3,2,1,0:T(8,128)(2,1)S(1)} %collective-permute-done.15.refs_6_), channel_id=1, source_target_pairs={{0,3},{16,28},{32,35},{48,60},{64,67},{80,92},{96,99},{112,124},{1... | collective-permute-start | bytes 3145736 | tf_op jit(solution)/shard_map/ppermute | solution.py:42
  48.7 2.7 %collective-permute-start.20 = (bf16[528,512]{1,0:T(8,128)(2,1)S(1)}, bf16[528,512]{1,0:T(8,128)(2,1)S(1)}, u32[]{:S(2)}, u32[]{:S(2)}) collective-permute-start(bf16[528,512]{1,0:T(8,128)(2,1)S(1)} %shard_map.91._), channel_id=1, source_target_pairs={{0,32},{16,48},{32,64},{48,80},{64,96},{80,112},{1,33},{17,49},{33... | collective-permute-start | bytes 1622024 | tf_op jit(solution)/shard_map/ppermute | solution.py:42
  51.4 3.9 %shard_map.92 = bf16[528,512]{1,0:T(8,128)(2,1)S(1)} custom-call(s32[4]{0:T(128)S(1)} %copy-done.6, bf16[528,512]{1,0:T(8,128)(2,1)S(1)} %collective-permute-done.4.refs_3_.q3, bf16[512,512]{1,0:T(8,128)(2,1)S(1)} %copy-done.2, bf16[512,512]{1,0:T(8,128)(2,1)S(1)} %copy-done.3, bf16[528,512]{1,0:T(8,128)(2,1)S(1)} %shard_map.91._), custom_call_target="tpu_custom_call" | custom-call | flops 536870912 | bytes 2097152 | tf_op jit(solution)/shard_map/pallas_call | solution.py:233
  56.2 4.8 %collective-permute-start.21 = (bf16[528,512]{1,0:T(8,128)(2,1)S(1)}, bf16[528,512]{1,0:T(8,128)(2,1)S(1)}, u32[]{:S(2)}, u32[]{:S(2)}) collective-permute-start(bf16[528,512]{1,0:T(8,128)(2,1)S(1)} %shard_map.92), channel_id=1, source_target_pairs={{0,64},{16,80},{32,96},{48,112},{1,65},{17,81},{33,97},{49,113},{2... | collective-permute-start | bytes 1622024 | tf_op jit(solution)/shard_map/ppermute | solution.py:42
  61.2 2.4 %shard_map.84 = (s32[144]{0:T(256)S(1)}, s32[80]{0:T(128)S(1)}) custom-call(s32[4]{0:T(128)S(1)} %copy-done.6, s32[128]{0:T(128)S(1)} %maximum_convert_fusion.ids), custom_call_target="tpu_custom_call" | custom-call | flops 1000 | bytes 1000 | tf_op jit(solution)/shard_map/pallas_call | solution.py:337
  63.6 5.8 %shard_map.86 = (bf16[272,512]{1,0:T(8,128)(2,1)S(1)}, bf16[272,512]{1,0:T(8,128)(2,1)S(1)}, bf16[272,512]{1,0:T(8,128)(2,1)S(1)}, bf16[272,512]{1,0:T(8,128)(2,1)S(1)}) custom-call(s32[144]{0:T(256)S(1)} %get-tuple-element.34.slots, s32[80]{0:T(128)S(1)} %get-tuple-element.35.blocks, bf16[528,512]{1,0:T(8,128)(2,1)S(1)} %copy-done, ...), custom_call_target="tpu_custom_call" | custom-call | flops 536870912 | bytes 6291456 | tf_op jit(solution)/shard_map/pallas_call | solution.py:426
  70.5 1.6 %collective-permute-start.12 = (bf16[272,512]{1,0:T(8,128)(2,1)S(1)}, bf16[272,512]{1,0:T(8,128)(2,1)S(1)}, u32[]{:S(2)}, u32[]{:S(2)}) collective-permute-start(bf16[272,512]{1,0:T(8,128)(2,1)S(1)} %get-tuple-element.39), channel_id=1, source_target_pairs={{0,32},{16,112},{32,64},{48,16},{64,96},{80,48},{96,0},{112,80},{1... | collective-permute-start | bytes 835592 | tf_op jit(solution)/shard_map/ppermute | solution.py:42
  72.4 5.0 %shard_map.89 = (bf16[272,512]{1,0:T(8,128)(2,1)S(1)}, bf16[272,512]{1,0:T(8,128)(2,1)S(1)}, bf16[272,512]{1,0:T(8,128)(2,1)S(1)}, bf16[272,512]{1,0:T(8,128)(2,1)S(1)}) custom-call(s32[144]{0:T(256)S(1)} %get-tuple-element.34.slots, s32[80]{0:T(128)S(1)} %get-tuple-element.35.blocks, bf16[528,512]{1,0:T(8,128)(2,1)S(1)} %copy-done, ...), custom_call_target="tpu_custom_call" | custom-call | flops 536870912 | bytes 6291456 | tf_op jit(solution)/shard_map/pallas_call | solution.py:426
  78.5 1.6 %collective-permute-start.18 = (bf16[272,512]{1,0:T(8,128)(2,1)S(1)}, bf16[272,512]{1,0:T(8,128)(2,1)S(1)}, u32[]{:S(2)}, u32[]{:S(2)}) collective-permute-start(bf16[272,512]{1,0:T(8,128)(2,1)S(1)} %get-tuple-element.44), channel_id=1, source_target_pairs={{0,32},{16,112},{32,64},{48,16},{64,96},{80,48},{96,0},{112,80},{1... | collective-permute-start | bytes 835592 | tf_op jit(solution)/shard_map/ppermute | solution.py:42
  80.2 6.5 %collective-permute-start.19 = (bf16[272,512]{1,0:T(8,128)(2,1)S(1)}, bf16[272,512]{1,0:T(8,128)(2,1)S(1)}, u32[]{:S(2)}, u32[]{:S(2)}) collective-permute-start(bf16[272,512]{1,0:T(8,128)(2,1)S(1)} %get-tuple-element.45), channel_id=1, source_target_pairs={{0,64},{16,80},{32,96},{48,112},{64,0},{80,16},{96,32},{112,48},{1... | collective-permute-start | bytes 835592 | tf_op jit(solution)/shard_map/ppermute | solution.py:42
  86.6 3.4 %shard_map.90.refs_8_ = bf16[528,512]{1,0:T(8,128)(2,1)S(1)} custom-call(s32[4]{0:T(128)S(1)} %copy-done.6, bf16[528,512]{1,0:T(8,128)(2,1)S(1)} %copy-done, bf16[512,512]{1,0:T(8,128)(2,1)S(1)} %copy-done.2, bf16[512,512]{1,0:T(8,128)(2,1)S(1)} %copy-done.3), custom_call_target="tpu_custom_call" | custom-call | flops 536870912 | bytes 2097152 | tf_op jit(solution)/shard_map/pallas_call | solution.py:233
  90.0 1.8 %collective-permute-done.17.refs_5_ = bf16[272,512]{1,0:T(8,128)(2,1)S(1)} collective-permute-done((bf16[272,512]{1,0:T(8,128)(2,1)S(1)}, bf16[272,512]{1,0:T(8,128)(2,1)S(1)}, u32[]{:S(2)}, u32[]{:S(2)}) %collective-permute-start.17) | collective-permute-done | bytes 278560 | tf_op jit(solution)/shard_map/ppermute | solution.py:42
  91.8 5.3 %collective-permute-done.19.refs_7_ = bf16[272,512]{1,0:T(8,128)(2,1)S(1)} collective-permute-done((bf16[272,512]{1,0:T(8,128)(2,1)S(1)}, bf16[272,512]{1,0:T(8,128)(2,1)S(1)}, u32[]{:S(2)}, u32[]{:S(2)}) %collective-permute-start.19) | collective-permute-done | bytes 278560 | tf_op jit(solution)/shard_map/ppermute | solution.py:42
  97.1 1.6 %shard_map.93 = (bf16[256,512]{1,0:T(8,128)(2,1)S(1)}, bf16[256,512]{1,0:T(8,128)(2,1)S(1)}) custom-call(s32[4]{0:T(128)S(1)} %copy-done.6, f32[8]{0:T(128)S(1)} %copy-done.7, bf16[272,512]{1,0:T(8,128)(2,1)S(1)} %get-tuple-element.37.refs_0_, bf16[272,512]{1,0:T(8,128)(2,1)S(1)} %collective-permute-done.11.refs_1_, ...), custom_call_target="tpu_custom_call" | custom-call | flops 5406720 | bytes 4325376 | tf_op jit(solution)/shard_map/pallas_call | solution.py:483
  98.7 2.3 %collective-permute-start.22 = (bf16[256,512]{1,0:T(8,128)(2,1)S(1)}, bf16[256,512]{1,0:T(8,128)(2,1)S(1)}, u32[]{:S(2)}, u32[]{:S(2)}) collective-permute-start(bf16[256,512]{1,0:T(8,128)(2,1)S(1)} %get-tuple-element.48), channel_id=1, source_target_pairs={{0,16},{16,0},{32,48},{48,32},{64,80},{80,64},{96,112},{112,96},{1... | collective-permute-start | bytes 786440 | tf_op jit(solution)/shard_map/ppermute | solution.py:42
  101.0 1.2 %collective-permute-done.22.oth = bf16[256,512]{1,0:T(8,128)(2,1)S(1)} collective-permute-done((bf16[256,512]{1,0:T(8,128)(2,1)S(1)}, bf16[256,512]{1,0:T(8,128)(2,1)S(1)}, u32[]{:S(2)}, u32[]{:S(2)}) %collective-permute-start.22) | collective-permute-done | bytes 262176 | tf_op jit(solution)/shard_map/ppermute | solution.py:42
  102.2 2.8 %shard_map.94 = bf16[256,2048]{1,0:T(8,128)(2,1)} custom-call(s32[4]{0:T(128)S(1)} %copy-done.6, bf16[256,512]{1,0:T(8,128)(2,1)S(1)} %get-tuple-element.47.own, bf16[256,512]{1,0:T(8,128)(2,1)S(1)} %collective-permute-done.22.oth, bf16[1024,2048]{1,0:T(8,128)(2,1)S(1)} %copy-done.4), custom_call_target="tpu_custom_call" | custom-call | flops 1073741824 | bytes 4194304 | tf_op jit(solution)/shard_map/pallas_call | solution.py:509
  (55 shorter events, 9.1 us)
Async XLA Ops:
  0.0 9.9 %copy-start.8 = (s32[1,2,8]{2,1,0:T(2,128)S(1)}, s32[1,2,8]{2,1,0:T(2,128)}, u32[]{:S(2)}) copy-start(s32[1,2,8]{2,1,0:T(2,128)} %param.11) | copy-start | bytes 196
  0.0 11.7 %collective-permute-start = (bf16[256,2048]{1,0:T(8,128)(2,1)}, bf16[256,2048]{1,0:T(8,128)(2,1)}, u32[]{:S(2)}, u32[]{:S(2)}) collective-permute-start(bf16[256,2048]{1,0:T(8,128)(2,1)} %bitcast.14), channel_id=1, source_target_pairs={{0,16},{16,0},{32,48},{48,32},{64,80},{80,64},{96,112},{112,96},{1... | collective-permute-start | bytes 3145736 | tf_op jit(solution)/shard_map/ppermute | solution.py:42
  4.6 17.2 %copy-start.5 = (bf16[1,2,2,2,2,128,128]{6,5,4,3,2,1,0:T(8,128)(2,1)S(1)}, bf16[1,2,2,2,2,128,128]{6,5,4,3,2,1,0:T(8,128)(2,1)}, u32[]{:S(2)}) copy-start(bf16[1,2,2,2,2,128,128]{6,5,4,3,2,1,0:T(8,128)(2,1)} %get-tuple-element.36.refs_0_) | copy-start | bytes 1572868
  4.6 14.6 %collective-permute-start.7 = (bf16[1,2,2,2,2,128,128]{6,5,4,3,2,1,0:T(8,128)(2,1)}, bf16[1,2,2,2,2,128,128]{6,5,4,3,2,1,0:T(8,128)(2,1)S(1)}, u32[]{:S(2)}, u32[]{:S(2)}) collective-permute-start(bf16[1,2,2,2,2,128,128]{6,5,4,3,2,1,0:T(8,128)(2,1)} %get-tuple-element.36.refs_0_), channel_id=1, source_target_pairs={{0,8},{16,18},{32,40},{48,50},{64,72},{80,82},{96,104},{112,114},{... | collective-permute-start | bytes 1572872 | tf_op jit(solution)/shard_map/ppermute | solution.py:42
  8.4 13.5 %collective-permute-start.6 = (bf16[1,2,2,2,2,128,128]{6,5,4,3,2,1,0:T(8,128)(2,1)}, bf16[1,2,2,2,2,128,128]{6,5,4,3,2,1,0:T(8,128)(2,1)S(1)}, u32[]{:S(2)}, u32[]{:S(2)}) collective-permute-start(bf16[1,2,2,2,2,128,128]{6,5,4,3,2,1,0:T(8,128)(2,1)} %get-tuple-element.36.refs_0_), channel_id=1, source_target_pairs={{0,12},{16,19},{32,44},{48,51},{64,76},{80,83},{96,108},{112,115},... | collective-permute-start | bytes 1572872 | tf_op jit(solution)/shard_map/ppermute | solution.py:42
  8.8 13.0 %collective-permute-start.5 = (bf16[1,2,2,2,2,128,128]{6,5,4,3,2,1,0:T(8,128)(2,1)}, bf16[1,2,2,2,2,128,128]{6,5,4,3,2,1,0:T(8,128)(2,1)S(1)}, u32[]{:S(2)}, u32[]{:S(2)}) collective-permute-start(bf16[1,2,2,2,2,128,128]{6,5,4,3,2,1,0:T(8,128)(2,1)} %get-tuple-element.36.refs_0_), channel_id=1, source_target_pairs={{0,4},{16,17},{32,36},{48,49},{64,68},{80,81},{96,100},{112,113},{... | collective-permute-start | bytes 1572872 | tf_op jit(solution)/shard_map/ppermute | solution.py:42
  9.9 1.1 %collective-permute-start.1 = (s32[1,16]{1,0:T(1,128)S(1)}, s32[1,16]{1,0:T(1,128)S(1)}, u32[]{:S(2)}, u32[]{:S(2)}) collective-permute-start(s32[1,16]{1,0:T(1,128)S(1)} %concatenate.19), channel_id=1, source_target_pairs={{0,16},{16,0},{32,48},{48,32},{64,80},{80,64},{96,112},{112,96},{1... | collective-permute-start | bytes 200 | tf_op jit(solution)/shard_map/ppermute | solution.py:42
  16.5 13.2 %collective-permute-start.2 = (bf16[528,512]{1,0:T(8,128)(2,1)}, bf16[528,512]{1,0:T(8,128)(2,1)S(1)}, u32[]{:S(2)}, u32[]{:S(2)}) collective-permute-start(bf16[528,512]{1,0:T(8,128)(2,1)} %shard_map.83.refs_0_._.q), channel_id=1, source_target_pairs={{0,32},{16,112},{32,64},{48,16},{64,96},{80,48},{96,0},{112,80},{1... | collective-permute-start | bytes 1622024 | tf_op jit(solution)/shard_map/ppermute | solution.py:42
  22.0 15.3 %collective-permute-start.8 = (bf16[4,2,2,2,128,128]{5,4,3,2,1,0:T(8,128)(2,1)S(1)}, bf16[4,2,2,2,128,128]{5,4,3,2,1,0:T(8,128)(2,1)}, u32[]{:S(2)}, u32[]{:S(2)}) collective-permute-start(bf16[4,2,2,2,128,128]{5,4,3,2,1,0:T(8,128)(2,1)S(1)} %shard_map.85.refs_4_), channel_id=1, source_target_pairs={{0,1},{16,20},{32,33},{48,52},{64,65},{80,84},{96,97},{112,116},{1... | collective-permute-start | bytes 3145736 | tf_op jit(solution)/shard_map/ppermute | solution.py:42
  23.3 18.7 %copy-start.6 = (s32[4]{0:T(128)S(1)}, s32[4]{0:T(128)}, u32[]{:S(2)}) copy-start(s32[4]{0:T(128)} %pad_add_fusion.info) | copy-start | bytes 52
  29.7 2.8 %copy-start = (bf16[528,512]{1,0:T(8,128)(2,1)S(1)}, bf16[528,512]{1,0:T(8,128)(2,1)}, u32[]{:S(2)}) copy-start(bf16[528,512]{1,0:T(8,128)(2,1)} %shard_map.83.refs_0_._.q) | copy-start | bytes 1622020
  29.7 1.1 %copy-start.1 = (bf16[512,512]{1,0:T(8,128)(2,1)S(1)}, bf16[512,512]{1,0:T(8,128)(2,1)}, u32[]{:S(2)}) copy-start(bf16[512,512]{1,0:T(8,128)(2,1)} %get-tuple-element.41.refs_5_.k) | copy-start | bytes 1572868
  30.8 11.1 %copy-start.2 = (bf16[512,512]{1,0:T(8,128)(2,1)S(1)}, bf16[512,512]{1,0:T(8,128)(2,1)}, u32[]{:S(2)}) copy-start(bf16[512,512]{1,0:T(8,128)(2,1)} %get-tuple-element.41.refs_5_.k) | copy-start | bytes 1572868
  30.8 11.2 %copy-start.3 = (bf16[512,512]{1,0:T(8,128)(2,1)S(1)}, bf16[512,512]{1,0:T(8,128)(2,1)}, u32[]{:S(2)}) copy-start(bf16[512,512]{1,0:T(8,128)(2,1)} %get-tuple-element.46.v) | copy-start | bytes 1572868
  31.0 14.8 %collective-permute-start.15 = (bf16[4,2,2,2,128,128]{5,4,3,2,1,0:T(8,128)(2,1)S(1)}, bf16[4,2,2,2,128,128]{5,4,3,2,1,0:T(8,128)(2,1)S(1)}, u32[]{:S(2)}, u32[]{:S(2)}) collective-permute-start(bf16[4,2,2,2,128,128]{5,4,3,2,1,0:T(8,128)(2,1)S(1)} %shard_map.88.refs_4_), channel_id=1, source_target_pairs={{0,3},{16,28},{32,35},{48,60},{64,67},{80,92},{96,99},{112,124},{1... | collective-permute-start | bytes 3145736 | tf_op jit(solution)/shard_map/ppermute | solution.py:42
  32.5 9.5 %collective-permute-start.3 = (bf16[528,512]{1,0:T(8,128)(2,1)S(1)}, bf16[528,512]{1,0:T(8,128)(2,1)S(1)}, u32[]{:S(2)}, u32[]{:S(2)}) collective-permute-start(bf16[528,512]{1,0:T(8,128)(2,1)S(1)} %copy-done), channel_id=1, source_target_pairs={{0,96},{16,48},{32,0},{48,80},{64,32},{80,112},{96,64},{112,16},{1... | collective-permute-start | bytes 1622024 | tf_op jit(solution)/shard_map/ppermute | solution.py:42
  33.8 22.4 %collective-permute-start.9 = (bf16[4,2,2,2,128,128]{5,4,3,2,1,0:T(8,128)(2,1)S(1)}, bf16[4,2,2,2,128,128]{5,4,3,2,1,0:T(8,128)(2,1)S(1)}, u32[]{:S(2)}, u32[]{:S(2)}) collective-permute-start(bf16[4,2,2,2,128,128]{5,4,3,2,1,0:T(8,128)(2,1)S(1)} %shard_map.85.refs_4_), channel_id=1, source_target_pairs={{0,3},{16,28},{32,35},{48,60},{64,67},{80,92},{96,99},{112,124},{1... | collective-permute-start | bytes 3145736 | tf_op jit(solution)/shard_map/ppermute | solution.py:42
  37.3 26.2 %collective-permute-start.10 = (bf16[4,2,2,2,128,128]{5,4,3,2,1,0:T(8,128)(2,1)}, bf16[4,2,2,2,128,128]{5,4,3,2,1,0:T(8,128)(2,1)S(1)}, u32[]{:S(2)}, u32[]{:S(2)}) collective-permute-start(bf16[4,2,2,2,128,128]{5,4,3,2,1,0:T(8,128)(2,1)} %collective-permute-done.8.refs_5_), channel_id=1, source_target_pairs={{0,1},{16,20},{32,33},{48,52},{64,65},{80,84},{96,97},{112,116},{1... | collective-permute-start | bytes 3145736 | tf_op jit(solution)/shard_map/ppermute | solution.py:42
  37.3 11.4 %collective-permute-start.4 = (bf16[528,512]{1,0:T(8,128)(2,1)S(1)}, bf16[528,512]{1,0:T(8,128)(2,1)S(1)}, u32[]{:S(2)}, u32[]{:S(2)}) collective-permute-start(bf16[528,512]{1,0:T(8,128)(2,1)S(1)} %collective-permute-done.2.refs_1_.refs_4_.q1), channel_id=1, source_target_pairs={{0,32},{16,112},{32,64},{48,16},{64,96},{80,48},{96,0},{112,80},{1... | collective-permute-start | bytes 1622024 | tf_op jit(solution)/shard_map/ppermute | solution.py:42
  42.0 28.5 %collective-permute-start.14 = (bf16[4,2,2,2,128,128]{5,4,3,2,1,0:T(8,128)(2,1)S(1)}, bf16[4,2,2,2,128,128]{5,4,3,2,1,0:T(8,128)(2,1)S(1)}, u32[]{:S(2)}, u32[]{:S(2)}) collective-permute-start(bf16[4,2,2,2,128,128]{5,4,3,2,1,0:T(8,128)(2,1)S(1)} %shard_map.88.refs_4_), channel_id=1, source_target_pairs={{0,1},{16,20},{32,33},{48,52},{64,65},{80,84},{96,97},{112,116},{1... | collective-permute-start | bytes 3145736 | tf_op jit(solution)/shard_map/ppermute | solution.py:42
  45.8 26.3 %collective-permute-start.16 = (bf16[4,2,2,2,128,128]{5,4,3,2,1,0:T(8,128)(2,1)S(1)}, bf16[4,2,2,2,128,128]{5,4,3,2,1,0:T(8,128)(2,1)S(1)}, u32[]{:S(2)}, u32[]{:S(2)}) collective-permute-start(bf16[4,2,2,2,128,128]{5,4,3,2,1,0:T(8,128)(2,1)S(1)} %collective-permute-done.15.refs_6_), channel_id=1, source_target_pairs={{0,3},{16,28},{32,35},{48,60},{64,67},{80,92},{96,99},{112,124},{1... | collective-permute-start | bytes 3145736 | tf_op jit(solution)/shard_map/ppermute | solution.py:42
  48.7 28.7 %collective-permute-start.20 = (bf16[528,512]{1,0:T(8,128)(2,1)S(1)}, bf16[528,512]{1,0:T(8,128)(2,1)S(1)}, u32[]{:S(2)}, u32[]{:S(2)}) collective-permute-start(bf16[528,512]{1,0:T(8,128)(2,1)S(1)} %shard_map.91._), channel_id=1, source_target_pairs={{0,32},{16,48},{32,64},{48,80},{64,96},{80,112},{1,33},{17,49},{33... | collective-permute-start | bytes 1622024 | tf_op jit(solution)/shard_map/ppermute | solution.py:42
  56.2 22.3 %collective-permute-start.21 = (bf16[528,512]{1,0:T(8,128)(2,1)S(1)}, bf16[528,512]{1,0:T(8,128)(2,1)S(1)}, u32[]{:S(2)}, u32[]{:S(2)}) collective-permute-start(bf16[528,512]{1,0:T(8,128)(2,1)S(1)} %shard_map.92), channel_id=1, source_target_pairs={{0,64},{16,80},{32,96},{48,112},{1,65},{17,81},{33,97},{49,113},{2... | collective-permute-start | bytes 1622024 | tf_op jit(solution)/shard_map/ppermute | solution.py:42
  69.3 10.8 %collective-permute-start.11 = (bf16[272,512]{1,0:T(8,128)(2,1)S(1)}, bf16[272,512]{1,0:T(8,128)(2,1)S(1)}, u32[]{:S(2)}, u32[]{:S(2)}) collective-permute-start(bf16[272,512]{1,0:T(8,128)(2,1)S(1)} %get-tuple-element.38), channel_id=1, source_target_pairs={{0,96},{16,48},{32,0},{48,80},{64,32},{80,112},{96,64},{112,16},{1... | collective-permute-start | bytes 835592 | tf_op jit(solution)/shard_map/ppermute | solution.py:42
  70.5 19.5 %collective-permute-start.12 = (bf16[272,512]{1,0:T(8,128)(2,1)S(1)}, bf16[272,512]{1,0:T(8,128)(2,1)S(1)}, u32[]{:S(2)}, u32[]{:S(2)}) collective-permute-start(bf16[272,512]{1,0:T(8,128)(2,1)S(1)} %get-tuple-element.39), channel_id=1, source_target_pairs={{0,32},{16,112},{32,64},{48,16},{64,96},{80,48},{96,0},{112,80},{1... | collective-permute-start | bytes 835592 | tf_op jit(solution)/shard_map/ppermute | solution.py:42
  72.1 25.0 %copy-start.7 = (f32[8]{0:T(128)S(1)}, f32[8]{0:T(128)}, u32[]{:S(2)}) copy-start(f32[8]{0:T(128)} %gate.1) | copy-start | bytes 100
  72.1 17.9 %collective-permute-start.13 = (bf16[272,512]{1,0:T(8,128)(2,1)S(1)}, bf16[272,512]{1,0:T(8,128)(2,1)S(1)}, u32[]{:S(2)}, u32[]{:S(2)}) collective-permute-start(bf16[272,512]{1,0:T(8,128)(2,1)S(1)} %get-tuple-element.40), channel_id=1, source_target_pairs={{0,64},{16,80},{32,96},{48,112},{64,0},{80,16},{96,32},{112,48},{1... | collective-permute-start | bytes 835592 | tf_op jit(solution)/shard_map/ppermute | solution.py:42
  77.4 24.8 %copy-start.4 = (bf16[1024,2048]{1,0:T(8,128)(2,1)S(1)}, bf16[1024,2048]{1,0:T(8,128)(2,1)}, u32[]{:S(2)}) copy-start(bf16[1024,2048]{1,0:T(8,128)(2,1)} %w.3) | copy-start | bytes 12582916
  77.4 14.4 %collective-permute-start.17 = (bf16[272,512]{1,0:T(8,128)(2,1)S(1)}, bf16[272,512]{1,0:T(8,128)(2,1)S(1)}, u32[]{:S(2)}, u32[]{:S(2)}) collective-permute-start(bf16[272,512]{1,0:T(8,128)(2,1)S(1)} %get-tuple-element.43), channel_id=1, source_target_pairs={{0,96},{16,48},{32,0},{48,80},{64,32},{80,112},{96,64},{112,16},{1... | collective-permute-start | bytes 835592 | tf_op jit(solution)/shard_map/ppermute | solution.py:42
  78.5 13.3 %collective-permute-start.18 = (bf16[272,512]{1,0:T(8,128)(2,1)S(1)}, bf16[272,512]{1,0:T(8,128)(2,1)S(1)}, u32[]{:S(2)}, u32[]{:S(2)}) collective-permute-start(bf16[272,512]{1,0:T(8,128)(2,1)S(1)} %get-tuple-element.44), channel_id=1, source_target_pairs={{0,32},{16,112},{32,64},{48,16},{64,96},{80,48},{96,0},{112,80},{1... | collective-permute-start | bytes 835592 | tf_op jit(solution)/shard_map/ppermute | solution.py:42
  80.2 17.0 %collective-permute-start.19 = (bf16[272,512]{1,0:T(8,128)(2,1)S(1)}, bf16[272,512]{1,0:T(8,128)(2,1)S(1)}, u32[]{:S(2)}, u32[]{:S(2)}) collective-permute-start(bf16[272,512]{1,0:T(8,128)(2,1)S(1)} %get-tuple-element.45), channel_id=1, source_target_pairs={{0,64},{16,80},{32,96},{48,112},{64,0},{80,16},{96,32},{112,48},{1... | collective-permute-start | bytes 835592 | tf_op jit(solution)/shard_map/ppermute | solution.py:42
  98.7 3.5 %collective-permute-start.22 = (bf16[256,512]{1,0:T(8,128)(2,1)S(1)}, bf16[256,512]{1,0:T(8,128)(2,1)S(1)}, u32[]{:S(2)}, u32[]{:S(2)}) collective-permute-start(bf16[256,512]{1,0:T(8,128)(2,1)S(1)} %get-tuple-element.48), channel_id=1, source_target_pairs={{0,16},{16,0},{32,48},{48,32},{64,80},{80,64},{96,112},{112,96},{1... | collective-permute-start | bytes 786440 | tf_op jit(solution)/shard_map/ppermute | solution.py:42

commit v5 on v4

--- a/solution.py
+++ b/solution.py
@@ -305,21 +305,23 @@
     )(*near, *earlier)
 
 
+def codes(info, ids):
+    x, y, z, c = info[0], info[1], info[2], info[3]
+    ax = (120 >> ((((ids >> 5) - x) & 3) * 2)) & 3
+    az = (120 >> (((((ids >> 3) & 3) - z) & 3) * 2)) & 3
+    slot = jnp.where(c == 0, az * 4 + ax, ax * 4 + az)
+    mine = ((ids >> 1) & 3) == y
+    return slot * 2 + (ids & 1) + 256 * mine.astype(jnp.int32)
+
+
 def plan_kernel(info, ids, slots, blocks):
-    x, y, z, c = info[0], info[1], info[2], info[3]
-    order = 120
-    shift_x = jnp.where(c == 0, 0, 2)
-
     def look(n, used):
         count = used
         for t in range(8):
-            ident = ids[n * 8 + t]
-            ax = (order >> ((((ident >> 5) - x) & 3) * 2)) & 3
-            az = (order >> (((((ident >> 3) & 3) - z) & 3) * 2)) & 3
-            slot = (ax << shift_x) + (az << (2 - shift_x))
-            slots[count] = slot * 2 + (ident & 1)
+            code = ids[n * 8 + t]
+            slots[count] = code & 255
             blocks[count >> 1] = n
-            count = count + (((ident >> 1) & 3) == y).astype(jnp.int32)
+            count = count + (code >> 8)
         slots[count] = 32
         return count + (count & 1)
 
@@ -553,7 +555,7 @@
 
     (local0,) = local_attention(same_kernel, info, [query], k, v)
     ids = jnp.concatenate([q[CHIP, 0:32] for q in queries]).astype(jnp.int32)
-    plan = plan_units(info, ids)
+    plan = plan_units(info, codes(info, ids))
     (local1,) = local_attention(next_kernel, info, queries[1:3], k, v)
     (local2,) = local_attention(second_kernel, info, queries[3:], k, v, local1)
     local1 = send(local1, later1)

time: 105 us -> 112 us (1.067); the launches traced: 105 us -> 111 us
  Pallas kernels: 42.5 us -> 46.5 us
  local copies, waits for them, and re-layouts: 1.21 us -> 3.3 us
    pallas_call x2, Pallas kernels: 10.8 us -> 13.7 us  [memory_attention(): pl.pallas_call(functools.partial(memory_kernel, group), grid_spec=pltpu.P...]
    unnamed x18 -> x26, local copies, waits for them, and re-layouts: 1.13 us -> 3.22 us
    pallas_call x2, Pallas kernels: 0.23 us -> 2.02 us  [join(): pl.pallas_call(functools.partial(join_kernel, group), in_specs=any_specs(...]
  transfers between devices with their start and end apart: 23 -> 23, of which waited for: 9 -> 8; matrix products, arithmetic and copies ran while one was open for 1% -> 1% of each run, Pallas kernels for 36% -> 38%
where the time goes in v5:
time: 112 us; the launch traced here: 111 us
  Pallas kernels  46.5 us (42%)
  starting transfers between devices  42.7 us (38%)
  waiting for transfers between devices  16.5 us (15%)
  local copies, waits for them, and re-layouts  3.3 us (3%)
  other arithmetic  1.38 us (1%)
    ppermute x23, starting transfers between devices, send(): return lax.ppermute(array, ('seq', 'mem'), pairs)  42.7 us
    ppermute x23, waiting for transfers between devices, send(): return lax.ppermute(array, ('seq', 'mem'), pairs)  16.5 us
    pallas_call x2, Pallas kernels, memory_attention(): pl.pallas_call(functools.partial(memory_kernel, group), grid_spec=pltpu.P...  13.7 us
    pallas_call x3, Pallas kernels, local_attention(): pl.pallas_call(kernel, in_specs=scalars(1) + held_specs(len(queries) + 2)...  11 us
    pallas_call x1, Pallas kernels, project_keyvalue(): pl.pallas_call(keyvalue_kernel, grid_spec=pltpu.PrefetchScalarGridSpec(nu...  6.43 us
    pallas_call x1, Pallas kernels, project_query(): pl.pallas_call(query_kernel, grid_spec=pltpu.PrefetchScalarGridSpec(num_s...  4.76 us
    unnamed x26, local copies, waits for them, and re-layouts  3.22 us
    pallas_call x1, Pallas kernels, project_output(): pl.pallas_call(output_kernel, grid_spec=pltpu.PrefetchScalarGridSpec(num_...  2.77 us
  transfers between devices with their start and end apart: 23, of which 8 were waited for; matrix products, arithmetic and copies ran while one was open for 1% of the time, Pallas kernels for 38%

profile of v5, /device:TPU:1, one launch (start us, length us, event | category | flops | bytes accessed | tf_op | source)
XLA Modules:
  0.0 110.6 jit_solution(14008040562833045382)
XLA Ops:
  0.0 1.4 %collective-permute-start = (bf16[256,2048]{1,0:T(8,128)(2,1)}, bf16[256,2048]{1,0:T(8,128)(2,1)}, u32[]{:S(2)}, u32[]{:S(2)}) collective-permute-start(bf16[256,2048]{1,0:T(8,128)(2,1)} %bitcast.14), channel_id=1, source_target_pairs={{0,16},{16,0},{32,48},{48,32},{64,80},{80,64},{96,112},{112,96},{1... | collective-permute-start | bytes 3145736 | tf_op jit(solution)/shard_map/ppermute | solution.py:42
  2.0 2.6 %shard_map.82 = (bf16[1,2,2,2,2,128,128]{6,5,4,3,2,1,0:T(8,128)(2,1)}, f32[8,128]{1,0:T(8,128)}) custom-call(s32[4]{0:T(128)} %pad_add_fusion.info, bf16[8,2,128,1024]{3,2,1,0:T(8,128)(2,1)} %mem.1), custom_call_target="tpu_custom_call" | custom-call | bytes 1048576 | tf_op jit(solution)/shard_map/pallas_call | solution.py:259
  4.7 1.8 %collective-permute-start.5 = (bf16[1,2,2,2,2,128,128]{6,5,4,3,2,1,0:T(8,128)(2,1)}, bf16[1,2,2,2,2,128,128]{6,5,4,3,2,1,0:T(8,128)(2,1)S(1)}, u32[]{:S(2)}, u32[]{:S(2)}) collective-permute-start(bf16[1,2,2,2,2,128,128]{6,5,4,3,2,1,0:T(8,128)(2,1)} %get-tuple-element.36.refs_0_), channel_id=1, source_target_pairs={{0,4},{16,17},{32,36},{48,49},{64,68},{80,81},{96,100},{112,113},{... | collective-permute-start | bytes 1572872 | tf_op jit(solution)/shard_map/ppermute | solution.py:42
  6.5 2.2 %collective-permute-start.6 = (bf16[1,2,2,2,2,128,128]{6,5,4,3,2,1,0:T(8,128)(2,1)}, bf16[1,2,2,2,2,128,128]{6,5,4,3,2,1,0:T(8,128)(2,1)S(1)}, u32[]{:S(2)}, u32[]{:S(2)}) collective-permute-start(bf16[1,2,2,2,2,128,128]{6,5,4,3,2,1,0:T(8,128)(2,1)} %get-tuple-element.36.refs_0_), channel_id=1, source_target_pairs={{0,12},{16,19},{32,44},{48,51},{64,76},{80,83},{96,108},{112,115},... | collective-permute-start | bytes 1572872 | tf_op jit(solution)/shard_map/ppermute | solution.py:42
  8.7 1.2 %collective-permute-start.7 = (bf16[1,2,2,2,2,128,128]{6,5,4,3,2,1,0:T(8,128)(2,1)}, bf16[1,2,2,2,2,128,128]{6,5,4,3,2,1,0:T(8,128)(2,1)S(1)}, u32[]{:S(2)}, u32[]{:S(2)}) collective-permute-start(bf16[1,2,2,2,2,128,128]{6,5,4,3,2,1,0:T(8,128)(2,1)} %get-tuple-element.36.refs_0_), channel_id=1, source_target_pairs={{0,8},{16,18},{32,40},{48,50},{64,72},{80,82},{96,104},{112,114},{... | collective-permute-start | bytes 1572872 | tf_op jit(solution)/shard_map/ppermute | solution.py:42
  11.8 4.8 %shard_map.83.refs_0_._.q = bf16[528,512]{1,0:T(8,128)(2,1)} custom-call(s32[4]{0:T(128)} %pad_add_fusion.info, bf16[256,2048]{1,0:T(8,128)(2,1)} %bitcast.15, bf16[256,2048]{1,0:T(8,128)(2,1)} %collective-permute-done.oth, bf16[2048,1024]{1,0:T(8,128)(2,1)} %w.2, bf16[16,512]{1,0:T(8,128)(2,1)} %fusion.5.ids, f32[8,128]{1,0:T(8,128)} %get-tuple-element.33._), custom_call_target="tpu_custom_call" | custom-call | flops 1073741824 | bytes 4194304 | tf_op jit(solution)/shard_map/pallas_call | solution.py:100
  16.6 2.7 %collective-permute-start.2 = (bf16[528,512]{1,0:T(8,128)(2,1)}, bf16[528,512]{1,0:T(8,128)(2,1)S(1)}, u32[]{:S(2)}, u32[]{:S(2)}) collective-permute-start(bf16[528,512]{1,0:T(8,128)(2,1)} %shard_map.83.refs_0_._.q), channel_id=1, source_target_pairs={{0,32},{16,112},{32,64},{48,16},{64,96},{80,48},{96,0},{112,80},{1... | collective-permute-start | bytes 1622024 | tf_op jit(solution)/shard_map/ppermute | solution.py:42
  19.3 1.5 %collective-permute-done.6.refs_2_ = bf16[1,2,2,2,2,128,128]{6,5,4,3,2,1,0:T(8,128)(2,1)S(1)} collective-permute-done((bf16[1,2,2,2,2,128,128]{6,5,4,3,2,1,0:T(8,128)(2,1)}, bf16[1,2,2,2,2,128,128]{6,5,4,3,2,1,0:T(8,128)(2,1)S(1)}, u32[]{:S(2)}, u32[]{:S(2)}) %collective-permute-start.6) | collective-permute-done | bytes 524320 | tf_op jit(solution)/shard_map/ppermute | solution.py:42
  20.8 1.4 %collective-permute-done.7.refs_3_ = bf16[1,2,2,2,2,128,128]{6,5,4,3,2,1,0:T(8,128)(2,1)S(1)} collective-permute-done((bf16[1,2,2,2,2,128,128]{6,5,4,3,2,1,0:T(8,128)(2,1)}, bf16[1,2,2,2,2,128,128]{6,5,4,3,2,1,0:T(8,128)(2,1)S(1)}, u32[]{:S(2)}, u32[]{:S(2)}) %collective-permute-start.7) | collective-permute-done | bytes 524320 | tf_op jit(solution)/shard_map/ppermute | solution.py:42
  23.2 1.3 %collective-permute-start.8 = (bf16[4,2,2,2,128,128]{5,4,3,2,1,0:T(8,128)(2,1)}, bf16[4,2,2,2,128,128]{5,4,3,2,1,0:T(8,128)(2,1)}, u32[]{:S(2)}, u32[]{:S(2)}) collective-permute-start(bf16[4,2,2,2,128,128]{5,4,3,2,1,0:T(8,128)(2,1)} %shard_map.85.refs_4_), channel_id=1, source_target_pairs={{0,1},{16,20},{32,33},{48,52},{64,65},{80,84},{96,97},{112,116},{1... | collective-permute-start | bytes 3145736 | tf_op jit(solution)/shard_map/ppermute | solution.py:42
  24.5 6.4 %shard_map.87 = (bf16[512,512]{1,0:T(8,128)(2,1)}, bf16[512,512]{1,0:T(8,128)(2,1)}) custom-call(s32[4]{0:T(128)} %pad_add_fusion.info, bf16[256,2048]{1,0:T(8,128)(2,1)} %bitcast.16, bf16[256,2048]{1,0:T(8,128)(2,1)} %collective-permute-done.oth, bf16[2048,1024]{1,0:T(8,128)(2,1)} %wk.1, bf16[2048,1024]{1,0:T(8,128)(2,1)} %wv.1, ...), custom_call_target="tpu_custom_call" | custom-call | flops 2147483648 | bytes 6291456 | tf_op jit(solution)/shard_map/pallas_call | solution.py:133
  35.1 1.5 %collective-permute-start.15 = (bf16[4,2,2,2,128,128]{5,4,3,2,1,0:T(8,128)(2,1)}, bf16[4,2,2,2,128,128]{5,4,3,2,1,0:T(8,128)(2,1)}, u32[]{:S(2)}, u32[]{:S(2)}) collective-permute-start(bf16[4,2,2,2,128,128]{5,4,3,2,1,0:T(8,128)(2,1)} %shard_map.88.refs_4_), channel_id=1, source_target_pairs={{0,3},{16,28},{32,35},{48,60},{64,67},{80,92},{96,99},{112,124},{1... | collective-permute-start | bytes 3145736 | tf_op jit(solution)/shard_map/ppermute | solution.py:42
  36.7 1.3 %collective-permute-start.3 = (bf16[528,512]{1,0:T(8,128)(2,1)S(1)}, bf16[528,512]{1,0:T(8,128)(2,1)S(1)}, u32[]{:S(2)}, u32[]{:S(2)}) collective-permute-start(bf16[528,512]{1,0:T(8,128)(2,1)S(1)} %copy-done), channel_id=1, source_target_pairs={{0,96},{16,48},{32,0},{48,80},{64,32},{80,112},{96,64},{112,16},{1... | collective-permute-start | bytes 1622024 | tf_op jit(solution)/shard_map/ppermute | solution.py:42
  38.0 1.3 %collective-permute-start.9 = (bf16[4,2,2,2,128,128]{5,4,3,2,1,0:T(8,128)(2,1)}, bf16[4,2,2,2,128,128]{5,4,3,2,1,0:T(8,128)(2,1)}, u32[]{:S(2)}, u32[]{:S(2)}) collective-permute-start(bf16[4,2,2,2,128,128]{5,4,3,2,1,0:T(8,128)(2,1)} %shard_map.85.refs_4_), channel_id=1, source_target_pairs={{0,3},{16,28},{32,35},{48,60},{64,67},{80,92},{96,99},{112,124},{1... | collective-permute-start | bytes 3145736 | tf_op jit(solution)/shard_map/ppermute | solution.py:42
  39.4 2.0 %collective-permute-start.4 = (bf16[528,512]{1,0:T(8,128)(2,1)S(1)}, bf16[528,512]{1,0:T(8,128)(2,1)S(1)}, u32[]{:S(2)}, u32[]{:S(2)}) collective-permute-start(bf16[528,512]{1,0:T(8,128)(2,1)S(1)} %collective-permute-done.2.refs_1_.refs_4_.q1), channel_id=1, source_target_pairs={{0,32},{16,112},{32,64},{48,16},{64,96},{80,48},{96,0},{112,80},{1... | collective-permute-start | bytes 1622024 | tf_op jit(solution)/shard_map/ppermute | solution.py:42
  41.5 4.7 %collective-permute-done.3.refs_2_.q2 = bf16[528,512]{1,0:T(8,128)(2,1)S(1)} collective-permute-done((bf16[528,512]{1,0:T(8,128)(2,1)S(1)}, bf16[528,512]{1,0:T(8,128)(2,1)S(1)}, u32[]{:S(2)}, u32[]{:S(2)}) %collective-permute-start.3) | collective-permute-done | bytes 540704 | tf_op jit(solution)/shard_map/ppermute | solution.py:42
  46.2 3.7 %shard_map.91._ = bf16[528,512]{1,0:T(8,128)(2,1)S(1)} custom-call(s32[4]{0:T(128)S(1)} %copy-done.10, bf16[528,512]{1,0:T(8,128)(2,1)S(1)} %collective-permute-done.2.refs_1_.refs_4_.q1, bf16[528,512]{1,0:T(8,128)(2,1)S(1)} %collective-permute-done.3.refs_2_.q2, bf16[512,512]{1,0:T(8,128)(2,1)S(1)} %copy-done.2, bf16[512,512]{1,0:T(8,128)(2,1)S(1)} %copy-done.3), custom_call_target="tpu_custom_call" | custom-call | flops 536870912 | bytes 2097152 | tf_op jit(solution)/shard_map/pallas_call | solution.py:233
  49.9 2.7 %collective-permute-start.16 = (bf16[4,2,2,2,128,128]{5,4,3,2,1,0:T(8,128)(2,1)}, bf16[4,2,2,2,128,128]{5,4,3,2,1,0:T(8,128)(2,1)S(1)}, u32[]{:S(2)}, u32[]{:S(2)}) collective-permute-start(bf16[4,2,2,2,128,128]{5,4,3,2,1,0:T(8,128)(2,1)} %collective-permute-done.15.refs_6_), channel_id=1, source_target_pairs={{0,3},{16,28},{32,35},{48,60},{64,67},{80,92},{96,99},{112,124},{1... | collective-permute-start | bytes 3145736 | tf_op jit(solution)/shard_map/ppermute | solution.py:42
  53.2 2.8 %collective-permute-start.20 = (bf16[528,512]{1,0:T(8,128)(2,1)S(1)}, bf16[528,512]{1,0:T(8,128)(2,1)S(1)}, u32[]{:S(2)}, u32[]{:S(2)}) collective-permute-start(bf16[528,512]{1,0:T(8,128)(2,1)S(1)} %shard_map.91._), channel_id=1, source_target_pairs={{0,32},{16,48},{32,64},{48,80},{64,96},{80,112},{1,33},{17,49},{33... | collective-permute-start | bytes 1622024 | tf_op jit(solution)/shard_map/ppermute | solution.py:42
  56.0 3.9 %shard_map.92 = bf16[528,512]{1,0:T(8,128)(2,1)S(1)} custom-call(s32[4]{0:T(128)S(1)} %copy-done.10, bf16[528,512]{1,0:T(8,128)(2,1)S(1)} %collective-permute-done.4.refs_3_.q3, bf16[512,512]{1,0:T(8,128)(2,1)S(1)} %copy-done.2, bf16[512,512]{1,0:T(8,128)(2,1)S(1)} %copy-done.3, bf16[528,512]{1,0:T(8,128)(2,1)S(1)} %shard_map.91._), custom_call_target="tpu_custom_call" | custom-call | flops 536870912 | bytes 2097152 | tf_op jit(solution)/shard_map/pallas_call | solution.py:233
  60.7 4.8 %collective-permute-start.21 = (bf16[528,512]{1,0:T(8,128)(2,1)S(1)}, bf16[528,512]{1,0:T(8,128)(2,1)S(1)}, u32[]{:S(2)}, u32[]{:S(2)}) collective-permute-start(bf16[528,512]{1,0:T(8,128)(2,1)S(1)} %shard_map.92), channel_id=1, source_target_pairs={{0,64},{16,80},{32,96},{48,112},{1,65},{17,81},{33,97},{49,113},{2... | collective-permute-start | bytes 1622024 | tf_op jit(solution)/shard_map/ppermute | solution.py:42
  65.6 1.6 %shard_map.84 = (s32[144]{0:T(256)S(1)}, s32[80]{0:T(128)S(1)}) custom-call(s32[4]{0:T(128)S(1)} %copy-done.10, s32[128]{0:T(128)S(1)} %fusion.8.ids), custom_call_target="tpu_custom_call" | custom-call | flops 1000 | bytes 1000 | tf_op jit(solution)/shard_map/pallas_call | solution.py:339
  67.3 7.0 %shard_map.86 = (bf16[272,512]{1,0:T(8,128)(2,1)S(1)}, bf16[272,512]{1,0:T(8,128)(2,1)S(1)}, bf16[272,512]{1,0:T(8,128)(2,1)S(1)}, bf16[272,512]{1,0:T(8,128)(2,1)S(1)}) custom-call(s32[144]{0:T(256)S(1)} %get-tuple-element.34.slots, s32[80]{0:T(128)S(1)} %get-tuple-element.35.blocks, bf16[528,512]{1,0:T(8,128)(2,1)S(1)} %copy-done, ...), custom_call_target="tpu_custom_call" | custom-call | flops 536870912 | bytes 6291456 | tf_op jit(solution)/shard_map/pallas_call | solution.py:428
  74.7 2.3 %collective-permute-start.12 = (bf16[272,512]{1,0:T(8,128)(2,1)S(1)}, bf16[272,512]{1,0:T(8,128)(2,1)S(1)}, u32[]{:S(2)}, u32[]{:S(2)}) collective-permute-start(bf16[272,512]{1,0:T(8,128)(2,1)S(1)} %get-tuple-element.39), channel_id=1, source_target_pairs={{0,32},{16,112},{32,64},{48,16},{64,96},{80,48},{96,0},{112,80},{1... | collective-permute-start | bytes 835592 | tf_op jit(solution)/shard_map/ppermute | solution.py:42
  77.0 6.7 %shard_map.89 = (bf16[272,512]{1,0:T(8,128)(2,1)S(1)}, bf16[272,512]{1,0:T(8,128)(2,1)S(1)}, bf16[272,512]{1,0:T(8,128)(2,1)S(1)}, bf16[272,512]{1,0:T(8,128)(2,1)S(1)}) custom-call(s32[144]{0:T(256)S(1)} %get-tuple-element.34.slots, s32[80]{0:T(128)S(1)} %get-tuple-element.35.blocks, bf16[528,512]{1,0:T(8,128)(2,1)S(1)} %copy-done, ...), custom_call_target="tpu_custom_call" | custom-call | flops 536870912 | bytes 6291456 | tf_op jit(solution)/shard_map/pallas_call | solution.py:428
  84.5 2.0 %collective-permute-start.18 = (bf16[272,512]{1,0:T(8,128)(2,1)S(1)}, bf16[272,512]{1,0:T(8,128)(2,1)S(1)}, u32[]{:S(2)}, u32[]{:S(2)}) collective-permute-start(bf16[272,512]{1,0:T(8,128)(2,1)S(1)} %get-tuple-element.44), channel_id=1, source_target_pairs={{0,32},{16,112},{32,64},{48,16},{64,96},{80,48},{96,0},{112,80},{1... | collective-permute-start | bytes 835592 | tf_op jit(solution)/shard_map/ppermute | solution.py:42
  86.5 6.3 %collective-permute-start.19 = (bf16[272,512]{1,0:T(8,128)(2,1)S(1)}, bf16[272,512]{1,0:T(8,128)(2,1)S(1)}, u32[]{:S(2)}, u32[]{:S(2)}) collective-permute-start(bf16[272,512]{1,0:T(8,128)(2,1)S(1)} %get-tuple-element.45), channel_id=1, source_target_pairs={{0,64},{16,80},{32,96},{48,112},{64,0},{80,16},{96,32},{112,48},{1... | collective-permute-start | bytes 835592 | tf_op jit(solution)/shard_map/ppermute | solution.py:42
  92.8 3.4 %shard_map.90.refs_8_ = bf16[528,512]{1,0:T(8,128)(2,1)S(1)} custom-call(s32[4]{0:T(128)S(1)} %copy-done.10, bf16[528,512]{1,0:T(8,128)(2,1)S(1)} %copy-done, bf16[512,512]{1,0:T(8,128)(2,1)S(1)} %copy-done.2, bf16[512,512]{1,0:T(8,128)(2,1)S(1)} %copy-done.3), custom_call_target="tpu_custom_call" | custom-call | flops 536870912 | bytes 2097152 | tf_op jit(solution)/shard_map/pallas_call | solution.py:233
  96.3 5.3 %collective-permute-done.19.refs_7_ = bf16[272,512]{1,0:T(8,128)(2,1)S(1)} collective-permute-done((bf16[272,512]{1,0:T(8,128)(2,1)S(1)}, bf16[272,512]{1,0:T(8,128)(2,1)S(1)}, u32[]{:S(2)}, u32[]{:S(2)}) %collective-permute-start.19) | collective-permute-done | bytes 278560 | tf_op jit(solution)/shard_map/ppermute | solution.py:42
  101.6 1.6 %shard_map.93 = (bf16[256,512]{1,0:T(8,128)(2,1)S(1)}, bf16[256,512]{1,0:T(8,128)(2,1)S(1)}) custom-call(s32[4]{0:T(128)S(1)} %copy-done.10, f32[8]{0:T(128)S(1)} %copy-done.11, bf16[272,512]{1,0:T(8,128)(2,1)S(1)} %get-tuple-element.37.refs_0_, bf16[272,512]{1,0:T(8,128)(2,1)S(1)} %collective-permute-done.11.refs_1_, ...), custom_call_target="tpu_custom_call" | custom-call | flops 5406720 | bytes 4325376 | tf_op jit(solution)/shard_map/pallas_call | solution.py:485
  103.1 3.5 %collective-permute-start.22 = (bf16[256,512]{1,0:T(8,128)(2,1)S(1)}, bf16[256,512]{1,0:T(8,128)(2,1)S(1)}, u32[]{:S(2)}, u32[]{:S(2)}) collective-permute-start(bf16[256,512]{1,0:T(8,128)(2,1)S(1)} %get-tuple-element.48), channel_id=1, source_target_pairs={{0,16},{16,0},{32,48},{48,32},{64,80},{80,64},{96,112},{112,96},{1... | collective-permute-start | bytes 786440 | tf_op jit(solution)/shard_map/ppermute | solution.py:42
  107.8 2.8 %shard_map.94 = bf16[256,2048]{1,0:T(8,128)(2,1)} custom-call(s32[4]{0:T(128)S(1)} %copy-done.10, bf16[256,512]{1,0:T(8,128)(2,1)S(1)} %get-tuple-element.47.own, bf16[256,512]{1,0:T(8,128)(2,1)S(1)} %collective-permute-done.22.oth, bf16[1024,2048]{1,0:T(8,128)(2,1)S(1)} %copy-done.4), custom_call_target="tpu_custom_call" | custom-call | flops 1073741824 | bytes 4194304 | tf_op jit(solution)/shard_map/pallas_call | solution.py:511
  (63 shorter events, 11.8 us)
Async XLA Ops:
  0.0 9.9 %copy-start.12 = (s32[1,2,8]{2,1,0:T(2,128)S(1)}, s32[1,2,8]{2,1,0:T(2,128)}, u32[]{:S(2)}) copy-start(s32[1,2,8]{2,1,0:T(2,128)} %param.11) | copy-start | bytes 196
  0.0 11.8 %collective-permute-start = (bf16[256,2048]{1,0:T(8,128)(2,1)}, bf16[256,2048]{1,0:T(8,128)(2,1)}, u32[]{:S(2)}, u32[]{:S(2)}) collective-permute-start(bf16[256,2048]{1,0:T(8,128)(2,1)} %bitcast.14), channel_id=1, source_target_pairs={{0,16},{16,0},{32,48},{48,32},{64,80},{80,64},{96,112},{112,96},{1... | collective-permute-start | bytes 3145736 | tf_op jit(solution)/shard_map/ppermute | solution.py:42
  4.7 17.5 %copy-start.5 = (bf16[1,2,2,2,2,128,128]{6,5,4,3,2,1,0:T(8,128)(2,1)S(1)}, bf16[1,2,2,2,2,128,128]{6,5,4,3,2,1,0:T(8,128)(2,1)}, u32[]{:S(2)}) copy-start(bf16[1,2,2,2,2,128,128]{6,5,4,3,2,1,0:T(8,128)(2,1)} %get-tuple-element.36.refs_0_) | copy-start | bytes 1572868
  4.7 14.6 %collective-permute-start.5 = (bf16[1,2,2,2,2,128,128]{6,5,4,3,2,1,0:T(8,128)(2,1)}, bf16[1,2,2,2,2,128,128]{6,5,4,3,2,1,0:T(8,128)(2,1)S(1)}, u32[]{:S(2)}, u32[]{:S(2)}) collective-permute-start(bf16[1,2,2,2,2,128,128]{6,5,4,3,2,1,0:T(8,128)(2,1)} %get-tuple-element.36.refs_0_), channel_id=1, source_target_pairs={{0,4},{16,17},{32,36},{48,49},{64,68},{80,81},{96,100},{112,113},{... | collective-permute-start | bytes 1572872 | tf_op jit(solution)/shard_map/ppermute | solution.py:42
  6.5 14.3 %collective-permute-start.6 = (bf16[1,2,2,2,2,128,128]{6,5,4,3,2,1,0:T(8,128)(2,1)}, bf16[1,2,2,2,2,128,128]{6,5,4,3,2,1,0:T(8,128)(2,1)S(1)}, u32[]{:S(2)}, u32[]{:S(2)}) collective-permute-start(bf16[1,2,2,2,2,128,128]{6,5,4,3,2,1,0:T(8,128)(2,1)} %get-tuple-element.36.refs_0_), channel_id=1, source_target_pairs={{0,12},{16,19},{32,44},{48,51},{64,76},{80,83},{96,108},{112,115},... | collective-permute-start | bytes 1572872 | tf_op jit(solution)/shard_map/ppermute | solution.py:42
  8.7 13.5 %collective-permute-start.7 = (bf16[1,2,2,2,2,128,128]{6,5,4,3,2,1,0:T(8,128)(2,1)}, bf16[1,2,2,2,2,128,128]{6,5,4,3,2,1,0:T(8,128)(2,1)S(1)}, u32[]{:S(2)}, u32[]{:S(2)}) collective-permute-start(bf16[1,2,2,2,2,128,128]{6,5,4,3,2,1,0:T(8,128)(2,1)} %get-tuple-element.36.refs_0_), channel_id=1, source_target_pairs={{0,8},{16,18},{32,40},{48,50},{64,72},{80,82},{96,104},{112,114},{... | collective-permute-start | bytes 1572872 | tf_op jit(solution)/shard_map/ppermute | solution.py:42
  10.0 1.1 %collective-permute-start.1 = (s32[1,16]{1,0:T(1,128)S(1)}, s32[1,16]{1,0:T(1,128)S(1)}, u32[]{:S(2)}, u32[]{:S(2)}) collective-permute-start(s32[1,16]{1,0:T(1,128)S(1)} %concatenate.19), channel_id=1, source_target_pairs={{0,16},{16,0},{32,48},{48,32},{64,80},{80,64},{96,112},{112,96},{1... | collective-permute-start | bytes 200 | tf_op jit(solution)/shard_map/ppermute | solution.py:42
  16.6 14.4 %collective-permute-start.2 = (bf16[528,512]{1,0:T(8,128)(2,1)}, bf16[528,512]{1,0:T(8,128)(2,1)S(1)}, u32[]{:S(2)}, u32[]{:S(2)}) collective-permute-start(bf16[528,512]{1,0:T(8,128)(2,1)} %shard_map.83.refs_0_._.q), channel_id=1, source_target_pairs={{0,32},{16,112},{32,64},{48,16},{64,96},{80,48},{96,0},{112,80},{1... | collective-permute-start | bytes 1622024 | tf_op jit(solution)/shard_map/ppermute | solution.py:42
  20.8 10.2 %copy-start.6 = (bf16[1,2,2,2,2,128,128]{6,5,4,3,2,1,0:T(8,128)(2,1)}, bf16[1,2,2,2,2,128,128]{6,5,4,3,2,1,0:T(8,128)(2,1)S(1)}, u32[]{:S(2)}) copy-start(bf16[1,2,2,2,2,128,128]{6,5,4,3,2,1,0:T(8,128)(2,1)S(1)} %collective-permute-done.6.refs_2_) | copy-start | bytes 1572868
  23.2 16.0 %collective-permute-start.8 = (bf16[4,2,2,2,128,128]{5,4,3,2,1,0:T(8,128)(2,1)}, bf16[4,2,2,2,128,128]{5,4,3,2,1,0:T(8,128)(2,1)}, u32[]{:S(2)}, u32[]{:S(2)}) collective-permute-start(bf16[4,2,2,2,128,128]{5,4,3,2,1,0:T(8,128)(2,1)} %shard_map.85.refs_4_), channel_id=1, source_target_pairs={{0,1},{16,20},{32,33},{48,52},{64,65},{80,84},{96,97},{112,116},{1... | collective-permute-start | bytes 3145736 | tf_op jit(solution)/shard_map/ppermute | solution.py:42
  24.5 21.7 %copy-start.10 = (s32[4]{0:T(128)S(1)}, s32[4]{0:T(128)}, u32[]{:S(2)}) copy-start(s32[4]{0:T(128)} %pad_add_fusion.info) | copy-start | bytes 52
  30.9 5.7 %copy-start = (bf16[528,512]{1,0:T(8,128)(2,1)S(1)}, bf16[528,512]{1,0:T(8,128)(2,1)}, u32[]{:S(2)}) copy-start(bf16[528,512]{1,0:T(8,128)(2,1)} %shard_map.83.refs_0_._.q) | copy-start | bytes 1622020
  34.1 12.0 %copy-start.2 = (bf16[512,512]{1,0:T(8,128)(2,1)S(1)}, bf16[512,512]{1,0:T(8,128)(2,1)}, u32[]{:S(2)}) copy-start(bf16[512,512]{1,0:T(8,128)(2,1)} %get-tuple-element.41.refs_5_.k) | copy-start | bytes 1572868
  34.1 12.0 %copy-start.3 = (bf16[512,512]{1,0:T(8,128)(2,1)S(1)}, bf16[512,512]{1,0:T(8,128)(2,1)}, u32[]{:S(2)}) copy-start(bf16[512,512]{1,0:T(8,128)(2,1)} %get-tuple-element.46.v) | copy-start | bytes 1572868
  35.1 14.8 %collective-permute-start.15 = (bf16[4,2,2,2,128,128]{5,4,3,2,1,0:T(8,128)(2,1)}, bf16[4,2,2,2,128,128]{5,4,3,2,1,0:T(8,128)(2,1)}, u32[]{:S(2)}, u32[]{:S(2)}) collective-permute-start(bf16[4,2,2,2,128,128]{5,4,3,2,1,0:T(8,128)(2,1)} %shard_map.88.refs_4_), channel_id=1, source_target_pairs={{0,3},{16,28},{32,35},{48,60},{64,67},{80,92},{96,99},{112,124},{1... | collective-permute-start | bytes 3145736 | tf_op jit(solution)/shard_map/ppermute | solution.py:42
  36.7 9.5 %collective-permute-start.3 = (bf16[528,512]{1,0:T(8,128)(2,1)S(1)}, bf16[528,512]{1,0:T(8,128)(2,1)S(1)}, u32[]{:S(2)}, u32[]{:S(2)}) collective-permute-start(bf16[528,512]{1,0:T(8,128)(2,1)S(1)} %copy-done), channel_id=1, source_target_pairs={{0,96},{16,48},{32,0},{48,80},{64,32},{80,112},{96,64},{112,16},{1... | collective-permute-start | bytes 1622024 | tf_op jit(solution)/shard_map/ppermute | solution.py:42
  38.0 22.7 %collective-permute-start.9 = (bf16[4,2,2,2,128,128]{5,4,3,2,1,0:T(8,128)(2,1)}, bf16[4,2,2,2,128,128]{5,4,3,2,1,0:T(8,128)(2,1)}, u32[]{:S(2)}, u32[]{:S(2)}) collective-permute-start(bf16[4,2,2,2,128,128]{5,4,3,2,1,0:T(8,128)(2,1)} %shard_map.85.refs_4_), channel_id=1, source_target_pairs={{0,3},{16,28},{32,35},{48,60},{64,67},{80,92},{96,99},{112,124},{1... | collective-permute-start | bytes 3145736 | tf_op jit(solution)/shard_map/ppermute | solution.py:42
  39.2 28.0 %collective-permute-start.10 = (bf16[4,2,2,2,128,128]{5,4,3,2,1,0:T(8,128)(2,1)}, bf16[4,2,2,2,128,128]{5,4,3,2,1,0:T(8,128)(2,1)S(1)}, u32[]{:S(2)}, u32[]{:S(2)}) collective-permute-start(bf16[4,2,2,2,128,128]{5,4,3,2,1,0:T(8,128)(2,1)} %collective-permute-done.8.refs_5_), channel_id=1, source_target_pairs={{0,1},{16,20},{32,33},{48,52},{64,65},{80,84},{96,97},{112,116},{1... | collective-permute-start | bytes 3145736 | tf_op jit(solution)/shard_map/ppermute | solution.py:42
  39.4 13.8 %collective-permute-start.4 = (bf16[528,512]{1,0:T(8,128)(2,1)S(1)}, bf16[528,512]{1,0:T(8,128)(2,1)S(1)}, u32[]{:S(2)}, u32[]{:S(2)}) collective-permute-start(bf16[528,512]{1,0:T(8,128)(2,1)S(1)} %collective-permute-done.2.refs_1_.refs_4_.q1), channel_id=1, source_target_pairs={{0,32},{16,112},{32,64},{48,16},{64,96},{80,48},{96,0},{112,80},{1... | collective-permute-start | bytes 1622024 | tf_op jit(solution)/shard_map/ppermute | solution.py:42
  46.1 28.6 %collective-permute-start.14 = (bf16[4,2,2,2,128,128]{5,4,3,2,1,0:T(8,128)(2,1)}, bf16[4,2,2,2,128,128]{5,4,3,2,1,0:T(8,128)(2,1)S(1)}, u32[]{:S(2)}, u32[]{:S(2)}) collective-permute-start(bf16[4,2,2,2,128,128]{5,4,3,2,1,0:T(8,128)(2,1)} %shard_map.88.refs_4_), channel_id=1, source_target_pairs={{0,1},{16,20},{32,33},{48,52},{64,65},{80,84},{96,97},{112,116},{1... | collective-permute-start | bytes 3145736 | tf_op jit(solution)/shard_map/ppermute | solution.py:42
  49.9 27.1 %collective-permute-start.16 = (bf16[4,2,2,2,128,128]{5,4,3,2,1,0:T(8,128)(2,1)}, bf16[4,2,2,2,128,128]{5,4,3,2,1,0:T(8,128)(2,1)S(1)}, u32[]{:S(2)}, u32[]{:S(2)}) collective-permute-start(bf16[4,2,2,2,128,128]{5,4,3,2,1,0:T(8,128)(2,1)} %collective-permute-done.15.refs_6_), channel_id=1, source_target_pairs={{0,3},{16,28},{32,35},{48,60},{64,67},{80,92},{96,99},{112,124},{1... | collective-permute-start | bytes 3145736 | tf_op jit(solution)/shard_map/ppermute | solution.py:42
  53.2 30.5 %collective-permute-start.20 = (bf16[528,512]{1,0:T(8,128)(2,1)S(1)}, bf16[528,512]{1,0:T(8,128)(2,1)S(1)}, u32[]{:S(2)}, u32[]{:S(2)}) collective-permute-start(bf16[528,512]{1,0:T(8,128)(2,1)S(1)} %shard_map.91._), channel_id=1, source_target_pairs={{0,32},{16,48},{32,64},{48,80},{64,96},{80,112},{1,33},{17,49},{33... | collective-permute-start | bytes 1622024 | tf_op jit(solution)/shard_map/ppermute | solution.py:42
  60.7 23.8 %collective-permute-start.21 = (bf16[528,512]{1,0:T(8,128)(2,1)S(1)}, bf16[528,512]{1,0:T(8,128)(2,1)S(1)}, u32[]{:S(2)}, u32[]{:S(2)}) collective-permute-start(bf16[528,512]{1,0:T(8,128)(2,1)S(1)} %shard_map.92), channel_id=1, source_target_pairs={{0,64},{16,80},{32,96},{48,112},{1,65},{17,81},{33,97},{49,113},{2... | collective-permute-start | bytes 1622024 | tf_op jit(solution)/shard_map/ppermute | solution.py:42
  74.3 12.2 %collective-permute-start.11 = (bf16[272,512]{1,0:T(8,128)(2,1)S(1)}, bf16[272,512]{1,0:T(8,128)(2,1)S(1)}, u32[]{:S(2)}, u32[]{:S(2)}) collective-permute-start(bf16[272,512]{1,0:T(8,128)(2,1)S(1)} %get-tuple-element.38), channel_id=1, source_target_pairs={{0,96},{16,48},{32,0},{48,80},{64,32},{80,112},{96,64},{112,16},{1... | collective-permute-start | bytes 835592 | tf_op jit(solution)/shard_map/ppermute | solution.py:42
  74.7 21.5 %collective-permute-start.12 = (bf16[272,512]{1,0:T(8,128)(2,1)S(1)}, bf16[272,512]{1,0:T(8,128)(2,1)S(1)}, u32[]{:S(2)}, u32[]{:S(2)}) collective-permute-start(bf16[272,512]{1,0:T(8,128)(2,1)S(1)} %get-tuple-element.39), channel_id=1, source_target_pairs={{0,32},{16,112},{32,64},{48,16},{64,96},{80,48},{96,0},{112,80},{1... | collective-permute-start | bytes 835592 | tf_op jit(solution)/shard_map/ppermute | solution.py:42
  77.0 24.5 %copy-start.11 = (f32[8]{0:T(128)S(1)}, f32[8]{0:T(128)}, u32[]{:S(2)}) copy-start(f32[8]{0:T(128)} %gate.1) | copy-start | bytes 100
  77.0 19.2 %collective-permute-start.13 = (bf16[272,512]{1,0:T(8,128)(2,1)S(1)}, bf16[272,512]{1,0:T(8,128)(2,1)S(1)}, u32[]{:S(2)}, u32[]{:S(2)}) collective-permute-start(bf16[272,512]{1,0:T(8,128)(2,1)S(1)} %get-tuple-element.40), channel_id=1, source_target_pairs={{0,64},{16,80},{32,96},{48,112},{64,0},{80,16},{96,32},{112,48},{1... | collective-permute-start | bytes 835592 | tf_op jit(solution)/shard_map/ppermute | solution.py:42
  83.7 24.1 %copy-start.4 = (bf16[1024,2048]{1,0:T(8,128)(2,1)S(1)}, bf16[1024,2048]{1,0:T(8,128)(2,1)}, u32[]{:S(2)}) copy-start(bf16[1024,2048]{1,0:T(8,128)(2,1)} %w.3) | copy-start | bytes 12582916
  83.8 12.5 %collective-permute-start.17 = (bf16[272,512]{1,0:T(8,128)(2,1)S(1)}, bf16[272,512]{1,0:T(8,128)(2,1)S(1)}, u32[]{:S(2)}, u32[]{:S(2)}) collective-permute-start(bf16[272,512]{1,0:T(8,128)(2,1)S(1)} %get-tuple-element.43), channel_id=1, source_target_pairs={{0,96},{16,48},{32,0},{48,80},{64,32},{80,112},{96,64},{112,16},{1... | collective-permute-start | bytes 835592 | tf_op jit(solution)/shard_map/ppermute | solution.py:42
  84.5 11.8 %collective-permute-start.18 = (bf16[272,512]{1,0:T(8,128)(2,1)S(1)}, bf16[272,512]{1,0:T(8,128)(2,1)S(1)}, u32[]{:S(2)}, u32[]{:S(2)}) collective-permute-start(bf16[272,512]{1,0:T(8,128)(2,1)S(1)} %get-tuple-element.44), channel_id=1, source_target_pairs={{0,32},{16,112},{32,64},{48,16},{64,96},{80,48},{96,0},{112,80},{1... | collective-permute-start | bytes 835592 | tf_op jit(solution)/shard_map/ppermute | solution.py:42
  86.5 15.0 %collective-permute-start.19 = (bf16[272,512]{1,0:T(8,128)(2,1)S(1)}, bf16[272,512]{1,0:T(8,128)(2,1)S(1)}, u32[]{:S(2)}, u32[]{:S(2)}) collective-permute-start(bf16[272,512]{1,0:T(8,128)(2,1)S(1)} %get-tuple-element.45), channel_id=1, source_target_pairs={{0,64},{16,80},{32,96},{48,112},{64,0},{80,16},{96,32},{112,48},{1... | collective-permute-start | bytes 835592 | tf_op jit(solution)/shard_map/ppermute | solution.py:42
  103.1 4.7 %collective-permute-start.22 = (bf16[256,512]{1,0:T(8,128)(2,1)S(1)}, bf16[256,512]{1,0:T(8,128)(2,1)S(1)}, u32[]{:S(2)}, u32[]{:S(2)}) collective-permute-start(bf16[256,512]{1,0:T(8,128)(2,1)S(1)} %get-tuple-element.48), channel_id=1, source_target_pairs={{0,16},{16,0},{32,48},{48,32},{64,80},{80,64},{96,112},{112,96},{1... | collective-permute-start | bytes 786440 | tf_op jit(solution)/shard_map/ppermute | solution.py:42
  (4 other events, 5.5 us)
